TPU v7x, 768 devices: a whole 4x8x12 slice. The times are simulated.
768 devices in a mesh: occ: 24 (over z, x_hi), vir: 32 (over x_lo, y, core).
Axes of the slice: x: 4 (x_hi: 2, x_lo: 2; x = x_hi * 2 + x_lo), y: 8, z: 12, core: 2. Of those that a mesh axis runs over, the one named last changes fastest.
Arguments:
- integrals: float32 [24, 768, 1536], P(None, 'vir', 'occ'), may hold values from -1.5 to 1.5
- occ_bins: int32 [24], replicated, may hold values from 0 to 99
- vir_bins: int32 [768], replicated, may hold values from 0 to 299
Outputs:
- density: float32 [768, 24, 1536], P('vir', 'occ')
All inputs are finite; a program needn't handle non-finite values.
Results may differ from a plain program's by a relative error of at most 0.0032.
Values may be sent and summed in bfloat16 or wider, within the bound.
No kernel may reach another device: no remote copies, remote signals or barrier semaphores. Data moves between devices by JAX's collectives and lax.ppermute only.
A program may use at most 32 MiB of HBM per device.

v0:
```python
import jax
import jax.numpy as jnp
from jax import lax
from jax.sharding import PartitionSpec as P

occupied_base = -0.4
occupied_step = 0.01
virtual_base = 0.1
virtual_step = 0.01
spin_scale = 1.3


def amplitudes(resident_part, j_blocks, occ_own, vir_rows, occupied, vir_slab):
    pair_values = jnp.einsum(
        "iap,jbp->iajb", resident_part, j_blocks, preferred_element_type=jnp.float32
    )
    denominator = (
        vir_rows[None, :, None, None]
        + vir_slab[None, None, None, :]
        - occ_own[:, None, None, None]
        - occupied[None, None, :, None]
    )
    return (spin_scale * pair_values / denominator).astype(jnp.bfloat16)


def shards(integrals, occ_bins, vir_bins):
    rounded = integrals.astype(jnp.bfloat16)
    j_blocks = lax.all_gather(rounded, "occ", axis=2, tiled=True)
    slab_rows = j_blocks.shape[1]
    own_count = j_blocks.shape[0] // lax.axis_size("occ")
    occ_start = lax.axis_index("occ") * own_count
    vir_start = lax.axis_index("vir") * slab_rows
    own_blocks = lax.dynamic_slice_in_dim(j_blocks, occ_start, own_count, 0)
    resident = lax.all_gather(own_blocks, "vir", axis=1, tiled=True)
    occupied = occupied_base - occupied_step * occ_bins.astype(jnp.float32)
    virtual = virtual_base + virtual_step * vir_bins.astype(jnp.float32)
    occ_own = lax.dynamic_slice_in_dim(occupied, occ_start, own_count, 0)
    vir_slab = lax.dynamic_slice_in_dim(virtual, vir_start, slab_rows, 0)
    amplitude = amplitudes(resident, j_blocks, occ_own, virtual, occupied, vir_slab)
    partial_term = jnp.einsum(
        "iajb,jbp->aip", amplitude, j_blocks, preferred_element_type=jnp.float32
    )
    density = lax.psum_scatter(partial_term, "vir", scatter_dimension=0, tiled=True)
    return density


def solution(mesh):
    in_specs = (P(None, "vir", "occ"), P(), P())
    out_specs = P("vir", "occ", None)
    return jax.shard_map(shards, mesh=mesh, in_specs=in_specs, out_specs=out_specs, check_vma=False)
```

profile of v0, /device:TPU:1, one launch (start us, length us, event | category | flops | bytes accessed | tf_op | source)
XLA Modules:
  0.0 410.4 jit_solution(13439245012184430699)
XLA Ops:
  6.5 0.0 all-gather.3.cloned.1.call-start
  6.5 1.0 convert_element_type.13
  7.5 0.0 copy-start.1
  7.5 0.0 copy-start
  7.5 1.0 copy.13
  8.5 0.0 all-gather.3.cloned.1.call-update
  8.6 0.0 all-gather.5.cloned.1.call-start
  8.6 186.2 %all-gather.3.cloned.1.call-done = bf16[24,24,1536]{1,0,2:T(8,128)(2,1)} async-done(((bf16[24,24,64]{1,0,2:T(8,128)(2,1)}), bf16[24,24,1536]{1,0,2:T(8,128)(2,1)}) %all-gather.3.cloned.1.call-update) | async-done | bytes 1769488 | tf_op jit(solution)/shard_map/all_gather | solution.py:28
  194.8 2.3 constant_dynamic-slice_fusion
  197.1 1.5 copy.14
  198.6 0.0 all-gather.5.cloned.1.call-update
  198.6 0.0 reduce-scatter.2.cloned.1.call-start
  198.7 0.0 copy-done.1
  198.7 0.6 dynamic_slice.11
  199.3 0.0 copy-done
  199.3 0.1 dynamic_slice.10
  199.4 0.7 add_subtract_fusion
  200.1 10.6 %copy.15 = bf16[24,24,1536]{2,0,1:T(8,128)(2,1)S(1)} copy(bf16[24,24,1536]{1,0,2:T(8,128)(2,1)} %all-gather.3.cloned.1.call-done) | data formatting | bytes 3538944 | tf_op jit(solution)/shard_map/all_gather | solution.py:28
  210.7 57.3 %all-gather.5.cloned.1.call-done = bf16[1,768,1536]{2,1,0:T(8,128)(2,1)} async-done(((bf16[1,24,1536]{2,1,0:T(8,128)(2,1)}), bf16[1,768,1536]{2,1,0:T(8,128)(2,1)}) %all-gather.5.cloned.1.call-update) | async-done | bytes 2359312 | tf_op jit(solution)/shard_map/all_gather | solution.py:34
  268.0 8.5 %convolution_bitcast_fusion = f32[768,1,1536]{2,0,1:T(8,128)} fusion(bf16[24,24,1536]{2,0,1:T(8,128)(2,1)S(1)} %copy.15, bf16[1,768,1536]{2,1,0:T(8,128)(2,1)} %all-gather.5.cloned.1.call-done, f32[24]{0:T(128)S(1)} %multiply_subtract_fusion, f32[768,24]{0,1:T(8,128)S(1)} %add_subtract_fusion), kind=kOutput, calls=%fused_computation | convolution fusion | flops 2719678464 | bytes 8921184 | tf_op jit(solution)/shard_map/iajb,jbp->aip/dot_general | solution.py:40
  276.4 0.0 reduce-scatter.2.cloned.1.call-update
  276.4 125.7 %reduce-scatter.2.cloned.1.call-done = f32[24,1,1536]{2,0,1:T(8,128)} async-done(((f32[768,1,1536]{2,0,1:T(8,128)}), f32[24,1,1536]{2,0,1:T(8,128)}) %reduce-scatter.2.cloned.1.call-update) | async-done | bytes 147472 | tf_op jit(solution)/shard_map/reduce_scatter | solution.py:43
  402.2 1.7 copy.17
  (2 shorter events, 0.0 us)
Async XLA Ops:
  6.5 188.3 %all-gather.3.cloned.1.call-start = ((), (), s32[]{:S(2)}) async-start(), calls=%async_computation.1 | async-start | bytes 9830400 | tf_op jit(solution)/shard_map/all_gather | solution.py:28
  7.5 191.2 %copy-start.1 = (s32[24]{0:T(128)S(1)}, s32[24]{0:T(128)}, u32[]{:S(2)}) copy-start(s32[24]{0:T(128)} %param.4) | copy-start | bytes 292
  7.5 191.8 %copy-start = (s32[768]{0:T(1024)S(1)}, s32[768]{0:T(1024)}, u32[]{:S(2)}) copy-start(s32[768]{0:T(1024)} %param.5) | copy-start | bytes 9220
  8.6 259.4 %all-gather.5.cloned.1.call-start = ((), (), s32[]{:S(2)}) async-start(), calls=%async_computation.2 | async-start | bytes 2433024 | tf_op jit(solution)/shard_map/all_gather | solution.py:34
  198.6 203.6 %reduce-scatter.2.cloned.1.call-start = ((), (), s32[]{:S(2)}) async-start(), calls=%async_computation.3 | async-start | bytes 4866048 | tf_op jit(solution)/shard_map/reduce_scatter | solution.py:43
Sparse Core Ops, SparseCore 0:
  10.9 183.8 all-gather.2
  198.7 69.1 all-gather.4
  276.6 125.5 reduce-scatter.1
where the time goes:
time: 411 us; the launch traced here: 410 us
  waiting for transfers between devices  369 us (90%)
  local copies, waits for them, and re-layouts  17.8 us (4%)
  between operations  13.2 us (3%)
  matrix products  8.45 us (2%)
    all_gather x1, waiting for transfers between devices, shards(): j_blocks = lax.all_gather(rounded, 'occ', axis=2, tiled=True)  186 us
    reduce_scatter x1, waiting for transfers between devices, shards(): lax.psum_scatter(partial_term, 'vir', scatter_dimension=0, tiled=True)  126 us
    all_gather x1, waiting for transfers between devices, shards(): resident = lax.all_gather(own_blocks, 'vir', axis=1, tiled=True)  57.3 us
    all_gather x1, local copies, waits for them, and re-layouts, shards(): j_blocks = lax.all_gather(rounded, 'occ', axis=2, tiled=True)  10.6 us
    dot_general x1, matrix products, shards(): jnp.einsum('iajb,jbp->aip', amplitude, j_blocks, preferred_element_type=j...  8.45 us
  transfers between devices with their start and end apart: 3, of which 3 were waited for; matrix products, arithmetic and copies ran while one was open for 3% of the time, Pallas kernels for 0%

commit v1 on v0

v1 whole, which is shorter than its diff:
```python
import jax
import jax.numpy as jnp
from jax import lax
from jax.experimental import pallas as pl
from jax.experimental.pallas import tpu as pltpu
from jax.sharding import Mesh, PartitionSpec as P

occupied_base = -0.4
occupied_step = 0.01
virtual_base = 0.1
virtual_step = 0.01
spin_scale = 1.3

SWAP = [(0, 1), (1, 0)]


def half_kernel(chunks, more, *refs):
    if more:
        rows_ref, cols_ref, row_e, col_e, before_ref, out_ref, full, sem = refs
    else:
        rows_ref, cols_ref, row_e, col_e, out_ref, full, sem = refs
    copies = []
    for k in range(chunks):
        copies.append(
            pltpu.make_async_copy(cols_ref.at[k], full.at[:, pl.ds(k * 128, 128)], sem.at[k])
        )
    for copy in copies:
        copy.start()
    for copy in copies:
        copy.wait()
    held = full[...]
    pair = lax.dot_general(
        rows_ref[...], held, (((1,), (1,)), ((), ())), preferred_element_type=jnp.float32
    )
    amplitude = (spin_scale * pair / (row_e[...] + col_e[...])).astype(jnp.bfloat16)
    term = jnp.dot(amplitude, held, preferred_element_type=jnp.float32)
    if more:
        term = term + before_ref[...]
    out_ref[...] = term.astype(out_ref.dtype)


def half(rows, cols, row_e, col_e, before=None):
    chunks, width, _ = cols.shape
    height, depth = rows.shape
    more = before is not None
    vmem = pl.BlockSpec(memory_space=pltpu.VMEM)
    ins = [rows, cols, row_e, col_e] + ([before] if more else [])
    specs = [vmem, pl.BlockSpec(memory_space=pl.ANY), vmem, vmem] + ([vmem] if more else [])

    def body(*refs):
        half_kernel(chunks, more, *refs)

    return pl.pallas_call(
        body,
        out_shape=jax.ShapeDtypeStruct((height, depth), jnp.bfloat16 if more else jnp.float32),
        in_specs=specs,
        out_specs=vmem,
        scratch_shapes=[
            pltpu.VMEM((width, depth), jnp.bfloat16),
            pltpu.SemaphoreType.DMA((chunks,)),
        ],
        compiler_params=pltpu.CompilerParams(vmem_limit_bytes=24 * 1024 * 1024),
        cost_estimate=pl.CostEstimate(
            flops=4 * height * width * depth, bytes_accessed=2 * depth * (2 * height + width), transcendentals=0
        ),
    )(*ins)


def shards(integrals, occ_bins, vir_bins):
    nz, nh, nl, ny = (lax.axis_size(k) for k in ("z", "h", "l", "y"))
    z, h, l, y, c = (lax.axis_index(k) for k in ("z", "h", "l", "y", "c"))
    nj, slab, part = integrals.shape
    own = integrals.astype(jnp.bfloat16)
    packed = jnp.concatenate([own[: nj // 2], own[nj // 2 :]], axis=2)
    there = lax.ppermute(packed, "h", SWAP)
    other = jnp.concatenate([there[:, :, :part], there[:, :, part:]], axis=0)
    first = h == 0
    wide = jnp.concatenate([jnp.where(first, own, other), jnp.where(first, other, own)], axis=2)
    cols = lax.all_gather(wide.reshape(nj * slab, 2 * part), "z", axis=0, tiled=False)
    seeds = lax.dynamic_index_in_dim(wide.reshape(nz, nh, slab, 2 * part), h, 1, keepdims=False)
    seeds = lax.all_to_all(seeds, "z", 0, 0)
    seeds = jnp.transpose(seeds, (1, 0, 2)).reshape(slab, nz * 2 * part)
    rows = lax.all_to_all(
        jnp.broadcast_to(seeds[None], (nl * ny,) + seeds.shape), ("l", "y"), 0, 0
    ).reshape(nl * ny * slab, nz * 2 * part)
    cols, rows = lax.optimization_barrier((cols, rows))
    cols_there = lax.ppermute(cols, "c", SWAP)

    occupied = occupied_base - occupied_step * occ_bins.astype(jnp.float32)
    virtual = virtual_base + virtual_step * vir_bins.astype(jnp.float32)
    virtual = virtual.reshape(nl * ny, 2, slab)
    occ_own = lax.dynamic_index_in_dim(occupied, z * nh + h, 0, keepdims=False)
    row_e = (lax.dynamic_index_in_dim(virtual, c, 1, keepdims=False) - occ_own).reshape(-1, 1)
    here = lax.dynamic_index_in_dim(virtual, l * ny + y, 0, keepdims=False)
    col_own = lax.dynamic_index_in_dim(here, c, 0, keepdims=False)
    col_there = lax.dynamic_index_in_dim(here, 1 - c, 0, keepdims=False)
    col_own = (col_own[None, :] - occupied[:, None]).reshape(1, -1)
    col_there = (col_there[None, :] - occupied[:, None]).reshape(1, -1)

    before = half(rows, cols, row_e, col_own)
    partial_term = half(rows, cols_there, row_e, col_there, before)
    shares = lax.all_to_all(
        partial_term.reshape(nl * ny, slab, nz * 2 * part), ("l", "y"), 0, 0
    )
    density = jnp.sum(shares.astype(jnp.float32), axis=0)
    return density[:, None, :]


def solution(mesh):
    fine = Mesh(mesh.devices.reshape(12, 2, 2, 8, 2), ("z", "h", "l", "y", "c"))
    in_specs = (P(None, ("l", "y", "c"), ("z", "h")), P(), P())
    out_specs = P(("l", "y", "c"), ("z", "h"), None)
    return jax.shard_map(shards, mesh=fine, in_specs=in_specs, out_specs=out_specs, check_vma=False)
```

time: 411 us -> 143 us (0.35)
  waiting for transfers between devices: 369 us -> 5.79 us
  blocking collectives: 0 us -> 94.8 us
  starting transfers between devices: 0.09 us -> 14.4 us
  local copies, waits for them, and re-layouts: 17.8 us -> 4.32 us
  matrix products: 8.45 us -> 0 us
  Pallas kernels: 0 us -> 5.79 us
    all_gather x2 -> x1, waiting for transfers between devices: 243 us -> 4.05 us  [shards(): lax.all_gather(wide.reshape(nj * slab, 2 * part), 'z', axis=0, tiled=False)]
    reduce_scatter x1 -> x0, waiting for transfers between devices: 126 us -> none  [shards(): lax.psum_scatter(partial_term, 'vir', scatter_dimension=0, tiled=True)]
    all_to_all x0 -> x3, blocking collectives: none -> 94.8 us  [the longest x1 36.7 us: shards(): lax.all_to_all(partial_term.reshape(nl * ny, slab, nz * 2 * part), ('l',...]
    ppermute x0 -> x2, starting transfers between devices: none -> 14.4 us  [the longest x1 8.96 us: shards(): cols_there = lax.ppermute(cols, 'c', SWAP)]
    all_gather x1 -> x0, local copies, waits for them, and re-layouts: 10.6 us -> none  [shards(): j_blocks = lax.all_gather(rounded, 'occ', axis=2, tiled=True)]
    dot_general x1 -> x0, matrix products: 8.45 us -> none  [shards(): jnp.einsum('iajb,jbp->aip', amplitude, j_blocks, preferred_element_type=j...]
    pallas_call x0 -> x2, Pallas kernels: none -> 5.79 us  [half(): pl.pallas_call(body, out_shape=jax.ShapeDtypeStruct((height, depth), jnp....]
  transfers between devices with their start and end apart: 3 -> 3, of which waited for: 3 -> 2; matrix products, arithmetic and copies ran while one was open for 3% -> 2% of each run, Pallas kernels for 0% -> 2%
where the time goes in v1:
time: 143 us; the launch traced here: 142 us
  blocking collectives  94.8 us (66%)
  starting transfers between devices  14.4 us (10%)
  between operations  13.6 us (10%)
  waiting for transfers between devices  5.79 us (4%)
  Pallas kernels  5.79 us (4%)
  local copies, waits for them, and re-layouts  4.32 us (3%)
  other arithmetic  2.9 us (2%)
    all_to_all x1, blocking collectives, shards(): lax.all_to_all(partial_term.reshape(nl * ny, slab, nz * 2 * part), ('l',...  36.7 us
    all_to_all x1, blocking collectives, shards(): lax.all_to_all(jnp.broadcast_to(seeds[None], (nl * ny,) + seeds.shape), (...  33.5 us
    all_to_all x1, blocking collectives, shards(): seeds = lax.all_to_all(seeds, 'z', 0, 0)  24.6 us
    ppermute x1, starting transfers between devices, shards(): cols_there = lax.ppermute(cols, 'c', SWAP)  8.96 us
    pallas_call x2, Pallas kernels, half(): pl.pallas_call(body, out_shape=jax.ShapeDtypeStruct((height, depth), jnp....  5.79 us
    ppermute x1, starting transfers between devices, shards(): there = lax.ppermute(packed, 'h', SWAP)  5.48 us
    all_gather x1, waiting for transfers between devices, shards(): lax.all_gather(wide.reshape(nj * slab, 2 * part), 'z', axis=0, tiled=False)  4.05 us
  transfers between devices with their start and end apart: 3, of which 2 were waited for; matrix products, arithmetic and copies ran while one was open for 2% of the time, Pallas kernels for 2%

profile of v1, /device:TPU:1, one launch (start us, length us, event | category | flops | bytes accessed | tf_op | source)
XLA Modules:
  0.0 141.6 jit_solution(1492348562109182786)
XLA Ops:
  6.5 0.0 copy-start.1
  6.5 0.0 all-gather.2.cloned.1.call-start
  6.5 1.1 convert_element_type.12
  7.6 0.1 pad_maximum_fusion.2
  7.7 5.5 %collective-permute-start = (bf16[12,24,128]{2,1,0:T(8,128)(2,1)S(1)}, bf16[12,24,128]{2,1,0:T(8,128)(2,1)S(1)}, u32[]{:S(2)}, u32[]{:S(2)}) collective-permute-start(bf16[12,24,128]{2,1,0:T(8,128)(2,1)S(1)} %pad_maximum_fusion.2), channel_id=1, source_target_pairs={{0,32},{32,0},{1,33},{33,1},{2,34},{34,2},{3,35},{35,3},{4,36},{36... | collective-permute-start | bytes 221192 | tf_op jit(solution)/shard_map/ppermute | solution.py:75
  13.2 1.7 %collective-permute-done = bf16[12,24,128]{2,1,0:T(8,128)(2,1)S(1)} collective-permute-done((bf16[12,24,128]{2,1,0:T(8,128)(2,1)S(1)}, bf16[12,24,128]{2,1,0:T(8,128)(2,1)S(1)}, u32[]{:S(2)}, u32[]{:S(2)}) %collective-permute-start) | collective-permute-done | bytes 73760 | tf_op jit(solution)/shard_map/ppermute | solution.py:75
  14.9 0.1 fusion.3
  15.0 0.0 copy-done.1
  15.0 0.1 broadcast_select_fusion.1
  15.1 0.8 pad_maximum_fusion.1
  15.9 0.0 all-gather.2.cloned.1.call-update
  15.9 0.9 dynamic-slice_bitcast_fusion
  16.8 24.6 %all_to_all.15 = bf16[12,24,128]{2,1,0:T(8,128)(2,1)S(1)} all-to-all(bf16[12,24,128]{2,1,0:T(8,128)(2,1)S(1)} %dynamic-slice_bitcast_fusion), channel_id=1, replica_groups=mesh['z'=12,'h'=2,'l'=2,'y'=8,'c'=2] {'z'}, dimensions={0} | all-to-all | bytes 147456 | tf_op jit(solution)/shard_map/all_to_all | solution.py:81
  41.4 0.1 broadcast_in_dim.7
  41.5 0.0 copy-start.2
  41.5 0.0 copy-start.3
  41.5 33.5 %all_to_all.16 = bf16[16,24,1536]{2,1,0:T(8,128)(2,1)S(1)} all-to-all(bf16[16,24,1536]{2,1,0:T(8,128)(2,1)S(1)} %broadcast_in_dim.7), channel_id=1, replica_groups=mesh['z'=12,'h'=2,'l'=2,'y'=8,'c'=2] {'l','y'}, dimensions={0} | all-to-all | bytes 2359296 | tf_op jit(solution)/shard_map/all_to_all | solution.py:83
  75.0 4.1 %all-gather.2.cloned.1.call-done.refs_1_ = bf16[12,576,128]{2,1,0:T(8,128)(2,1)} async-done(((bf16[1,576,128]{2,1,0:T(8,128)(2,1)}), bf16[12,576,128]{2,1,0:T(8,128)(2,1)}) %all-gather.2.cloned.1.call-update) | async-done | bytes 1769488 | tf_op jit(solution)/shard_map/all_gather | solution.py:79
  79.1 9.0 %collective-permute-start.1 = (bf16[12,576,128]{2,1,0:T(8,128)(2,1)}, bf16[12,576,128]{2,1,0:T(8,128)(2,1)S(1)}, u32[]{:S(2)}, u32[]{:S(2)}) collective-permute-start(bf16[12,576,128]{2,1,0:T(8,128)(2,1)} %all-gather.2.cloned.1.call-done.refs_1_), channel_id=1, source_target_pairs={{0,1},{1,0},{2,3},{3,2},{4,5},{5,4},{6,7},{7,6},{8,9},{9,8},{10,11... | collective-permute-start | bytes 5308424 | tf_op jit(solution)/shard_map/ppermute | solution.py:87
  88.1 0.0 copy-done.2
  88.1 0.1 reshape.79
  88.2 0.0 copy-done.3
  88.2 0.6 dynamic_slice.23
  88.8 0.1 broadcast_subtract_fusion
  88.9 0.1 sub.83.refs_3_
  89.0 0.1 sub.79.refs_3_
  89.1 0.7 subtract_reduce_fusion
  89.7 0.1 sub.84.refs_2_
  89.9 0.0 copy-start
  89.9 1.5 %copy-done = bf16[12,576,128]{2,1,0:T(8,128)(2,1)S(1)} copy-done((bf16[12,576,128]{2,1,0:T(8,128)(2,1)S(1)}, bf16[12,576,128]{2,1,0:T(8,128)(2,1)}, u32[]{:S(2)}) %copy-start) | copy-done | bytes 1769496
  91.3 2.9 %shard_map.37.refs_4_ = f32[384,1536]{1,0:T(8,128)S(1)} custom-call(bf16[384,1536]{1,0:T(8,128)(2,1)S(1)} %bitcast.17, bf16[12,576,128]{2,1,0:T(8,128)(2,1)S(1)} %copy-done, f32[384,1]{1,0:T(8,128)S(1)} %sub.84.refs_2_, f32[1,576]{1,0:T(1,128)S(1)} %sub.83.refs_3_), custom_call_target="tpu_custom_call" | custom-call | flops 1358954496 | bytes 4128768 | tf_op jit(solution)/shard_map/pallas_call | solution.py:53
  94.2 0.0 collective-permute-done.1.refs_1_
  94.3 2.9 %shard_map.38 = bf16[384,1536]{1,0:T(8,128)(2,1)S(1)} custom-call(bf16[384,1536]{1,0:T(8,128)(2,1)S(1)} %bitcast.18, bf16[12,576,128]{2,1,0:T(8,128)(2,1)S(1)} %collective-permute-done.1.refs_1_, f32[384,1]{1,0:T(8,128)S(1)} %sub.84.refs_2_, f32[1,576]{1,0:T(1,128)S(1)} %sub.79.refs_3_, f32[384,1536]{1,0:T(8,128)S(1)} %shard_map.37.refs_4_), custom_call_target="tpu_custom_call" | custom-call | flops 1358954496 | bytes 4128768 | tf_op jit(solution)/shard_map/pallas_call | solution.py:53
  97.2 36.7 %all_to_all.17 = bf16[16,24,1536]{2,1,0:T(8,128)(2,1)S(1)} all-to-all(bf16[16,24,1536]{2,1,0:T(8,128)(2,1)S(1)} %bitcast.19), channel_id=1, replica_groups=mesh['z'=12,'h'=2,'l'=2,'y'=8,'c'=2] {'l','y'}, dimensions={0} | all-to-all | bytes 2359296 | tf_op jit(solution)/shard_map/all_to_all | solution.py:102
  133.8 0.2 convert_reduce_fusion
  134.0 0.8 broadcast_in_dim.16
  (5 shorter events, 0.0 us)
Async XLA Ops:
  6.5 8.5 %copy-start.1 = (f32[24,24,64]{2,1,0:T(8,128)S(1)}, f32[24,24,64]{2,1,0:T(8,128)}, u32[]{:S(2)}) copy-start(f32[24,24,64]{2,1,0:T(8,128)} %param.3) | copy-start | bytes 442372
  6.5 72.5 %all-gather.2.cloned.1.call-start = ((), (), s32[]{:S(2)}) async-start(), calls=%async_computation.3 | async-start | bytes 1916928 | tf_op jit(solution)/shard_map/all_gather | solution.py:79
  7.7 7.2 %collective-permute-start = (bf16[12,24,128]{2,1,0:T(8,128)(2,1)S(1)}, bf16[12,24,128]{2,1,0:T(8,128)(2,1)S(1)}, u32[]{:S(2)}, u32[]{:S(2)}) collective-permute-start(bf16[12,24,128]{2,1,0:T(8,128)(2,1)S(1)} %pad_maximum_fusion.2), channel_id=1, source_target_pairs={{0,32},{32,0},{1,33},{33,1},{2,34},{34,2},{3,35},{35,3},{4,36},{36... | collective-permute-start | bytes 221192 | tf_op jit(solution)/shard_map/ppermute | solution.py:75
  41.5 46.6 %copy-start.2 = (s32[768]{0:T(1024)S(1)}, s32[768]{0:T(1024)}, u32[]{:S(2)}) copy-start(s32[768]{0:T(1024)} %param.5) | copy-start | bytes 9220
  41.5 46.7 %copy-start.3 = (s32[24]{0:T(128)S(1)}, s32[24]{0:T(128)}, u32[]{:S(2)}) copy-start(s32[24]{0:T(128)} %param.4) | copy-start | bytes 292
  79.1 15.2 %collective-permute-start.1 = (bf16[12,576,128]{2,1,0:T(8,128)(2,1)}, bf16[12,576,128]{2,1,0:T(8,128)(2,1)S(1)}, u32[]{:S(2)}, u32[]{:S(2)}) collective-permute-start(bf16[12,576,128]{2,1,0:T(8,128)(2,1)} %all-gather.2.cloned.1.call-done.refs_1_), channel_id=1, source_target_pairs={{0,1},{1,0},{2,3},{3,2},{4,5},{5,4},{6,7},{7,6},{8,9},{9,8},{10,11... | collective-permute-start | bytes 5308424 | tf_op jit(solution)/shard_map/ppermute | solution.py:87
  89.9 1.5 %copy-start = (bf16[12,576,128]{2,1,0:T(8,128)(2,1)S(1)}, bf16[12,576,128]{2,1,0:T(8,128)(2,1)}, u32[]{:S(2)}) copy-start(bf16[12,576,128]{2,1,0:T(8,128)(2,1)} %all-gather.2.cloned.1.call-done.refs_1_) | copy-start | bytes 5308420
Sparse Core Ops, SparseCore 0:
  16.0 63.0 all-gather.1

commit v2 on v1

v2 whole, which is shorter than its diff:
```python
import jax
import jax.numpy as jnp
from jax import lax
from jax.experimental import pallas as pl
from jax.experimental.pallas import tpu as pltpu
from jax.sharding import Mesh, PartitionSpec as P

occupied_base = -0.4
occupied_step = 0.01
virtual_base = 0.1
virtual_step = 0.01
spin_scale = 1.3

SWAP = [(0, 1), (1, 0)]


def load(cols_ref, full, sem):
    chunks = cols_ref.shape[0]
    copies = [
        pltpu.make_async_copy(cols_ref.at[k], full.at[:, pl.ds(k * 128, 128)], sem.at[k])
        for k in range(chunks)
    ]
    for copy in copies:
        copy.start()
    for copy in copies:
        copy.wait()


def term(rows, held, row_e, col_e):
    pair = lax.dot_general(
        rows, held, (((1,), (1,)), ((), ())), preferred_element_type=jnp.float32
    )
    amplitude = (spin_scale * pair / (row_e + col_e)).astype(jnp.bfloat16)
    return jnp.dot(amplitude, held, preferred_element_type=jnp.float32)


def both_kernel(cols_ref, col_e, there_ref, there_e, own_ref, own_e, there_out, own_out, full, sem):
    load(cols_ref, full, sem)
    there_out[...] = term(there_ref[...], full[...], there_e[...], col_e[...])
    own_out[...] = term(own_ref[...], full[...], own_e[...], col_e[...])


def add_kernel(cols_ref, col_e, rows_ref, row_e, before_ref, out_ref, full, sem):
    load(cols_ref, full, sem)
    total = before_ref[...] + term(rows_ref[...], full[...], row_e[...], col_e[...])
    out_ref[...] = total.astype(out_ref.dtype)


def run(kernel, cols, args, outs, space):
    chunks, width, lanes = cols.shape
    depth = chunks * lanes
    vmem = pl.BlockSpec(memory_space=pltpu.VMEM)
    work = 4 * sum(o.shape[0] for o in outs) * width * depth
    return pl.pallas_call(
        kernel,
        out_shape=outs,
        in_specs=[pl.BlockSpec(memory_space=space)] + [vmem] * len(args),
        out_specs=[vmem] * len(outs),
        scratch_shapes=[
            pltpu.VMEM((width, depth), jnp.bfloat16),
            pltpu.SemaphoreType.DMA((chunks,)),
        ],
        compiler_params=pltpu.CompilerParams(vmem_limit_bytes=24 * 1024 * 1024),
        cost_estimate=pl.CostEstimate(flops=work, bytes_accessed=4 * width * depth, transcendentals=0),
    )(cols, *args)


def shards(integrals, occ_bins, vir_bins):
    nz, nh, nl, ny = (lax.axis_size(k) for k in ("z", "h", "l", "y"))
    z, h, l, y, c = (lax.axis_index(k) for k in ("z", "h", "l", "y", "c"))
    nj, slab, part = integrals.shape
    depth = nz * nh * part
    own = integrals.astype(jnp.bfloat16)
    packed = jnp.concatenate([own[: nj // 2], own[nj // 2 :]], axis=2)
    there = lax.ppermute(packed, "h", SWAP)
    other = jnp.concatenate([there[:, :, :part], there[:, :, part:]], axis=0)
    first = h == 0
    wide = jnp.concatenate([jnp.where(first, own, other), jnp.where(first, other, own)], axis=2)
    cols = lax.all_gather(wide.reshape(nj * slab, nh * part), "z", axis=0, tiled=False)
    seeds = lax.dynamic_index_in_dim(wide.reshape(nz, nh, slab, nh * part), h, 1, keepdims=False)
    seeds = lax.all_to_all(seeds, "z", 0, 0)
    seeds = jnp.transpose(seeds, (1, 0, 2)).reshape(slab, depth)

    occupied = occupied_base - occupied_step * occ_bins.astype(jnp.float32)
    virtual = virtual_base + virtual_step * vir_bins.astype(jnp.float32)
    virtual = virtual.reshape(nl, ny, 2, slab)
    occ_own = lax.dynamic_index_in_dim(occupied, z * nh + h, 0, keepdims=False)
    of_core = lax.dynamic_index_in_dim(virtual, c, 2, keepdims=False) - occ_own
    own_e = lax.dynamic_index_in_dim(of_core, l, 0, keepdims=False).reshape(-1, 1)
    there_e = lax.dynamic_index_in_dim(of_core, 1 - l, 0, keepdims=False).reshape(-1, 1)
    of_chip = lax.dynamic_index_in_dim(virtual.reshape(nl * ny, 2, slab), l * ny + y, 0, keepdims=False)
    col_own = lax.dynamic_index_in_dim(of_chip, c, 0, keepdims=False)
    col_there = lax.dynamic_index_in_dim(of_chip, 1 - c, 0, keepdims=False)
    col_own = (col_own[None, :] - occupied[:, None]).reshape(1, -1)
    col_there = (col_there[None, :] - occupied[:, None]).reshape(1, -1)
    seeds, own_e, there_e, col_own, col_there = lax.optimization_barrier(
        (seeds, own_e, there_e, col_own, col_there)
    )

    rows_own = lax.all_to_all(jnp.broadcast_to(seeds[None], (ny, slab, depth)), "y", 0, 0)
    rows_own = rows_own.reshape(ny * slab, depth)
    rows_there = lax.ppermute(rows_own, "l", SWAP)
    cols, rows_own, rows_there = lax.optimization_barrier((cols, rows_own, rows_there))
    cols_there = lax.ppermute(cols, "c", SWAP)

    share = jax.ShapeDtypeStruct(rows_own.shape, jnp.float32)
    sent = jax.ShapeDtypeStruct(rows_own.shape, jnp.bfloat16)
    for_there, for_own = run(
        both_kernel, cols, (col_own, rows_there, there_e, rows_own, own_e), [share, share], pltpu.HBM
    )
    (for_there,) = run(
        add_kernel, cols_there, (col_there, rows_there, there_e, for_there), [sent], pl.ANY
    )
    arrived = lax.ppermute(for_there, "l", SWAP)
    (for_own,) = run(
        add_kernel, cols_there, (col_there, rows_own, own_e, for_own), [share], pl.ANY
    )
    pair_sum = (for_own + arrived.astype(jnp.float32)).astype(jnp.bfloat16)
    shares = lax.all_to_all(pair_sum.reshape(ny, slab, depth), "y", 0, 0)
    density = jnp.sum(shares.astype(jnp.float32), axis=0)
    return density[:, None, :]


def solution(mesh):
    fine = Mesh(mesh.devices.reshape(12, 2, 2, 8, 2), ("z", "h", "l", "y", "c"))
    in_specs = (P(None, ("l", "y", "c"), ("z", "h")), P(), P())
    out_specs = P(("l", "y", "c"), ("z", "h"), None)
    return jax.shard_map(shards, mesh=fine, in_specs=in_specs, out_specs=out_specs, check_vma=False)
```

time: 143 us -> 145 us (1.014)
  blocking collectives: 94.8 us -> 44.4 us
  waiting for transfers between devices: 5.79 us -> 33.9 us
  starting transfers between devices: 14.4 us -> 35.7 us
    all_to_all x3 -> x2, blocking collectives: 94.8 us -> 44.4 us  [the longest x1 23.5 us: shards(): shares = lax.all_to_all(pair_sum.reshape(ny, slab, depth), 'y', 0, 0)]
    ppermute x0 -> x2, waiting for transfers between devices: none -> 19.8 us  [the longest x1 11.7 us: shards(): arrived = lax.ppermute(for_there, 'l', SWAP)]
    all_to_all x0 -> x1, starting transfers between devices: none -> 15.1 us  [shards(): seeds = lax.all_to_all(seeds, 'z', 0, 0)]
    all_to_all x0 -> x1, waiting for transfers between devices: none -> 9.48 us  [shards(): seeds = lax.all_to_all(seeds, 'z', 0, 0)]
    ppermute x0 -> x2, starting transfers between devices: none -> 6.21 us  [the longest x1 3.11 us: shards(): rows_there = lax.ppermute(rows_own, 'l', SWAP)]
    pallas_call x2 -> x3, Pallas kernels: 5.79 us -> 7.09 us  [run(): pl.pallas_call(kernel, out_shape=outs, in_specs=[pl.BlockSpec(memory_spac...]
  transfers between devices with their start and end apart: 3 -> 6, of which waited for: 2 -> 5; matrix products, arithmetic and copies ran while one was open for 2% -> 3% of each run, Pallas kernels for 2% -> 4%
where the time goes in v2:
time: 145 us; the launch traced here: 143 us
  blocking collectives  44.4 us (31%)
  starting transfers between devices  35.7 us (25%)
  waiting for transfers between devices  33.9 us (23%)
  between operations  13.7 us (9%)
  Pallas kernels  7.09 us (5%)
  local copies, waits for them, and re-layouts  5.35 us (4%)
  other arithmetic  2.93 us (2%)
    all_to_all x1, blocking collectives, shards(): shares = lax.all_to_all(pair_sum.reshape(ny, slab, depth), 'y', 0, 0)  23.5 us
    all_to_all x1, blocking collectives, shards(): lax.all_to_all(jnp.broadcast_to(seeds[None], (ny, slab, depth)), 'y', 0, 0)  20.9 us
    all_to_all x1, starting transfers between devices, shards(): seeds = lax.all_to_all(seeds, 'z', 0, 0)  15.1 us
    ppermute x1, waiting for transfers between devices, shards(): arrived = lax.ppermute(for_there, 'l', SWAP)  11.7 us
    all_to_all x1, waiting for transfers between devices, shards(): seeds = lax.all_to_all(seeds, 'z', 0, 0)  9.48 us
    ppermute x1, starting transfers between devices, shards(): cols_there = lax.ppermute(cols, 'c', SWAP)  8.97 us
    ppermute x1, waiting for transfers between devices, shards(): rows_there = lax.ppermute(rows_own, 'l', SWAP)  8.09 us
    pallas_call x3, Pallas kernels, run(): pl.pallas_call(kernel, out_shape=outs, in_specs=[pl.BlockSpec(memory_spac...  7.09 us
  transfers between devices with their start and end apart: 6, of which 5 were waited for; matrix products, arithmetic and copies ran while one was open for 3% of the time, Pallas kernels for 4%

profile of v2, /device:TPU:1, one launch (start us, length us, event | category | flops | bytes accessed | tf_op | source)
XLA Modules:
  0.0 143.1 jit_solution(12339053946019453227)
XLA Ops:
  6.5 0.0 copy-start.1
  6.5 0.0 all-gather.2.cloned.1.call-start
  6.5 1.1 convert_element_type.18
  7.6 0.0 copy-start.2
  7.6 0.0 copy-start.3
  7.6 0.1 pad_maximum_fusion.2
  7.7 5.5 %collective-permute-start = (bf16[12,24,128]{2,1,0:T(8,128)(2,1)S(1)}, bf16[12,24,128]{2,1,0:T(8,128)(2,1)S(1)}, u32[]{:S(2)}, u32[]{:S(2)}) collective-permute-start(bf16[12,24,128]{2,1,0:T(8,128)(2,1)S(1)} %pad_maximum_fusion.2), channel_id=1, source_target_pairs={{0,32},{32,0},{1,33},{33,1},{2,34},{34,2},{3,35},{35,3},{4,36},{36... | collective-permute-start | bytes 221192 | tf_op jit(solution)/shard_map/ppermute | solution.py:75
  13.2 1.7 %collective-permute-done = bf16[12,24,128]{2,1,0:T(8,128)(2,1)S(1)} collective-permute-done((bf16[12,24,128]{2,1,0:T(8,128)(2,1)S(1)}, bf16[12,24,128]{2,1,0:T(8,128)(2,1)S(1)}, u32[]{:S(2)}, u32[]{:S(2)}) %collective-permute-start) | collective-permute-done | bytes 73760 | tf_op jit(solution)/shard_map/ppermute | solution.py:75
  15.0 0.1 fusion.3
  15.1 0.0 copy-done.1
  15.1 0.1 broadcast_select_fusion.1
  15.1 0.8 pad_maximum_fusion.1
  15.9 0.0 all-gather.2.cloned.1.call-update
  15.9 0.0 copy-done.2
  15.9 0.1 reshape_reshape.3
  16.0 0.1 reshape.83
  16.2 0.0 copy-done.3
  16.2 0.6 dynamic_slice.30
  16.8 0.6 dynamic-slice_subtract_fusion
  17.5 0.1 reshape.85
  17.6 0.1 reshape.84
  17.7 1.5 %dynamic-slice_bitcast_fusion = bf16[12,24,128]{2,1,0:T(8,128)(2,1)} fusion(bf16[12,2,24,128]{3,2,1,0:T(8,128)(2,1)} %bitcast.22, s32[]{:T(128)S(6)} %select_n.49), kind=kLoop, calls=%fused_computation.8 | loop fusion | bytes 147460 | tf_op jit(solution)/shard_map/jit(dynamic_index_in_dim)/squeeze | solution.py:80
  19.2 15.1 %all-to-all-start = ((bf16[12,24,128]{2,1,0:T(8,128)(2,1)}), bf16[12,24,128]{2,1,0:T(8,128)(2,1)S(1)}, u32[]{:S(2)}, u32[]{:S(2)}) async-start(bf16[12,24,128]{2,1,0:T(8,128)(2,1)} %dynamic-slice_bitcast_fusion), calls=%async_computation | async-start | bytes 147456 | tf_op jit(solution)/shard_map/all_to_all | solution.py:81
  34.3 0.1 broadcast_subtract_fusion
  34.4 0.1 sub.77.col_e
  34.5 0.1 sub.72.col_e
  34.6 9.5 %all-to-all-done = bf16[12,24,128]{2,1,0:T(8,128)(2,1)S(1)} async-done(((bf16[12,24,128]{2,1,0:T(8,128)(2,1)}), bf16[12,24,128]{2,1,0:T(8,128)(2,1)S(1)}, u32[]{:S(2)}, u32[]{:S(2)}) %all-to-all-start) | async-done | bytes 73760 | tf_op jit(solution)/shard_map/all_to_all | solution.py:81
  44.1 20.9 %all_to_all.15 = bf16[8,24,1536]{2,1,0:T(8,128)(2,1)S(1)} all-to-all(bf16[8,24,1536]{2,1,0:T(8,128)(2,1)S(1)} %broadcast_in_dim.4), channel_id=1, replica_groups=mesh['z'=12,'h'=2,'l'=2,'y'=8,'c'=2] {'y'}, dimensions={0} | all-to-all | bytes 1179648 | tf_op jit(solution)/shard_map/all_to_all | solution.py:100
  65.0 3.1 %collective-permute-start.1 = (bf16[192,1536]{1,0:T(8,128)(2,1)S(1)}, bf16[192,1536]{1,0:T(8,128)(2,1)S(1)}, u32[]{:S(2)}, u32[]{:S(2)}) collective-permute-start(bf16[192,1536]{1,0:T(8,128)(2,1)S(1)} %bitcast.17), channel_id=1, source_target_pairs={{0,16},{16,0},{1,17},{17,1},{2,18},{18,2},{3,19},{19,3},{4,20},{20... | collective-permute-start | bytes 1769480 | tf_op jit(solution)/shard_map/ppermute | solution.py:102
  68.1 8.1 %collective-permute-done.1.there_ref.rows_ref = bf16[192,1536]{1,0:T(8,128)(2,1)S(1)} collective-permute-done((bf16[192,1536]{1,0:T(8,128)(2,1)S(1)}, bf16[192,1536]{1,0:T(8,128)(2,1)S(1)}, u32[]{:S(2)}, u32[]{:S(2)}) %collective-permute-start.1) | collective-permute-done | bytes 589856 | tf_op jit(solution)/shard_map/ppermute | solution.py:102
  76.2 2.9 %all-gather.2.cloned.1.call-done.cols_ref = bf16[12,576,128]{2,1,0:T(8,128)(2,1)} async-done(((bf16[1,576,128]{2,1,0:T(8,128)(2,1)}), bf16[12,576,128]{2,1,0:T(8,128)(2,1)}) %all-gather.2.cloned.1.call-update) | async-done | bytes 1769488 | tf_op jit(solution)/shard_map/all_gather | solution.py:79
  79.1 9.0 %collective-permute-start.2 = (bf16[12,576,128]{2,1,0:T(8,128)(2,1)}, bf16[12,576,128]{2,1,0:T(8,128)(2,1)S(1)}, u32[]{:S(2)}, u32[]{:S(2)}) collective-permute-start(bf16[12,576,128]{2,1,0:T(8,128)(2,1)} %all-gather.2.cloned.1.call-done.cols_ref), channel_id=1, source_target_pairs={{0,1},{1,0},{2,3},{3,2},{4,5},{5,4},{6,7},{7,6},{8,9},{9,8},{10,11... | collective-permute-start | bytes 5308424 | tf_op jit(solution)/shard_map/ppermute | solution.py:104
  88.0 0.1 copy.17.own_e.row_e
  88.2 0.1 copy.15.there_e.row_e
  88.3 0.0 copy-start
  88.3 1.5 %copy-done = bf16[12,576,128]{2,1,0:T(8,128)(2,1)S(1)} copy-done((bf16[12,576,128]{2,1,0:T(8,128)(2,1)S(1)}, bf16[12,576,128]{2,1,0:T(8,128)(2,1)}, u32[]{:S(2)}) %copy-start) | copy-done | bytes 1769496
  89.8 3.1 %shard_map.37 = (f32[192,1536]{1,0:T(8,128)S(1)}, f32[192,1536]{1,0:T(8,128)S(1)}) custom-call(bf16[12,576,128]{2,1,0:T(8,128)(2,1)S(1)} %copy-done, f32[1,576]{1,0:T(1,128)S(1)} %sub.72.col_e, bf16[192,1536]{1,0:T(8,128)(2,1)S(1)} %collective-permute-done.1.there_ref.rows_ref, f32[192,1]{1,0:T(8,128)S(1)} %copy.15.there_e.row_e, ...), custom_call_target="tpu_custom_call" | custom-call | flops 1358954496 | bytes 3538944 | tf_op jit(solution)/shard_map/pallas_call | solution.py:54
  92.9 0.0 collective-permute-done.2.cols_ref
  92.9 2.0 %shard_map.39 = bf16[192,1536]{1,0:T(8,128)(2,1)S(1)} custom-call(bf16[12,576,128]{2,1,0:T(8,128)(2,1)S(1)} %collective-permute-done.2.cols_ref, f32[1,576]{1,0:T(1,128)S(1)} %sub.77.col_e, bf16[192,1536]{1,0:T(8,128)(2,1)S(1)} %collective-permute-done.1.there_ref.rows_ref, f32[192,1]{1,0:T(8,128)S(1)} %copy.15.there_e.row_e, ...), custom_call_target="tpu_custom_call" | custom-call | flops 679477248 | bytes 3538944 | tf_op jit(solution)/shard_map/pallas_call | solution.py:54
  94.9 3.1 %collective-permute-start.3 = (bf16[192,1536]{1,0:T(8,128)(2,1)S(1)}, bf16[192,1536]{1,0:T(8,128)(2,1)S(1)}, u32[]{:S(2)}, u32[]{:S(2)}) collective-permute-start(bf16[192,1536]{1,0:T(8,128)(2,1)S(1)} %shard_map.39), channel_id=1, source_target_pairs={{0,16},{16,0},{1,17},{17,1},{2,18},{18,2},{3,19},{19,3},{4,20},{20... | collective-permute-start | bytes 1769480 | tf_op jit(solution)/shard_map/ppermute | solution.py:114
  98.0 2.0 %shard_map.38 = f32[192,1536]{1,0:T(8,128)S(1)} custom-call(bf16[12,576,128]{2,1,0:T(8,128)(2,1)S(1)} %collective-permute-done.2.cols_ref, f32[1,576]{1,0:T(1,128)S(1)} %sub.77.col_e, bf16[192,1536]{1,0:T(8,128)(2,1)S(1)} %bitcast.19, f32[192,1]{1,0:T(8,128)S(1)} %copy.17.own_e.row_e, f32[192,1536]{1,0:T(8,128)S(1)} %get-tuple-element.23.before_ref), custom_call_target="tpu_custom_call" | custom-call | flops 679477248 | bytes 3538944 | tf_op jit(solution)/shard_map/pallas_call | solution.py:54
  100.0 11.7 %collective-permute-done.3 = bf16[192,1536]{1,0:T(8,128)(2,1)S(1)} collective-permute-done((bf16[192,1536]{1,0:T(8,128)(2,1)S(1)}, bf16[192,1536]{1,0:T(8,128)(2,1)S(1)}, u32[]{:S(2)}, u32[]{:S(2)}) %collective-permute-start.3) | collective-permute-done | bytes 589856 | tf_op jit(solution)/shard_map/ppermute | solution.py:114
  111.7 0.1 add_convert_fusion
  111.9 23.5 %all_to_all.16 = bf16[8,24,1536]{2,1,0:T(8,128)(2,1)S(1)} all-to-all(bf16[8,24,1536]{2,1,0:T(8,128)(2,1)S(1)} %bitcast.20), channel_id=1, replica_groups=mesh['z'=12,'h'=2,'l'=2,'y'=8,'c'=2] {'y'}, dimensions={0} | all-to-all | bytes 1179648 | tf_op jit(solution)/shard_map/all_to_all | solution.py:119
  135.4 0.1 convert_reduce_fusion
  135.5 0.8 broadcast_in_dim.5
  (7 shorter events, 0.1 us)
Async XLA Ops:
  6.5 8.5 %copy-start.1 = (f32[24,24,64]{2,1,0:T(8,128)S(1)}, f32[24,24,64]{2,1,0:T(8,128)}, u32[]{:S(2)}) copy-start(f32[24,24,64]{2,1,0:T(8,128)} %param.3) | copy-start | bytes 442372
  6.5 72.5 %all-gather.2.cloned.1.call-start = ((), (), s32[]{:S(2)}) async-start(), calls=%async_computation.3 | async-start | bytes 1916928 | tf_op jit(solution)/shard_map/all_gather | solution.py:79
  7.6 8.3 %copy-start.2 = (s32[768]{0:T(1024)S(1)}, s32[768]{0:T(1024)}, u32[]{:S(2)}) copy-start(s32[768]{0:T(1024)} %param.5) | copy-start | bytes 9220
  7.6 8.6 %copy-start.3 = (s32[24]{0:T(128)S(1)}, s32[24]{0:T(128)}, u32[]{:S(2)}) copy-start(s32[24]{0:T(128)} %param.4) | copy-start | bytes 292
  7.7 7.2 %collective-permute-start = (bf16[12,24,128]{2,1,0:T(8,128)(2,1)S(1)}, bf16[12,24,128]{2,1,0:T(8,128)(2,1)S(1)}, u32[]{:S(2)}, u32[]{:S(2)}) collective-permute-start(bf16[12,24,128]{2,1,0:T(8,128)(2,1)S(1)} %pad_maximum_fusion.2), channel_id=1, source_target_pairs={{0,32},{32,0},{1,33},{33,1},{2,34},{34,2},{3,35},{35,3},{4,36},{36... | collective-permute-start | bytes 221192 | tf_op jit(solution)/shard_map/ppermute | solution.py:75
  19.2 24.8 %all-to-all-start = ((bf16[12,24,128]{2,1,0:T(8,128)(2,1)}), bf16[12,24,128]{2,1,0:T(8,128)(2,1)S(1)}, u32[]{:S(2)}, u32[]{:S(2)}) async-start(bf16[12,24,128]{2,1,0:T(8,128)(2,1)} %dynamic-slice_bitcast_fusion), calls=%async_computation | async-start | bytes 147456 | tf_op jit(solution)/shard_map/all_to_all | solution.py:81
  65.0 11.2 %collective-permute-start.1 = (bf16[192,1536]{1,0:T(8,128)(2,1)S(1)}, bf16[192,1536]{1,0:T(8,128)(2,1)S(1)}, u32[]{:S(2)}, u32[]{:S(2)}) collective-permute-start(bf16[192,1536]{1,0:T(8,128)(2,1)S(1)} %bitcast.17), channel_id=1, source_target_pairs={{0,16},{16,0},{1,17},{17,1},{2,18},{18,2},{3,19},{19,3},{4,20},{20... | collective-permute-start | bytes 1769480 | tf_op jit(solution)/shard_map/ppermute | solution.py:102
  79.1 13.8 %collective-permute-start.2 = (bf16[12,576,128]{2,1,0:T(8,128)(2,1)}, bf16[12,576,128]{2,1,0:T(8,128)(2,1)S(1)}, u32[]{:S(2)}, u32[]{:S(2)}) collective-permute-start(bf16[12,576,128]{2,1,0:T(8,128)(2,1)} %all-gather.2.cloned.1.call-done.cols_ref), channel_id=1, source_target_pairs={{0,1},{1,0},{2,3},{3,2},{4,5},{5,4},{6,7},{7,6},{8,9},{9,8},{10,11... | collective-permute-start | bytes 5308424 | tf_op jit(solution)/shard_map/ppermute | solution.py:104
  88.3 1.5 %copy-start = (bf16[12,576,128]{2,1,0:T(8,128)(2,1)S(1)}, bf16[12,576,128]{2,1,0:T(8,128)(2,1)}, u32[]{:S(2)}) copy-start(bf16[12,576,128]{2,1,0:T(8,128)(2,1)} %all-gather.2.cloned.1.call-done.cols_ref) | copy-start | bytes 5308420
  94.9 16.8 %collective-permute-start.3 = (bf16[192,1536]{1,0:T(8,128)(2,1)S(1)}, bf16[192,1536]{1,0:T(8,128)(2,1)S(1)}, u32[]{:S(2)}, u32[]{:S(2)}) collective-permute-start(bf16[192,1536]{1,0:T(8,128)(2,1)S(1)} %shard_map.39), channel_id=1, source_target_pairs={{0,16},{16,0},{1,17},{17,1},{2,18},{18,2},{3,19},{19,3},{4,20},{20... | collective-permute-start | bytes 1769480 | tf_op jit(solution)/shard_map/ppermute | solution.py:114
Sparse Core Ops, SparseCore 0:
  16.0 62.9 all-gather.1

commit v3 on v0

v3 whole, which is shorter than its diff:
```python
import jax
import jax.numpy as jnp
from jax import lax
from jax.experimental import pallas as pl
from jax.experimental.pallas import tpu as pltpu
from jax.sharding import Mesh, PartitionSpec as P

occupied_base = -0.4
occupied_step = 0.01
virtual_base = 0.1
virtual_step = 0.01
spin_scale = 1.3

SWAP = [(0, 1), (1, 0)]


def density_kernel(places, nz, rows_ref, row_e, col_e, *refs):
    blocks, (out_ref, full, sem) = refs[:-3], refs[-3:]
    width = full.shape[0] // 2
    z, c = lax.axis_index("z"), lax.axis_index("c")
    sign = 1 - 2 * c
    copies = []
    for block, parts in zip(blocks, places):
        for first, slab, steps in parts:
            place = pl.multiple_of(lax.rem(z + sign * steps + nz, nz) * 128, 128)
            half = slab if isinstance(slab, int) else (c if slab == "c" else 1 - c)
            copies.append(
                pltpu.make_async_copy(
                    block.at[pl.ds(first, width)],
                    full.at[pl.ds(pl.multiple_of(half * width, width), width), pl.ds(place, 128)],
                    sem.at[len(copies)],
                )
            )
    for copy in copies:
        copy.start()
    for copy in copies:
        copy.wait()
    for first in range(0, full.shape[0], width):
        held = full[first : first + width]
        pair = lax.dot_general(
            rows_ref[...], held, (((1,), (1,)), ((), ())), preferred_element_type=jnp.float32
        )
        amplitude = spin_scale * pair / (row_e[...] + col_e[:, first : first + width])
        term = jnp.dot(amplitude.astype(jnp.bfloat16), held, preferred_element_type=jnp.float32)
        total = term if first == 0 else total + term
    out_ref[...] = total.astype(out_ref.dtype)


def shards(integrals, occ_bins, vir_bins):
    nz, nh, nl, ny = (lax.axis_size(k) for k in ("z", "h", "l", "y"))
    z, h, l, y, c = (lax.axis_index(k) for k in ("z", "h", "l", "y", "c"))
    nj, slab, part = integrals.shape
    depth = nz * nh * part
    width = nj * slab
    own = integrals.astype(jnp.bfloat16)
    packed = jnp.concatenate([own[: nj // 2], own[nj // 2 :]], axis=2)
    there = lax.ppermute(packed, "h", SWAP)
    other = jnp.concatenate([there[:, :, :part], there[:, :, part:]], axis=0)
    first = h == 0
    wide = jnp.concatenate([jnp.where(first, own, other), jnp.where(first, other, own)], axis=2)
    wide = wide.reshape(width, nh * part)
    seeds = lax.all_to_all(own, ("z", "h"), 0, 0)
    wide_there = lax.ppermute(wide, "c", SWAP)
    lead = c == 0
    block = jnp.concatenate(
        [jnp.where(lead, wide, wide_there), jnp.where(lead, wide_there, wide)], axis=0
    )
    ring = [(2 * k, 2 * ((k + 1) % nz)) for k in range(nz)]
    ring += [(2 * k + 1, 2 * ((k + nz - 1) % nz) + 1) for k in range(nz)]
    steps = nz // 2
    step_one, seeds = lax.optimization_barrier((lax.ppermute(block, ("z", "c"), ring), seeds))
    blocks = [block, step_one]
    for _ in range(steps - 2):
        blocks.append(lax.ppermute(blocks[-1], ("z", "c"), ring))
    seeds = jnp.transpose(seeds, (1, 0, 2)).reshape(slab, depth)
    rows = lax.all_to_all(jnp.broadcast_to(seeds[None], (nl * ny, slab, depth)), ("l", "y"), 0, 0)
    rows = rows.reshape(nl * ny * slab, depth)
    mine = lax.dynamic_slice_in_dim(blocks[-1], c * width, width, 0)
    last = lax.ppermute(mine, ("z", "c"), ring)
    early = jnp.concatenate(blocks[1:4], axis=0)
    late = jnp.concatenate(blocks[4:] + [last], axis=0)
    early_there = lax.ppermute(early, "c", SWAP)
    late_there = lax.ppermute(late, "c", SWAP)

    occupied = occupied_base - occupied_step * occ_bins.astype(jnp.float32)
    virtual = virtual_base + virtual_step * vir_bins.astype(jnp.float32)
    virtual = virtual.reshape(nl * ny, 2, slab)
    occ_own = lax.dynamic_index_in_dim(occupied, z * nh + h, 0, keepdims=False)
    row_e = (lax.dynamic_index_in_dim(virtual, c, 1, keepdims=False) - occ_own).reshape(-1, 1)
    of_chip = lax.dynamic_index_in_dim(virtual, l * ny + y, 0, keepdims=False)
    col_e = (of_chip[:, None, :] - occupied[None, :, None]).reshape(1, -1)

    def whole(at, ahead):
        return [(at, 0, ahead), (at + width, 1, ahead)]

    places = [whole(0, -k) for k in range(steps)]
    places.append([(0, "c", steps)])
    places.append(sum([whole(2 * width * k, k + 1) for k in range(3)], []))
    rest = steps - 4
    places.append(
        sum([whole(2 * width * k, k + 4) for k in range(rest)], []) + [(2 * width * rest, "d", steps)]
    )

    vmem = pl.BlockSpec(memory_space=pltpu.VMEM)
    hbm = pl.BlockSpec(memory_space=pl.ANY)
    held = blocks + [last, early_there, late_there]
    partial_term = pl.pallas_call(
        lambda *refs: density_kernel(places, nz, *refs),
        out_shape=jax.ShapeDtypeStruct(rows.shape, jnp.bfloat16),
        in_specs=[vmem, vmem, vmem] + [hbm] * len(held),
        out_specs=vmem,
        scratch_shapes=[
            pltpu.VMEM((2 * width, depth), jnp.bfloat16),
            pltpu.SemaphoreType.DMA((2 * nz,)),
        ],
        compiler_params=pltpu.CompilerParams(vmem_limit_bytes=32 * 1024 * 1024),
        cost_estimate=pl.CostEstimate(
            flops=8 * rows.shape[0] * width * depth, bytes_accessed=4 * width * depth, transcendentals=0
        ),
    )(rows, row_e, col_e, *held)
    shares = lax.all_to_all(partial_term.reshape(nl * ny, slab, depth), ("l", "y"), 0, 0)
    density = jnp.sum(shares.astype(jnp.float32), axis=0)
    return density[:, None, :]


def solution(mesh):
    fine = Mesh(mesh.devices.reshape(12, 2, 2, 8, 2), ("z", "h", "l", "y", "c"))
    in_specs = (P(None, ("l", "y", "c"), ("z", "h")), P(), P())
    out_specs = P(("l", "y", "c"), ("z", "h"), None)
    return jax.shard_map(shards, mesh=fine, in_specs=in_specs, out_specs=out_specs, check_vma=False)
```

time: 411 us -> 146 us (0.36)
  waiting for transfers between devices: 369 us -> 17.2 us
  starting transfers between devices: 0.09 us -> 60.3 us
  blocking collectives: 0 us -> 52.7 us
  local copies, waits for them, and re-layouts: 17.8 us -> 3.34 us
  between operations: 13.2 us -> 0.3 us
  matrix products: 8.45 us -> 0 us
  Pallas kernels: 0 us -> 5.91 us
    all_gather x2 -> x0, waiting for transfers between devices: 243 us -> none  [the longest x1 186 us: shards(): j_blocks = lax.all_gather(rounded, 'occ', axis=2, tiled=True)]
    reduce_scatter x1 -> x0, waiting for transfers between devices: 126 us -> none  [shards(): lax.psum_scatter(partial_term, 'vir', scatter_dimension=0, tiled=True)]
    ppermute x0 -> x10, starting transfers between devices: none -> 53.1 us  [the longest x4 13.8 us: shards(): blocks.append(lax.ppermute(blocks[-1], ('z', 'c'), ring))]
    all_to_all x0 -> x2, blocking collectives: none -> 52.7 us  [the longest x1 36.2 us: shards(): lax.all_to_all(partial_term.reshape(nl * ny, slab, depth), ('l', 'y'), 0, 0)]
    ppermute x0 -> x10, waiting for transfers between devices: none -> 17.2 us  [the longest x4 14.1 us: shards(): blocks.append(lax.ppermute(blocks[-1], ('z', 'c'), ring))]
    all_gather x1 -> x0, local copies, waits for them, and re-layouts: 10.6 us -> none  [shards(): j_blocks = lax.all_gather(rounded, 'occ', axis=2, tiled=True)]
    dot_general x1 -> x0, matrix products: 8.45 us -> none  [shards(): jnp.einsum('iajb,jbp->aip', amplitude, j_blocks, preferred_element_type=j...]
    all_to_all x0 -> x1, starting transfers between devices: none -> 7.24 us  [shards(): lax.all_to_all(jnp.broadcast_to(seeds[None], (nl * ny, slab, depth)), ('l...]
  transfers between devices with their start and end apart: 3 -> 11, of which waited for: 3 -> 6; matrix products, arithmetic and copies ran while one was open for 3% -> 4% of each run, Pallas kernels for 0% -> 0%
where the time goes in v3:
time: 146 us; the launch traced here: 144 us
  starting transfers between devices  60.3 us (41%)
  blocking collectives  52.7 us (36%)
  waiting for transfers between devices  17.2 us (12%)
  Pallas kernels  5.91 us (4%)
  other arithmetic  4.19 us (3%)
  local copies, waits for them, and re-layouts  3.34 us (2%)
    all_to_all x1, blocking collectives, shards(): lax.all_to_all(partial_term.reshape(nl * ny, slab, depth), ('l', 'y'), 0, 0)  36.2 us
    all_to_all x1, blocking collectives, shards(): seeds = lax.all_to_all(own, ('z', 'h'), 0, 0)  16.4 us
    ppermute x4, waiting for transfers between devices, shards(): blocks.append(lax.ppermute(blocks[-1], ('z', 'c'), ring))  14.1 us
    ppermute x4, starting transfers between devices, shards(): blocks.append(lax.ppermute(blocks[-1], ('z', 'c'), ring))  13.8 us
    ppermute x1, starting transfers between devices, shards(): wide_there = lax.ppermute(wide, 'c', SWAP)  13 us
    ppermute x1, starting transfers between devices, shards(): early_there = lax.ppermute(early, 'c', SWAP)  7.52 us
    all_to_all x1, starting transfers between devices, shards(): lax.all_to_all(jnp.broadcast_to(seeds[None], (nl * ny, slab, depth)), ('l...  7.24 us
    pallas_call x1, Pallas kernels, shards(): pl.pallas_call(lambda *refs: density_kernel(places, nz, *refs), out_shape...  5.91 us
  transfers between devices with their start and end apart: 11, of which 6 were waited for; matrix products, arithmetic and copies ran while one was open for 4% of the time, Pallas kernels for 0%

profile of v3, /device:TPU:1, one launch (start us, length us, event | category | flops | bytes accessed | tf_op | source)
XLA Modules:
  0.0 143.9 jit_solution(6493720957156702924)
XLA Ops:
  0.0 0.0 copy-start
  0.0 1.1 convert_element_type.12
  1.1 0.1 pad_maximum_fusion.5
  1.2 5.5 %collective-permute-start = (bf16[12,24,128]{2,1,0:T(8,128)(2,1)S(1)}, bf16[12,24,128]{2,1,0:T(8,128)(2,1)S(1)}, u32[]{:S(2)}, u32[]{:S(2)}) collective-permute-start(bf16[12,24,128]{2,1,0:T(8,128)(2,1)S(1)} %pad_maximum_fusion.5), channel_id=1, source_target_pairs={{0,32},{32,0},{1,33},{33,1},{2,34},{34,2},{3,35},{35,3},{4,36},{36... | collective-permute-start | bytes 221192 | tf_op jit(solution)/shard_map/ppermute | solution.py:57
  6.7 1.7 %collective-permute-done = bf16[12,24,128]{2,1,0:T(8,128)(2,1)S(1)} collective-permute-done((bf16[12,24,128]{2,1,0:T(8,128)(2,1)S(1)}, bf16[12,24,128]{2,1,0:T(8,128)(2,1)S(1)}, u32[]{:S(2)}, u32[]{:S(2)}) %collective-permute-start) | collective-permute-done | bytes 73760 | tf_op jit(solution)/shard_map/ppermute | solution.py:57
  8.4 0.1 fusion.1
  8.5 0.0 copy-done
  8.5 0.1 broadcast_select_fusion.1
  8.6 0.1 pad_maximum_fusion.4
  8.7 13.0 %collective-permute-start.1 = (bf16[576,128]{1,0:T(8,128)(2,1)S(1)}, bf16[576,128]{1,0:T(8,128)(2,1)S(1)}, u32[]{:S(2)}, u32[]{:S(2)}) collective-permute-start(bf16[576,128]{1,0:T(8,128)(2,1)S(1)} %bitcast.12), channel_id=1, source_target_pairs={{0,1},{1,0},{2,3},{3,2},{4,5},{5,4},{6,7},{7,6},{8,9},{9,8},{10,11... | collective-permute-start | bytes 442376 | tf_op jit(solution)/shard_map/ppermute | solution.py:63
  21.7 1.0 collective-permute-done.1
  22.7 5.3 %collective-permute-start.2 = (bf16[1152,128]{1,0:T(8,128)(2,1)S(1)}, bf16[1152,128]{1,0:T(8,128)(2,1)S(1)}, u32[]{:S(2)}, u32[]{:S(2)}) collective-permute-start(bf16[1152,128]{1,0:T(8,128)(2,1)S(1)} %pad_maximum_fusion.2.refs_3_), channel_id=1, source_target_pairs={{0,64},{64,128},{128,192},{192,256},{256,320},{320,384},{384,448},... | collective-permute-start | bytes 884744 | tf_op jit(solution)/shard_map/ppermute | solution.py:71
  28.0 0.1 reshape.63
  28.1 16.4 %all_to_all.15 = bf16[24,2,768]{2,1,0:T(2,128)(2,1)S(1)} all-to-all(bf16[24,2,768]{2,1,0:T(2,128)(2,1)S(1)} %reshape.63), channel_id=1, replica_groups=mesh['z'=12,'h'=2,'l'=2,'y'=8,'c'=2] {'z','h'}, dimensions={0} | all-to-all | bytes 147456 | tf_op jit(solution)/shard_map/all_to_all | solution.py:62
  44.6 0.1 reshape.64
  44.7 0.0 collective-permute-done.2.refs_4_
  44.7 2.8 %collective-permute-start.3 = (bf16[1152,128]{1,0:T(8,128)(2,1)S(1)}, bf16[1152,128]{1,0:T(8,128)(2,1)S(1)}, u32[]{:S(2)}, u32[]{:S(2)}) collective-permute-start(bf16[1152,128]{1,0:T(8,128)(2,1)S(1)} %collective-permute-done.2.refs_4_), channel_id=1, source_target_pairs={{0,64},{64,128},{128,192},{192,256},{256,320},{320,384},{384,448},... | collective-permute-start | bytes 884744 | tf_op jit(solution)/shard_map/ppermute | solution.py:74
  47.6 4.6 %collective-permute-done.3.refs_5_ = bf16[1152,128]{1,0:T(8,128)(2,1)S(1)} collective-permute-done((bf16[1152,128]{1,0:T(8,128)(2,1)S(1)}, bf16[1152,128]{1,0:T(8,128)(2,1)S(1)}, u32[]{:S(2)}, u32[]{:S(2)}) %collective-permute-start.3) | collective-permute-done | bytes 294944 | tf_op jit(solution)/shard_map/ppermute | solution.py:74
  52.2 4.0 %collective-permute-start.4 = (bf16[1152,128]{1,0:T(8,128)(2,1)S(1)}, bf16[1152,128]{1,0:T(8,128)(2,1)S(1)}, u32[]{:S(2)}, u32[]{:S(2)}) collective-permute-start(bf16[1152,128]{1,0:T(8,128)(2,1)S(1)} %collective-permute-done.3.refs_5_), channel_id=1, source_target_pairs={{0,64},{64,128},{128,192},{192,256},{256,320},{320,384},{384,448},... | collective-permute-start | bytes 884744 | tf_op jit(solution)/shard_map/ppermute | solution.py:74
  56.3 3.6 %collective-permute-done.4.refs_6_ = bf16[1152,128]{1,0:T(8,128)(2,1)S(1)} collective-permute-done((bf16[1152,128]{1,0:T(8,128)(2,1)S(1)}, bf16[1152,128]{1,0:T(8,128)(2,1)S(1)}, u32[]{:S(2)}, u32[]{:S(2)}) %collective-permute-start.4) | collective-permute-done | bytes 294944 | tf_op jit(solution)/shard_map/ppermute | solution.py:74
  59.9 5.0 %collective-permute-start.5 = (bf16[1152,128]{1,0:T(8,128)(2,1)S(1)}, bf16[1152,128]{1,0:T(8,128)(2,1)S(1)}, u32[]{:S(2)}, u32[]{:S(2)}) collective-permute-start(bf16[1152,128]{1,0:T(8,128)(2,1)S(1)} %collective-permute-done.4.refs_6_), channel_id=1, source_target_pairs={{0,64},{64,128},{128,192},{192,256},{256,320},{320,384},{384,448},... | collective-permute-start | bytes 884744 | tf_op jit(solution)/shard_map/ppermute | solution.py:74
  65.0 0.2 broadcast_in_dim.12
  65.1 1.1 broadcast_in_dim.13
  66.2 7.2 %all-to-all-start.1 = ((bf16[16,24,1536]{2,1,0:T(8,128)(2,1)}), bf16[16,24,1536]{2,1,0:T(8,128)(2,1)S(1)}, u32[]{:S(2)}, u32[]{:S(2)}) async-start(bf16[16,24,1536]{2,1,0:T(8,128)(2,1)} %broadcast_in_dim.13), calls=%async_computation.1 | async-start | bytes 2359296 | tf_op jit(solution)/shard_map/all_to_all | solution.py:76
  73.5 0.0 collective-permute-done.5.refs_7_
  73.5 1.9 %collective-permute-start.6 = (bf16[1152,128]{1,0:T(8,128)(2,1)S(1)}, bf16[1152,128]{1,0:T(8,128)(2,1)S(1)}, u32[]{:S(2)}, u32[]{:S(2)}) collective-permute-start(bf16[1152,128]{1,0:T(8,128)(2,1)S(1)} %collective-permute-done.5.refs_7_), channel_id=1, source_target_pairs={{0,64},{64,128},{128,192},{192,256},{256,320},{320,384},{384,448},... | collective-permute-start | bytes 884744 | tf_op jit(solution)/shard_map/ppermute | solution.py:74
  75.4 5.8 %collective-permute-done.6.refs_8_ = bf16[1152,128]{1,0:T(8,128)(2,1)S(1)} collective-permute-done((bf16[1152,128]{1,0:T(8,128)(2,1)S(1)}, bf16[1152,128]{1,0:T(8,128)(2,1)S(1)}, u32[]{:S(2)}, u32[]{:S(2)}) %collective-permute-start.6) | collective-permute-done | bytes 294944 | tf_op jit(solution)/shard_map/ppermute | solution.py:74
  81.3 2.8 %collective-permute-start.7 = (bf16[576,128]{1,0:T(8,128)(2,1)S(1)}, bf16[576,128]{1,0:T(8,128)(2,1)S(1)}, u32[]{:S(2)}, u32[]{:S(2)}) collective-permute-start(bf16[576,128]{1,0:T(8,128)(2,1)S(1)} %constant_dynamic-slice_fusion), channel_id=1, source_target_pairs={{0,64},{64,128},{128,192},{192,256},{256,320},{320,384},{384,448},... | collective-permute-start | bytes 442376 | tf_op jit(solution)/shard_map/ppermute | solution.py:79
  84.1 1.0 pad_maximum_fusion
  85.1 7.5 %collective-permute-start.8 = (bf16[3456,128]{1,0:T(8,128)(2,1)}, bf16[3456,128]{1,0:T(8,128)(2,1)}, u32[]{:S(2)}, u32[]{:S(2)}) collective-permute-start(bf16[3456,128]{1,0:T(8,128)(2,1)} %pad_maximum_fusion), channel_id=1, source_target_pairs={{0,1},{1,0},{2,3},{3,2},{4,5},{5,4},{6,7},{7,6},{8,9},{9,8},{10,11... | collective-permute-start | bytes 2654216 | tf_op jit(solution)/shard_map/ppermute | solution.py:82
  92.6 0.0 collective-permute-done.7.refs_9_
  92.6 0.9 pad_maximum_fusion.1
  93.6 5.2 %collective-permute-start.9 = (bf16[2880,128]{1,0:T(8,128)(2,1)}, bf16[2880,128]{1,0:T(8,128)(2,1)}, u32[]{:S(2)}, u32[]{:S(2)}) collective-permute-start(bf16[2880,128]{1,0:T(8,128)(2,1)} %pad_maximum_fusion.1), channel_id=1, source_target_pairs={{0,1},{1,0},{2,3},{3,2},{4,5},{5,4},{6,7},{7,6},{8,9},{9,8},{10,11... | collective-permute-start | bytes 2211848 | tf_op jit(solution)/shard_map/ppermute | solution.py:83
  98.7 0.0 copy-done.1
  98.8 0.1 reshape.54
  98.8 0.0 copy-done.2
  98.9 0.6 dynamic_slice.16
  99.5 0.7 subtract_reduce_fusion
  100.1 0.1 sub.53.refs_1_
  100.3 0.1 broadcast_subtract_fusion
  100.4 0.1 sub.52.refs_2_
  100.5 0.0 collective-permute-done.8.refs_10_
  100.5 0.4 collective-permute-done.9.refs_11_
  100.9 0.0 all-to-all-done.1
  100.9 5.9 %shard_map.37 = bf16[384,1536]{1,0:T(8,128)(2,1)S(1)} custom-call(bf16[384,1536]{1,0:T(8,128)(2,1)S(1)} %bitcast.9, f32[384,1]{1,0:T(8,128)S(1)} %sub.53.refs_1_, f32[1,1152]{1,0:T(1,128)S(1)} %sub.52.refs_2_, bf16[1152,128]{1,0:T(8,128)(2,1)S(1)} %pad_maximum_fusion.2.refs_3_, bf16[1152,128]{1,0:T(8,128)(2,1)S(1)} %collective-permute-done.2.refs_4_, ...), custom_call_target="tpu_custom_call" | custom-call | flops 2717908992 | bytes 3538944 | tf_op jit(solution)/shard_map/pallas_call | solution.py:107
  106.8 36.2 %all_to_all.16 = bf16[16,24,1536]{2,1,0:T(8,128)(2,1)S(1)} all-to-all(bf16[16,24,1536]{2,1,0:T(8,128)(2,1)S(1)} %bitcast.10), channel_id=1, replica_groups=mesh['z'=12,'h'=2,'l'=2,'y'=8,'c'=2] {'l','y'}, dimensions={0} | all-to-all | bytes 2359296 | tf_op jit(solution)/shard_map/all_to_all | solution.py:121
  143.0 0.2 convert_reduce_fusion
  143.2 0.8 broadcast_in_dim.14
  (10 shorter events, 0.1 us)
Async XLA Ops:
  0.0 8.5 %copy-start = (f32[24,24,64]{2,1,0:T(8,128)S(1)}, f32[24,24,64]{2,1,0:T(8,128)}, u32[]{:S(2)}) copy-start(f32[24,24,64]{2,1,0:T(8,128)} %param.3) | copy-start | bytes 442372
  1.2 7.2 %collective-permute-start = (bf16[12,24,128]{2,1,0:T(8,128)(2,1)S(1)}, bf16[12,24,128]{2,1,0:T(8,128)(2,1)S(1)}, u32[]{:S(2)}, u32[]{:S(2)}) collective-permute-start(bf16[12,24,128]{2,1,0:T(8,128)(2,1)S(1)} %pad_maximum_fusion.5), channel_id=1, source_target_pairs={{0,32},{32,0},{1,33},{33,1},{2,34},{34,2},{3,35},{35,3},{4,36},{36... | collective-permute-start | bytes 221192 | tf_op jit(solution)/shard_map/ppermute | solution.py:57
  8.7 14.0 %collective-permute-start.1 = (bf16[576,128]{1,0:T(8,128)(2,1)S(1)}, bf16[576,128]{1,0:T(8,128)(2,1)S(1)}, u32[]{:S(2)}, u32[]{:S(2)}) collective-permute-start(bf16[576,128]{1,0:T(8,128)(2,1)S(1)} %bitcast.12), channel_id=1, source_target_pairs={{0,1},{1,0},{2,3},{3,2},{4,5},{5,4},{6,7},{7,6},{8,9},{9,8},{10,11... | collective-permute-start | bytes 442376 | tf_op jit(solution)/shard_map/ppermute | solution.py:63
  22.7 22.0 %collective-permute-start.2 = (bf16[1152,128]{1,0:T(8,128)(2,1)S(1)}, bf16[1152,128]{1,0:T(8,128)(2,1)S(1)}, u32[]{:S(2)}, u32[]{:S(2)}) collective-permute-start(bf16[1152,128]{1,0:T(8,128)(2,1)S(1)} %pad_maximum_fusion.2.refs_3_), channel_id=1, source_target_pairs={{0,64},{64,128},{128,192},{192,256},{256,320},{320,384},{384,448},... | collective-permute-start | bytes 884744 | tf_op jit(solution)/shard_map/ppermute | solution.py:71
  44.7 7.5 %collective-permute-start.3 = (bf16[1152,128]{1,0:T(8,128)(2,1)S(1)}, bf16[1152,128]{1,0:T(8,128)(2,1)S(1)}, u32[]{:S(2)}, u32[]{:S(2)}) collective-permute-start(bf16[1152,128]{1,0:T(8,128)(2,1)S(1)} %collective-permute-done.2.refs_4_), channel_id=1, source_target_pairs={{0,64},{64,128},{128,192},{192,256},{256,320},{320,384},{384,448},... | collective-permute-start | bytes 884744 | tf_op jit(solution)/shard_map/ppermute | solution.py:74
  52.2 7.7 %collective-permute-start.4 = (bf16[1152,128]{1,0:T(8,128)(2,1)S(1)}, bf16[1152,128]{1,0:T(8,128)(2,1)S(1)}, u32[]{:S(2)}, u32[]{:S(2)}) collective-permute-start(bf16[1152,128]{1,0:T(8,128)(2,1)S(1)} %collective-permute-done.3.refs_5_), channel_id=1, source_target_pairs={{0,64},{64,128},{128,192},{192,256},{256,320},{320,384},{384,448},... | collective-permute-start | bytes 884744 | tf_op jit(solution)/shard_map/ppermute | solution.py:74
  59.9 13.6 %collective-permute-start.5 = (bf16[1152,128]{1,0:T(8,128)(2,1)S(1)}, bf16[1152,128]{1,0:T(8,128)(2,1)S(1)}, u32[]{:S(2)}, u32[]{:S(2)}) collective-permute-start(bf16[1152,128]{1,0:T(8,128)(2,1)S(1)} %collective-permute-done.4.refs_6_), channel_id=1, source_target_pairs={{0,64},{64,128},{128,192},{192,256},{256,320},{320,384},{384,448},... | collective-permute-start | bytes 884744 | tf_op jit(solution)/shard_map/ppermute | solution.py:74
  66.2 34.7 %all-to-all-start.1 = ((bf16[16,24,1536]{2,1,0:T(8,128)(2,1)}), bf16[16,24,1536]{2,1,0:T(8,128)(2,1)S(1)}, u32[]{:S(2)}, u32[]{:S(2)}) async-start(bf16[16,24,1536]{2,1,0:T(8,128)(2,1)} %broadcast_in_dim.13), calls=%async_computation.1 | async-start | bytes 2359296 | tf_op jit(solution)/shard_map/all_to_all | solution.py:76
  73.5 7.8 %collective-permute-start.6 = (bf16[1152,128]{1,0:T(8,128)(2,1)S(1)}, bf16[1152,128]{1,0:T(8,128)(2,1)S(1)}, u32[]{:S(2)}, u32[]{:S(2)}) collective-permute-start(bf16[1152,128]{1,0:T(8,128)(2,1)S(1)} %collective-permute-done.5.refs_7_), channel_id=1, source_target_pairs={{0,64},{64,128},{128,192},{192,256},{256,320},{320,384},{384,448},... | collective-permute-start | bytes 884744 | tf_op jit(solution)/shard_map/ppermute | solution.py:74
  81.3 11.4 %collective-permute-start.7 = (bf16[576,128]{1,0:T(8,128)(2,1)S(1)}, bf16[576,128]{1,0:T(8,128)(2,1)S(1)}, u32[]{:S(2)}, u32[]{:S(2)}) collective-permute-start(bf16[576,128]{1,0:T(8,128)(2,1)S(1)} %constant_dynamic-slice_fusion), channel_id=1, source_target_pairs={{0,64},{64,128},{128,192},{192,256},{256,320},{320,384},{384,448},... | collective-permute-start | bytes 442376 | tf_op jit(solution)/shard_map/ppermute | solution.py:79
  85.1 13.6 %copy-start.1 = (s32[768]{0:T(1024)S(1)}, s32[768]{0:T(1024)}, u32[]{:S(2)}) copy-start(s32[768]{0:T(1024)} %param.5) | copy-start | bytes 9220
  85.1 13.7 %copy-start.2 = (s32[24]{0:T(128)S(1)}, s32[24]{0:T(128)}, u32[]{:S(2)}) copy-start(s32[24]{0:T(128)} %param.4) | copy-start | bytes 292
  85.1 15.4 %collective-permute-start.8 = (bf16[3456,128]{1,0:T(8,128)(2,1)}, bf16[3456,128]{1,0:T(8,128)(2,1)}, u32[]{:S(2)}, u32[]{:S(2)}) collective-permute-start(bf16[3456,128]{1,0:T(8,128)(2,1)} %pad_maximum_fusion), channel_id=1, source_target_pairs={{0,1},{1,0},{2,3},{3,2},{4,5},{5,4},{6,7},{7,6},{8,9},{9,8},{10,11... | collective-permute-start | bytes 2654216 | tf_op jit(solution)/shard_map/ppermute | solution.py:82
  93.6 7.3 %collective-permute-start.9 = (bf16[2880,128]{1,0:T(8,128)(2,1)}, bf16[2880,128]{1,0:T(8,128)(2,1)}, u32[]{:S(2)}, u32[]{:S(2)}) collective-permute-start(bf16[2880,128]{1,0:T(8,128)(2,1)} %pad_maximum_fusion.1), channel_id=1, source_target_pairs={{0,1},{1,0},{2,3},{3,2},{4,5},{5,4},{6,7},{7,6},{8,9},{9,8},{10,11... | collective-permute-start | bytes 2211848 | tf_op jit(solution)/shard_map/ppermute | solution.py:83

commit v4 on v1

v4 whole, which is shorter than its diff:
```python
import jax
import jax.numpy as jnp
from jax import lax
from jax.experimental import pallas as pl
from jax.experimental.pallas import tpu as pltpu
from jax.sharding import Mesh, PartitionSpec as P

occupied_base = -0.4
occupied_step = 0.01
virtual_base = 0.1
virtual_step = 0.01
spin_scale = 1.3

SWAP = [(0, 1), (1, 0)]


def load(cols_refs, full, sem):
    copies = []
    for n, cols_ref in enumerate(cols_refs):
        chunks, width, lanes = cols_ref.shape
        for k in range(chunks):
            place = full.at[pl.ds(n * width, width), pl.ds(k * lanes, lanes)]
            copies.append(pltpu.make_async_copy(cols_ref.at[k], place, sem.at[n, k]))
    for copy in copies:
        copy.start()
    for copy in copies:
        copy.wait()


def density_kernel(blocks, more, rows_ref, row_e, col_e, *refs):
    cols_refs, refs = refs[:blocks], refs[blocks:]
    before_ref = refs[0] if more else None
    out_ref, full, sem = refs[-3:]
    load(cols_refs, full, sem)
    pair = lax.dot_general(
        rows_ref[...], full[...], (((1,), (1,)), ((), ())), preferred_element_type=jnp.float32
    )
    amplitude = (spin_scale * pair / (row_e[...] + col_e[...])).astype(jnp.bfloat16)
    term = jnp.dot(amplitude, full[...], preferred_element_type=jnp.float32)
    if more:
        term = term + before_ref[...]
    out_ref[...] = term.astype(out_ref.dtype)


def run(rows, row_e, col_e, cols, before=None):
    chunks, width, lanes = cols[0].shape
    blocks, more = len(cols), before is not None
    vmem = pl.BlockSpec(memory_space=pltpu.VMEM)
    anywhere = pl.BlockSpec(memory_space=pl.ANY)
    work = 4 * rows.shape[0] * blocks * width * chunks * lanes
    return pl.pallas_call(
        lambda *refs: density_kernel(blocks, more, *refs),
        out_shape=jax.ShapeDtypeStruct(rows.shape, jnp.bfloat16 if more else jnp.float32),
        in_specs=[vmem] * 3 + [anywhere] * blocks + [vmem] * more,
        out_specs=vmem,
        scratch_shapes=[
            pltpu.VMEM((blocks * width, chunks * lanes), jnp.bfloat16),
            pltpu.SemaphoreType.DMA((blocks, chunks)),
        ],
        compiler_params=pltpu.CompilerParams(vmem_limit_bytes=24 * 1024 * 1024),
        cost_estimate=pl.CostEstimate(flops=work, bytes_accessed=work // 256, transcendentals=0),
    )(rows, row_e, col_e, *cols, *([before] if more else []))


def shards(integrals, occ_bins, vir_bins):
    nz, nh, nl, ny = (lax.axis_size(k) for k in ("z", "h", "l", "y"))
    z, h, l, y, c = (lax.axis_index(k) for k in ("z", "h", "l", "y", "c"))
    nj, slab, part = integrals.shape
    depth = nz * nh * part
    own = integrals.astype(jnp.bfloat16)
    packed = jnp.concatenate([own[: nj // 2], own[nj // 2 :]], axis=2)
    there = lax.ppermute(packed, "h", SWAP)
    other = jnp.concatenate([there[:, :, :part], there[:, :, part:]], axis=0)
    first = h == 0
    wide = jnp.concatenate([jnp.where(first, own, other), jnp.where(first, other, own)], axis=2)
    early = wide[: nj // 2].reshape(nj // 2 * slab, nh * part)
    late = wide[nj // 2 :].reshape(nj // 2 * slab, nh * part)
    seeds = lax.dynamic_index_in_dim(wide.reshape(nz, nh, slab, nh * part), h, 1, keepdims=False)
    seeds = lax.all_to_all(seeds, "z", 0, 0)
    cols_early = lax.all_gather(early, "z", axis=0, tiled=False)
    cols_early, seeds = lax.optimization_barrier((cols_early, seeds))
    seeds = jnp.transpose(seeds, (1, 0, 2)).reshape(slab, depth)
    seeds = jnp.broadcast_to(seeds[None], (nl * ny, slab, depth))
    late, seeds = lax.optimization_barrier((late, seeds))
    cols_late = lax.all_gather(late, "z", axis=0, tiled=False)
    rows = lax.all_to_all(seeds, ("l", "y"), 0, 0).reshape(nl * ny * slab, depth)
    early_there = lax.ppermute(cols_early, "c", SWAP)
    late_there = lax.ppermute(cols_late, "c", SWAP)

    occupied = occupied_base - occupied_step * occ_bins.astype(jnp.float32)
    virtual = virtual_base + virtual_step * vir_bins.astype(jnp.float32)
    virtual = virtual.reshape(nl * ny, 2, slab)
    occ_own = lax.dynamic_index_in_dim(occupied, z * nh + h, 0, keepdims=False)
    row_e = (lax.dynamic_index_in_dim(virtual, c, 1, keepdims=False) - occ_own).reshape(-1, 1)
    of_chip = lax.dynamic_index_in_dim(virtual, l * ny + y, 0, keepdims=False)
    col_own = lax.dynamic_index_in_dim(of_chip, c, 0, keepdims=False)
    col_there = lax.dynamic_index_in_dim(of_chip, 1 - c, 0, keepdims=False)
    halves = occupied.reshape(2, nj // 2, 1)
    pick = lambda half, col: (col[None, :] - halves[half]).reshape(1, -1)
    col_most = jnp.concatenate([pick(0, col_own), pick(0, col_there), pick(1, col_own)], axis=1)
    col_rest = pick(1, col_there)

    most = run(rows, row_e, col_most, [cols_early, early_there, cols_late])
    partial_term = run(rows, row_e, col_rest, [late_there], most)
    shares = lax.all_to_all(partial_term.reshape(nl * ny, slab, depth), ("l", "y"), 0, 0)
    density = jnp.sum(shares.astype(jnp.float32), axis=0)
    return density[:, None, :]


def solution(mesh):
    fine = Mesh(mesh.devices.reshape(12, 2, 2, 8, 2), ("z", "h", "l", "y", "c"))
    in_specs = (P(None, ("l", "y", "c"), ("z", "h")), P(), P())
    out_specs = P(("l", "y", "c"), ("z", "h"), None)
    return jax.shard_map(shards, mesh=fine, in_specs=in_specs, out_specs=out_specs, check_vma=False)
```

time: 143 us -> 144 us (level)
  starting transfers between devices: 14.4 us -> 42.5 us
  between operations: 13.6 us -> 0.23 us
  blocking collectives: 94.8 us -> 85.8 us
  waiting for transfers between devices: 5.79 us -> 1.73 us
    all_to_all x3 -> x1, blocking collectives: 94.8 us -> 37.1 us  [shards(): lax.all_to_all(partial_term.reshape(nl * ny, slab, depth), ('l', 'y'), 0, 0)]
    all_gather x0 -> x2, blocking collectives: none -> 48.7 us  [the longest x1 24.8 us: shards(): cols_early = lax.all_gather(early, 'z', axis=0, tiled=False)]
    all_to_all x0 -> x2, starting transfers between devices: none -> 23.1 us  [the longest x1 15.1 us: shards(): seeds = lax.all_to_all(seeds, 'z', 0, 0)]
    ppermute x1 -> x2, starting transfers between devices: 8.96 us -> 13.9 us  [the longest x1 8.82 us: shards(): early_there = lax.ppermute(cols_early, 'c', SWAP)]
    all_gather x1 -> x0, waiting for transfers between devices: 4.05 us -> none  [shards(): lax.all_gather(wide.reshape(nj * slab, 2 * part), 'z', axis=0, tiled=False)]
    unnamed x8 -> x6, local copies, waits for them, and re-layouts: 1.49 us -> 0.01 us
  transfers between devices with their start and end apart: 3 -> 5, of which waited for: 2 -> 1; matrix products, arithmetic and copies ran while one was open for 2% -> 1% of each run, Pallas kernels for 2% -> 3%
where the time goes in v4:
time: 144 us; the launch traced here: 143 us
  blocking collectives  85.8 us (60%)
  starting transfers between devices  42.5 us (30%)
  Pallas kernels  6.39 us (4%)
  local copies, waits for them, and re-layouts  3.83 us (3%)
  other arithmetic  2.43 us (2%)
  waiting for transfers between devices  1.73 us (1%)
    all_to_all x1, blocking collectives, shards(): lax.all_to_all(partial_term.reshape(nl * ny, slab, depth), ('l', 'y'), 0, 0)  37.1 us
    all_gather x1, blocking collectives, shards(): cols_early = lax.all_gather(early, 'z', axis=0, tiled=False)  24.8 us
    all_gather x1, blocking collectives, shards(): cols_late = lax.all_gather(late, 'z', axis=0, tiled=False)  23.9 us
    all_to_all x1, starting transfers between devices, shards(): seeds = lax.all_to_all(seeds, 'z', 0, 0)  15.1 us
    ppermute x1, starting transfers between devices, shards(): early_there = lax.ppermute(cols_early, 'c', SWAP)  8.82 us
    all_to_all x1, starting transfers between devices, shards(): lax.all_to_all(seeds, ('l', 'y'), 0, 0).reshape(nl * ny * slab, depth)  7.98 us
    pallas_call x2, Pallas kernels, run(): pl.pallas_call(lambda *refs: density_kernel(blocks, more, *refs), out_sha...  6.39 us
    ppermute x1, starting transfers between devices, shards(): there = lax.ppermute(packed, 'h', SWAP)  5.48 us
  transfers between devices with their start and end apart: 5, of which 1 were waited for; matrix products, arithmetic and copies ran while one was open for 1% of the time, Pallas kernels for 3%

profile of v4, /device:TPU:1, one launch (start us, length us, event | category | flops | bytes accessed | tf_op | source)
XLA Modules:
  0.0 142.8 jit_solution(5042969353183429254)
XLA Ops:
  0.0 0.0 copy-start
  0.0 1.1 convert_element_type.12
  1.1 0.1 pad_maximum_fusion.2
  1.2 5.5 %collective-permute-start = (bf16[12,24,128]{2,1,0:T(8,128)(2,1)S(1)}, bf16[12,24,128]{2,1,0:T(8,128)(2,1)S(1)}, u32[]{:S(2)}, u32[]{:S(2)}) collective-permute-start(bf16[12,24,128]{2,1,0:T(8,128)(2,1)S(1)} %pad_maximum_fusion.2), channel_id=1, source_target_pairs={{0,32},{32,0},{1,33},{33,1},{2,34},{34,2},{3,35},{35,3},{4,36},{36... | collective-permute-start | bytes 221192 | tf_op jit(solution)/shard_map/ppermute | solution.py:72
  6.7 1.7 %collective-permute-done = bf16[12,24,128]{2,1,0:T(8,128)(2,1)S(1)} collective-permute-done((bf16[12,24,128]{2,1,0:T(8,128)(2,1)S(1)}, bf16[12,24,128]{2,1,0:T(8,128)(2,1)S(1)}, u32[]{:S(2)}, u32[]{:S(2)}) %collective-permute-start) | collective-permute-done | bytes 73760 | tf_op jit(solution)/shard_map/ppermute | solution.py:72
  8.4 0.1 fusion.5
  8.5 0.0 copy-done
  8.6 0.1 pad_maximum_fusion.1
  8.7 0.1 fusion.1
  8.8 0.6 dynamic-slice_bitcast_fusion
  9.4 15.1 %all-to-all-start = ((bf16[12,24,128]{2,1,0:T(8,128)(2,1)}), bf16[12,24,128]{2,1,0:T(8,128)(2,1)S(1)}, u32[]{:S(2)}, u32[]{:S(2)}) async-start(bf16[12,24,128]{2,1,0:T(8,128)(2,1)} %dynamic-slice_bitcast_fusion), calls=%async_computation | async-start | bytes 147456 | tf_op jit(solution)/shard_map/all_to_all | solution.py:79
  24.5 24.8 %all_gather.9.refs_3_ = bf16[12,288,128]{2,1,0:T(8,128)(2,1)S(1)} all-gather(bf16[1,288,128]{2,1,0:T(8,128)(2,1)S(1)} %bitcast.24), channel_id=1, replica_groups=mesh['z'=12,'h'=2,'l'=2,'y'=8,'c'=2] {'z'}, dimensions={0}, use_global_device_ids=true | all-gather | bytes 958464 | tf_op jit(solution)/shard_map/all_gather | solution.py:80
  49.3 0.0 all-to-all-done
  49.4 1.1 broadcast_in_dim.7
  50.5 0.0 copy-start.1
  50.5 0.0 copy-start.2
  50.5 8.0 %all-to-all-start.1 = ((bf16[16,24,1536]{2,1,0:T(8,128)(2,1)}), bf16[16,24,1536]{2,1,0:T(8,128)(2,1)S(1)}, u32[]{:S(2)}, u32[]{:S(2)}) async-start(bf16[16,24,1536]{2,1,0:T(8,128)(2,1)} %broadcast_in_dim.7), calls=%async_computation.1 | async-start | bytes 2359296 | tf_op jit(solution)/shard_map/all_to_all | solution.py:86
  58.5 0.0 copy-done.1
  58.5 8.8 %collective-permute-start.2 = (bf16[12,288,128]{2,1,0:T(8,128)(2,1)S(1)}, bf16[12,288,128]{2,1,0:T(8,128)(2,1)}, u32[]{:S(2)}, u32[]{:S(2)}) collective-permute-start(bf16[12,288,128]{2,1,0:T(8,128)(2,1)S(1)} %all_gather.9.refs_3_), channel_id=1, source_target_pairs={{0,1},{1,0},{2,3},{3,2},{4,5},{5,4},{6,7},{7,6},{8,9},{9,8},{10,11... | collective-permute-start | bytes 2654216 | tf_op jit(solution)/shard_map/ppermute | solution.py:87
  67.3 23.9 %all-gather = bf16[3456,128]{1,0:T(8,128)(2,1)} all-gather(bf16[288,128]{1,0:T(8,128)(2,1)S(1)} %bitcast.23), channel_id=2, replica_groups=mesh['z'=12,'h'=2,'l'=2,'y'=8,'c'=2] {'z'}, dimensions={0}, use_global_device_ids=true | all-gather | bytes 958464 | tf_op jit(solution)/shard_map/all_gather | solution.py:85
  91.2 5.1 %collective-permute-start.1 = (bf16[12,288,128]{2,1,0:T(8,128)(2,1)}, bf16[12,288,128]{2,1,0:T(8,128)(2,1)S(1)}, u32[]{:S(2)}, u32[]{:S(2)}) collective-permute-start(bf16[12,288,128]{2,1,0:T(8,128)(2,1)} %bitcast.8.refs_5_), channel_id=1, source_target_pairs={{0,1},{1,0},{2,3},{3,2},{4,5},{5,4},{6,7},{7,6},{8,9},{9,8},{10,11... | collective-permute-start | bytes 2654216 | tf_op jit(solution)/shard_map/ppermute | solution.py:88
  96.3 0.0 copy-done.2
  96.3 0.1 reshape.135
  96.4 0.6 dynamic_slice.23
  97.0 0.1 fusion.6
  97.1 0.1 broadcast_subtract_fusion.1
  97.2 0.1 sub.124
  97.3 0.1 sub.128
  97.3 0.1 sub.119.refs_2_
  97.4 0.1 sub.126
  97.5 0.7 subtract_reduce_fusion
  98.2 0.1 sub.129.refs_1_
  98.3 0.1 pad_maximum_fusion.3.refs_2_
  98.4 0.0 collective-permute-done.2.refs_4_
  98.4 0.0 all-to-all-done.1
  98.4 4.6 %shard_map.37.refs_4_ = f32[384,1536]{1,0:T(8,128)S(1)} custom-call(bf16[384,1536]{1,0:T(8,128)(2,1)S(1)} %bitcast.19, f32[384,1]{1,0:T(8,128)S(1)} %sub.129.refs_1_, f32[1,864]{1,0:T(1,128)S(1)} %pad_maximum_fusion.3.refs_2_, bf16[12,288,128]{2,1,0:T(8,128)(2,1)S(1)} %all_gather.9.refs_3_, bf16[12,288,128]{2,1,0:T(8,128)(2,1)} %collective-permute-done.2.refs_4_, ...), custom_call_target="tpu_custom_call" | custom-call | flops 2038431744 | bytes 7962624 | tf_op jit(solution)/shard_map/pallas_call | solution.py:51
  103.0 0.0 collective-permute-done.1.refs_3_
  103.1 1.8 %shard_map.38 = bf16[384,1536]{1,0:T(8,128)(2,1)S(1)} custom-call(bf16[384,1536]{1,0:T(8,128)(2,1)S(1)} %bitcast.20, f32[384,1]{1,0:T(8,128)S(1)} %sub.129.refs_1_, f32[1,288]{1,0:T(1,128)S(1)} %sub.119.refs_2_, bf16[12,288,128]{2,1,0:T(8,128)(2,1)S(1)} %collective-permute-done.1.refs_3_, f32[384,1536]{1,0:T(8,128)S(1)} %shard_map.37.refs_4_), custom_call_target="tpu_custom_call" | custom-call | flops 679477248 | bytes 2654208 | tf_op jit(solution)/shard_map/pallas_call | solution.py:51
  104.8 37.1 %all_to_all.15 = bf16[16,24,1536]{2,1,0:T(8,128)(2,1)S(1)} all-to-all(bf16[16,24,1536]{2,1,0:T(8,128)(2,1)S(1)} %bitcast.21), channel_id=1, replica_groups=mesh['z'=12,'h'=2,'l'=2,'y'=8,'c'=2] {'l','y'}, dimensions={0} | all-to-all | bytes 2359296 | tf_op jit(solution)/shard_map/all_to_all | solution.py:105
  141.9 0.2 convert_reduce_fusion
  142.1 0.8 broadcast_in_dim.16
  (6 shorter events, 0.1 us)
Async XLA Ops:
  0.0 8.5 %copy-start = (f32[24,24,64]{2,1,0:T(8,128)S(1)}, f32[24,24,64]{2,1,0:T(8,128)}, u32[]{:S(2)}) copy-start(f32[24,24,64]{2,1,0:T(8,128)} %param.3) | copy-start | bytes 442372
  1.2 7.2 %collective-permute-start = (bf16[12,24,128]{2,1,0:T(8,128)(2,1)S(1)}, bf16[12,24,128]{2,1,0:T(8,128)(2,1)S(1)}, u32[]{:S(2)}, u32[]{:S(2)}) collective-permute-start(bf16[12,24,128]{2,1,0:T(8,128)(2,1)S(1)} %pad_maximum_fusion.2), channel_id=1, source_target_pairs={{0,32},{32,0},{1,33},{33,1},{2,34},{34,2},{3,35},{35,3},{4,36},{36... | collective-permute-start | bytes 221192 | tf_op jit(solution)/shard_map/ppermute | solution.py:72
  9.4 39.9 %all-to-all-start = ((bf16[12,24,128]{2,1,0:T(8,128)(2,1)}), bf16[12,24,128]{2,1,0:T(8,128)(2,1)S(1)}, u32[]{:S(2)}, u32[]{:S(2)}) async-start(bf16[12,24,128]{2,1,0:T(8,128)(2,1)} %dynamic-slice_bitcast_fusion), calls=%async_computation | async-start | bytes 147456 | tf_op jit(solution)/shard_map/all_to_all | solution.py:79
  50.5 8.0 %copy-start.1 = (s32[768]{0:T(1024)S(1)}, s32[768]{0:T(1024)}, u32[]{:S(2)}) copy-start(s32[768]{0:T(1024)} %param.5) | copy-start | bytes 9220
  50.5 45.8 %copy-start.2 = (s32[24]{0:T(128)S(1)}, s32[24]{0:T(128)}, u32[]{:S(2)}) copy-start(s32[24]{0:T(128)} %param.4) | copy-start | bytes 292
  50.5 47.9 %all-to-all-start.1 = ((bf16[16,24,1536]{2,1,0:T(8,128)(2,1)}), bf16[16,24,1536]{2,1,0:T(8,128)(2,1)S(1)}, u32[]{:S(2)}, u32[]{:S(2)}) async-start(bf16[16,24,1536]{2,1,0:T(8,128)(2,1)} %broadcast_in_dim.7), calls=%async_computation.1 | async-start | bytes 2359296 | tf_op jit(solution)/shard_map/all_to_all | solution.py:86
  58.5 39.9 %collective-permute-start.2 = (bf16[12,288,128]{2,1,0:T(8,128)(2,1)S(1)}, bf16[12,288,128]{2,1,0:T(8,128)(2,1)}, u32[]{:S(2)}, u32[]{:S(2)}) collective-permute-start(bf16[12,288,128]{2,1,0:T(8,128)(2,1)S(1)} %all_gather.9.refs_3_), channel_id=1, source_target_pairs={{0,1},{1,0},{2,3},{3,2},{4,5},{5,4},{6,7},{7,6},{8,9},{9,8},{10,11... | collective-permute-start | bytes 2654216 | tf_op jit(solution)/shard_map/ppermute | solution.py:87
  91.2 11.9 %collective-permute-start.1 = (bf16[12,288,128]{2,1,0:T(8,128)(2,1)}, bf16[12,288,128]{2,1,0:T(8,128)(2,1)S(1)}, u32[]{:S(2)}, u32[]{:S(2)}) collective-permute-start(bf16[12,288,128]{2,1,0:T(8,128)(2,1)} %bitcast.8.refs_5_), channel_id=1, source_target_pairs={{0,1},{1,0},{2,3},{3,2},{4,5},{5,4},{6,7},{7,6},{8,9},{9,8},{10,11... | collective-permute-start | bytes 2654216 | tf_op jit(solution)/shard_map/ppermute | solution.py:88

commit v5 on v4

--- a/solution.py
+++ b/solution.py
@@ -15,12 +15,13 @@
 
 
 def load(cols_refs, full, sem):
-    copies = []
+    copies, first = [], 0
     for n, cols_ref in enumerate(cols_refs):
         chunks, width, lanes = cols_ref.shape
         for k in range(chunks):
-            place = full.at[pl.ds(n * width, width), pl.ds(k * lanes, lanes)]
+            place = full.at[pl.ds(first, width), pl.ds(k * lanes, lanes)]
             copies.append(pltpu.make_async_copy(cols_ref.at[k], place, sem.at[n, k]))
+        first += width
     for copy in copies:
         copy.start()
     for copy in copies:
@@ -43,23 +44,24 @@
 
 
 def run(rows, row_e, col_e, cols, before=None):
-    chunks, width, lanes = cols[0].shape
     blocks, more = len(cols), before is not None
+    chunks = cols[0].shape[0]
+    width = sum(block.shape[1] for block in cols)
     vmem = pl.BlockSpec(memory_space=pltpu.VMEM)
     anywhere = pl.BlockSpec(memory_space=pl.ANY)
-    work = 4 * rows.shape[0] * blocks * width * chunks * lanes
+    work = 4 * rows.size * width
     return pl.pallas_call(
         lambda *refs: density_kernel(blocks, more, *refs),
         out_shape=jax.ShapeDtypeStruct(rows.shape, jnp.bfloat16 if more else jnp.float32),
         in_specs=[vmem] * 3 + [anywhere] * blocks + [vmem] * more,
         out_specs=vmem,
         scratch_shapes=[
-            pltpu.VMEM((blocks * width, chunks * lanes), jnp.bfloat16),
+            pltpu.VMEM((width, rows.shape[1]), jnp.bfloat16),
             pltpu.SemaphoreType.DMA((blocks, chunks)),
         ],
         compiler_params=pltpu.CompilerParams(vmem_limit_bytes=24 * 1024 * 1024),
         cost_estimate=pl.CostEstimate(flops=work, bytes_accessed=work // 256, transcendentals=0),
-    )(rows, row_e, col_e, *cols, *([before] if more else []))
+    )(rows, row_e, jnp.concatenate(col_e, axis=1), *cols, *([before] if more else []))
 
 
 def shards(integrals, occ_bins, vir_bins):
@@ -67,23 +69,25 @@
     z, h, l, y, c = (lax.axis_index(k) for k in ("z", "h", "l", "y", "c"))
     nj, slab, part = integrals.shape
     depth = nz * nh * part
+    split = nj * slab // 3
     own = integrals.astype(jnp.bfloat16)
     packed = jnp.concatenate([own[: nj // 2], own[nj // 2 :]], axis=2)
     there = lax.ppermute(packed, "h", SWAP)
     other = jnp.concatenate([there[:, :, :part], there[:, :, part:]], axis=0)
     first = h == 0
     wide = jnp.concatenate([jnp.where(first, own, other), jnp.where(first, other, own)], axis=2)
-    early = wide[: nj // 2].reshape(nj // 2 * slab, nh * part)
-    late = wide[nj // 2 :].reshape(nj // 2 * slab, nh * part)
-    seeds = lax.dynamic_index_in_dim(wide.reshape(nz, nh, slab, nh * part), h, 1, keepdims=False)
-    seeds = lax.all_to_all(seeds, "z", 0, 0)
+    wide = wide.reshape(nj * slab, nh * part)
+    seeds = lax.all_to_all(own, ("z", "h"), 0, 0)
+    seeds = jnp.transpose(seeds, (1, 0, 2)).reshape(slab, depth)
+    early, late = wide[:split], wide[split:]
+    late = jnp.broadcast_to(late[None], (nz,) + late.shape)
+    seeds, late = lax.optimization_barrier((seeds, late))
+    cols_late = lax.all_to_all(late, "z", 0, 0)
+    rows = lax.all_gather(seeds, "y", axis=0, tiled=True)
+    early, rows = lax.optimization_barrier((early, rows))
+    rows_there = lax.ppermute(rows, "l", SWAP)
     cols_early = lax.all_gather(early, "z", axis=0, tiled=False)
-    cols_early, seeds = lax.optimization_barrier((cols_early, seeds))
-    seeds = jnp.transpose(seeds, (1, 0, 2)).reshape(slab, depth)
-    seeds = jnp.broadcast_to(seeds[None], (nl * ny, slab, depth))
-    late, seeds = lax.optimization_barrier((late, seeds))
-    cols_late = lax.all_gather(late, "z", axis=0, tiled=False)
-    rows = lax.all_to_all(seeds, ("l", "y"), 0, 0).reshape(nl * ny * slab, depth)
+    cols_early, cols_late = lax.optimization_barrier((cols_early, cols_late))
     early_there = lax.ppermute(cols_early, "c", SWAP)
     late_there = lax.ppermute(cols_late, "c", SWAP)
 
@@ -95,13 +99,15 @@
     of_chip = lax.dynamic_index_in_dim(virtual, l * ny + y, 0, keepdims=False)
     col_own = lax.dynamic_index_in_dim(of_chip, c, 0, keepdims=False)
     col_there = lax.dynamic_index_in_dim(of_chip, 1 - c, 0, keepdims=False)
-    halves = occupied.reshape(2, nj // 2, 1)
-    pick = lambda half, col: (col[None, :] - halves[half]).reshape(1, -1)
-    col_most = jnp.concatenate([pick(0, col_own), pick(0, col_there), pick(1, col_own)], axis=1)
-    col_rest = pick(1, col_there)
+    col_own = (col_own[None, :] - occupied[:, None]).reshape(1, -1)
+    col_there = (col_there[None, :] - occupied[:, None]).reshape(1, -1)
+    col_here = [col_own[:, split:], col_own[:, :split]]
+    col_rest = [col_there[:, split:], col_there[:, :split]]
 
-    most = run(rows, row_e, col_most, [cols_early, early_there, cols_late])
-    partial_term = run(rows, row_e, col_rest, [late_there], most)
+    both = jnp.concatenate([rows, rows_there], axis=0)
+    rows = jnp.where(l == 0, both, jnp.concatenate([rows_there, rows], axis=0))
+    here = run(rows, row_e, col_here, [cols_late, cols_early])
+    partial_term = run(rows, row_e, col_rest, [late_there, early_there], here)
     shares = lax.all_to_all(partial_term.reshape(nl * ny, slab, depth), ("l", "y"), 0, 0)
     density = jnp.sum(shares.astype(jnp.float32), axis=0)
     return density[:, None, :]

time: 144 us -> 154 us (1.069)
  waiting for transfers between devices: 1.73 us -> 10.9 us
  starting transfers between devices: 42.5 us -> 38.2 us
  blocking collectives: 85.8 us -> 87.8 us
  other arithmetic: 2.43 us -> 4.25 us
    all_to_all x2, waiting for transfers between devices: 0.01 us -> 10.9 us  [the longest x1 10.9 us: shards(): seeds = lax.all_to_all(own, ('z', 'h'), 0, 0)]
    ppermute x1, starting transfers between devices: 8.82 us -> 1.92 us  [shards(): early_there = lax.ppermute(cols_early, 'c', SWAP)]
    all_to_all x2, starting transfers between devices: 23.1 us -> 18.9 us  [the longest x1 15.1 us: shards(): seeds = lax.all_to_all(own, ('z', 'h'), 0, 0)]
    all_gather x1, blocking collectives: 24.8 us -> 28.8 us  [shards(): cols_early = lax.all_gather(early, 'z', axis=0, tiled=False)]
    ppermute x1, starting transfers between devices: 5.1 us -> 8.87 us  [shards(): late_there = lax.ppermute(cols_late, 'c', SWAP)]
    ppermute x0 -> x1, starting transfers between devices: none -> 3.05 us  [shards(): rows_there = lax.ppermute(rows, 'l', SWAP)]
    all_to_all x1, blocking collectives: 37.1 us -> 34.8 us  [shards(): lax.all_to_all(partial_term.reshape(nl * ny, slab, depth), ('l', 'y'), 0, 0)]
    select_n x1 -> x2, other arithmetic: 0.05 us -> 1.97 us  [the longest x1 1.92 us: shards(): rows = jnp.where(l == 0, both, jnp.concatenate([rows_there, rows], axis=0))]
  transfers between devices with their start and end apart: 5 -> 6, of which waited for: 1 -> 1; matrix products, arithmetic and copies ran while one was open for 1% -> 3% of each run, Pallas kernels for 3% -> 2%
where the time goes in v5:
time: 154 us; the launch traced here: 152 us
  blocking collectives  87.8 us (57%)
  starting transfers between devices  38.2 us (25%)
  waiting for transfers between devices  10.9 us (7%)
  Pallas kernels  6.11 us (4%)
  local copies, waits for them, and re-layouts  4.34 us (3%)
  other arithmetic  4.25 us (3%)
    all_to_all x1, blocking collectives, shards(): lax.all_to_all(partial_term.reshape(nl * ny, slab, depth), ('l', 'y'), 0, 0)  34.8 us
    all_gather x1, blocking collectives, shards(): cols_early = lax.all_gather(early, 'z', axis=0, tiled=False)  28.8 us
    all_gather x1, blocking collectives, shards(): rows = lax.all_gather(seeds, 'y', axis=0, tiled=True)  24.2 us
    all_to_all x1, starting transfers between devices, shards(): seeds = lax.all_to_all(own, ('z', 'h'), 0, 0)  15.1 us
    all_to_all x1, waiting for transfers between devices, shards(): seeds = lax.all_to_all(own, ('z', 'h'), 0, 0)  10.9 us
    ppermute x1, starting transfers between devices, shards(): late_there = lax.ppermute(cols_late, 'c', SWAP)  8.87 us
    pallas_call x2, Pallas kernels, run(): pl.pallas_call(lambda *refs: density_kernel(blocks, more, *refs), out_sha...  6.11 us
    ppermute x1, starting transfers between devices, shards(): there = lax.ppermute(packed, 'h', SWAP)  5.48 us
  transfers between devices with their start and end apart: 6, of which 1 were waited for; matrix products, arithmetic and copies ran while one was open for 3% of the time, Pallas kernels for 2%

profile of v5, /device:TPU:1, one launch (start us, length us, event | category | flops | bytes accessed | tf_op | source)
XLA Modules:
  0.0 152.0 jit_solution(14031165328933963519)
XLA Ops:
  0.0 0.0 copy-start
  0.0 1.1 convert_element_type.12
  1.1 0.1 pad_maximum_fusion.2
  1.2 5.5 %collective-permute-start = (bf16[12,24,128]{2,1,0:T(8,128)(2,1)S(1)}, bf16[12,24,128]{2,1,0:T(8,128)(2,1)S(1)}, u32[]{:S(2)}, u32[]{:S(2)}) collective-permute-start(bf16[12,24,128]{2,1,0:T(8,128)(2,1)S(1)} %pad_maximum_fusion.2), channel_id=1, source_target_pairs={{0,32},{32,0},{1,33},{33,1},{2,34},{34,2},{3,35},{35,3},{4,36},{36... | collective-permute-start | bytes 221192 | tf_op jit(solution)/shard_map/ppermute | solution.py:75
  6.7 0.8 reshape.89
  7.4 15.1 %all-to-all-start = ((bf16[24,2,768]{2,1,0:T(2,128)(2,1)}), bf16[24,2,768]{2,1,0:T(2,128)(2,1)S(1)}, u32[]{:S(2)}, u32[]{:S(2)}) async-start(bf16[24,2,768]{2,1,0:T(2,128)(2,1)} %reshape.89), calls=%async_computation | async-start | bytes 147456 | tf_op jit(solution)/shard_map/all_to_all | solution.py:80
  22.6 0.0 collective-permute-done
  22.6 0.1 fusion.3
  22.7 0.0 copy-done
  22.7 0.1 broadcast_select_fusion.1
  22.7 0.1 pad_maximum_fusion.1
  22.8 10.9 %all-to-all-done = bf16[24,2,768]{2,1,0:T(2,128)(2,1)S(1)} async-done(((bf16[24,2,768]{2,1,0:T(2,128)(2,1)}), bf16[24,2,768]{2,1,0:T(2,128)(2,1)S(1)}, u32[]{:S(2)}, u32[]{:S(2)}) %all-to-all-start) | async-done | bytes 73760 | tf_op jit(solution)/shard_map/all_to_all | solution.py:80
  33.8 0.1 reshape.90
  34.0 0.2 reshape.78
  34.1 1.2 broadcast_in_dim.7
  35.3 0.0 copy-start.1
  35.3 3.8 %all-to-all-start.1 = ((bf16[12,384,128]{2,1,0:T(8,128)(2,1)}), bf16[12,384,128]{2,1,0:T(8,128)(2,1)S(1)}, u32[]{:S(2)}, u32[]{:S(2)}) async-start(bf16[12,384,128]{2,1,0:T(8,128)(2,1)} %broadcast_in_dim.7), calls=%async_computation.1 | async-start | bytes 2359296 | tf_op jit(solution)/shard_map/all_to_all | solution.py:85
  39.2 0.0 copy-done.1
  39.2 0.0 copy-start.2
  39.2 0.1 pad_maximum_fusion.3
  39.3 24.2 %all_gather.9 = bf16[192,1536]{1,0:T(8,128)(2,1)} all-gather(bf16[24,1536]{1,0:T(8,128)(2,1)S(1)} %reshape.78), channel_id=1, replica_groups=mesh['z'=12,'h'=2,'l'=2,'y'=8,'c'=2] {'y'}, dimensions={0}, use_global_device_ids=true | all-gather | bytes 663552 | tf_op jit(solution)/shard_map/all_gather | solution.py:86
  63.5 3.1 %collective-permute-start.1 = (bf16[192,1536]{1,0:T(8,128)(2,1)}, bf16[192,1536]{1,0:T(8,128)(2,1)}, u32[]{:S(2)}, u32[]{:S(2)}) collective-permute-start(bf16[192,1536]{1,0:T(8,128)(2,1)} %all_gather.9), channel_id=1, source_target_pairs={{0,16},{16,0},{1,17},{17,1},{2,18},{18,2},{3,19},{19,3},{4,20},{20... | collective-permute-start | bytes 1769480 | tf_op jit(solution)/shard_map/ppermute | solution.py:88
  66.5 28.8 %all-gather = bf16[2304,128]{1,0:T(8,128)(2,1)S(1)} all-gather(bf16[192,128]{1,0:T(8,128)(2,1)S(1)} %bitcast.15), channel_id=2, replica_groups=mesh['z'=12,'h'=2,'l'=2,'y'=8,'c'=2] {'z'}, dimensions={0}, use_global_device_ids=true | all-gather | bytes 638976 | tf_op jit(solution)/shard_map/all_gather | solution.py:89
  95.4 0.0 all-to-all-done.1.refs_3_
  95.4 8.9 %collective-permute-start.2 = (bf16[12,384,128]{2,1,0:T(8,128)(2,1)S(1)}, bf16[12,384,128]{2,1,0:T(8,128)(2,1)S(1)}, u32[]{:S(2)}, u32[]{:S(2)}) collective-permute-start(bf16[12,384,128]{2,1,0:T(8,128)(2,1)S(1)} %all-to-all-done.1.refs_3_), channel_id=1, source_target_pairs={{0,1},{1,0},{2,3},{3,2},{4,5},{5,4},{6,7},{7,6},{8,9},{9,8},{10,11... | collective-permute-start | bytes 3538952 | tf_op jit(solution)/shard_map/ppermute | solution.py:92
  104.3 0.0 copy-done.2
  104.3 0.1 reshape.79
  104.4 0.1 broadcast_subtract_fusion
  104.5 0.1 sub.83
  104.6 0.1 slice.51
  104.7 0.1 sub.79
  104.8 0.1 slice.49
  104.8 0.6 dynamic_slice.18
  105.4 0.7 subtract_reduce_fusion
  106.1 0.1 sub.84.refs_1_
  106.2 1.9 %collective-permute-start.3 = (bf16[12,192,128]{2,1,0:T(8,128)(2,1)S(1)}, bf16[12,192,128]{2,1,0:T(8,128)(2,1)S(1)}, u32[]{:S(2)}, u32[]{:S(2)}) collective-permute-start(bf16[12,192,128]{2,1,0:T(8,128)(2,1)S(1)} %bitcast.11), channel_id=1, source_target_pairs={{0,1},{1,0},{2,3},{3,2},{4,5},{5,4},{6,7},{7,6},{8,9},{9,8},{10,11... | collective-permute-start | bytes 1769480 | tf_op jit(solution)/shard_map/ppermute | solution.py:91
  108.2 0.0 collective-permute-done.1
  108.2 1.9 %maximum_select_fusion.refs_0_ = bf16[384,1536]{1,0:T(8,128)(2,1)S(1)} fusion(bf16[192,1536]{1,0:T(8,128)(2,1)} %collective-permute-done.1, bf16[192,1536]{1,0:T(8,128)(2,1)} %all_gather.9, pred[]{:T(512)S(6)} %eq.6), kind=kLoop, calls=%fused_computation.1 | loop fusion | flops 5308416 | bytes 2359297 | tf_op jit(solution)/shard_map/jit(_where)/select_n | solution.py:108
  110.1 3.0 %shard_map.37.refs_5_ = f32[384,1536]{1,0:T(8,128)S(1)} custom-call(bf16[384,1536]{1,0:T(8,128)(2,1)S(1)} %maximum_select_fusion.refs_0_, f32[384,1]{1,0:T(8,128)S(1)} %sub.84.refs_1_, f32[1,576]{1,0:T(1,128)S(1)} %pad_maximum_fusion.5.refs_2_, bf16[12,384,128]{2,1,0:T(8,128)(2,1)S(1)} %all-to-all-done.1.refs_3_, bf16[12,192,128]{2,1,0:T(8,128)(2,1)S(1)} %bitcast.12), custom_call_target="tpu_custom_call" | custom-call | flops 1358954496 | bytes 5308416 | tf_op jit(solution)/shard_map/pallas_call | solution.py:53
  113.2 0.0 collective-permute-done.3.refs_4_
  113.2 0.0 collective-permute-done.2.refs_3_
  113.2 3.1 %shard_map.38 = bf16[384,1536]{1,0:T(8,128)(2,1)S(1)} custom-call(bf16[384,1536]{1,0:T(8,128)(2,1)S(1)} %maximum_select_fusion.refs_0_, f32[384,1]{1,0:T(8,128)S(1)} %sub.84.refs_1_, f32[1,576]{1,0:T(1,128)S(1)} %pad_maximum_fusion.4.refs_2_, bf16[12,384,128]{2,1,0:T(8,128)(2,1)S(1)} %collective-permute-done.2.refs_3_, ...), custom_call_target="tpu_custom_call" | custom-call | flops 1358954496 | bytes 5308416 | tf_op jit(solution)/shard_map/pallas_call | solution.py:53
  116.3 34.8 %all_to_all.15 = bf16[16,24,1536]{2,1,0:T(8,128)(2,1)S(1)} all-to-all(bf16[16,24,1536]{2,1,0:T(8,128)(2,1)S(1)} %bitcast.10), channel_id=1, replica_groups=mesh['z'=12,'h'=2,'l'=2,'y'=8,'c'=2] {'l','y'}, dimensions={0} | all-to-all | bytes 2359296 | tf_op jit(solution)/shard_map/all_to_all | solution.py:111
  151.1 0.2 convert_reduce_fusion
  151.2 0.8 broadcast_in_dim.8
  (9 shorter events, 0.1 us)
Async XLA Ops:
  0.0 22.7 %copy-start = (f32[24,24,64]{2,1,0:T(8,128)S(1)}, f32[24,24,64]{2,1,0:T(8,128)}, u32[]{:S(2)}) copy-start(f32[24,24,64]{2,1,0:T(8,128)} %param.3) | copy-start | bytes 442372
  1.2 21.4 %collective-permute-start = (bf16[12,24,128]{2,1,0:T(8,128)(2,1)S(1)}, bf16[12,24,128]{2,1,0:T(8,128)(2,1)S(1)}, u32[]{:S(2)}, u32[]{:S(2)}) collective-permute-start(bf16[12,24,128]{2,1,0:T(8,128)(2,1)S(1)} %pad_maximum_fusion.2), channel_id=1, source_target_pairs={{0,32},{32,0},{1,33},{33,1},{2,34},{34,2},{3,35},{35,3},{4,36},{36... | collective-permute-start | bytes 221192 | tf_op jit(solution)/shard_map/ppermute | solution.py:75
  7.4 26.3 %all-to-all-start = ((bf16[24,2,768]{2,1,0:T(2,128)(2,1)}), bf16[24,2,768]{2,1,0:T(2,128)(2,1)S(1)}, u32[]{:S(2)}, u32[]{:S(2)}) async-start(bf16[24,2,768]{2,1,0:T(2,128)(2,1)} %reshape.89), calls=%async_computation | async-start | bytes 147456 | tf_op jit(solution)/shard_map/all_to_all | solution.py:80
  35.3 3.8 %copy-start.1 = (s32[768]{0:T(1024)S(1)}, s32[768]{0:T(1024)}, u32[]{:S(2)}) copy-start(s32[768]{0:T(1024)} %param.5) | copy-start | bytes 9220
  35.3 60.0 %all-to-all-start.1 = ((bf16[12,384,128]{2,1,0:T(8,128)(2,1)}), bf16[12,384,128]{2,1,0:T(8,128)(2,1)S(1)}, u32[]{:S(2)}, u32[]{:S(2)}) async-start(bf16[12,384,128]{2,1,0:T(8,128)(2,1)} %broadcast_in_dim.7), calls=%async_computation.1 | async-start | bytes 2359296 | tf_op jit(solution)/shard_map/all_to_all | solution.py:85
  39.2 65.1 %copy-start.2 = (s32[24]{0:T(128)S(1)}, s32[24]{0:T(128)}, u32[]{:S(2)}) copy-start(s32[24]{0:T(128)} %param.4) | copy-start | bytes 292
  63.5 44.7 %collective-permute-start.1 = (bf16[192,1536]{1,0:T(8,128)(2,1)}, bf16[192,1536]{1,0:T(8,128)(2,1)}, u32[]{:S(2)}, u32[]{:S(2)}) collective-permute-start(bf16[192,1536]{1,0:T(8,128)(2,1)} %all_gather.9), channel_id=1, source_target_pairs={{0,16},{16,0},{1,17},{17,1},{2,18},{18,2},{3,19},{19,3},{4,20},{20... | collective-permute-start | bytes 1769480 | tf_op jit(solution)/shard_map/ppermute | solution.py:88
  95.4 17.8 %collective-permute-start.2 = (bf16[12,384,128]{2,1,0:T(8,128)(2,1)S(1)}, bf16[12,384,128]{2,1,0:T(8,128)(2,1)S(1)}, u32[]{:S(2)}, u32[]{:S(2)}) collective-permute-start(bf16[12,384,128]{2,1,0:T(8,128)(2,1)S(1)} %all-to-all-done.1.refs_3_), channel_id=1, source_target_pairs={{0,1},{1,0},{2,3},{3,2},{4,5},{5,4},{6,7},{7,6},{8,9},{9,8},{10,11... | collective-permute-start | bytes 3538952 | tf_op jit(solution)/shard_map/ppermute | solution.py:92
  106.2 6.9 %collective-permute-start.3 = (bf16[12,192,128]{2,1,0:T(8,128)(2,1)S(1)}, bf16[12,192,128]{2,1,0:T(8,128)(2,1)S(1)}, u32[]{:S(2)}, u32[]{:S(2)}) collective-permute-start(bf16[12,192,128]{2,1,0:T(8,128)(2,1)S(1)} %bitcast.11), channel_id=1, source_target_pairs={{0,1},{1,0},{2,3},{3,2},{4,5},{5,4},{6,7},{7,6},{8,9},{9,8},{10,11... | collective-permute-start | bytes 1769480 | tf_op jit(solution)/shard_map/ppermute | solution.py:91

commit v6 on v4

v6 whole, which is shorter than its diff:
```python
import jax
import jax.numpy as jnp
from jax import lax
from jax.experimental import pallas as pl
from jax.experimental.pallas import tpu as pltpu
from jax.sharding import Mesh, PartitionSpec as P

occupied_base = -0.4
occupied_step = 0.01
virtual_base = 0.1
virtual_step = 0.01
spin_scale = 1.3

SWAP = [(0, 1), (1, 0)]


def density_kernel(ahead, nz, more, rows_ref, row_e, col_e, *refs):
    cols_refs, refs = refs[: len(ahead)], refs[len(ahead) :]
    before_ref = refs[0] if more else None
    out_ref, full, sem = refs[-3:]
    z = lax.axis_index("z")
    copies = []
    for cols_ref, parts in zip(cols_refs, ahead):
        _, width, lanes = cols_ref.shape
        for k, (first, step) in enumerate(parts):
            place = pl.multiple_of(lax.rem(z + (step % nz), nz) * lanes, lanes)
            there = full.at[pl.ds(first, width), pl.ds(place, lanes)]
            copies.append(pltpu.make_async_copy(cols_ref.at[k], there, sem.at[len(copies)]))
    for copy in copies:
        copy.start()
    for copy in copies:
        copy.wait()
    pair = lax.dot_general(
        rows_ref[...], full[...], (((1,), (1,)), ((), ())), preferred_element_type=jnp.float32
    )
    amplitude = (spin_scale * pair / (row_e[...] + col_e[...])).astype(jnp.bfloat16)
    term = jnp.dot(amplitude, full[...], preferred_element_type=jnp.float32)
    if more:
        term = term + before_ref[...]
    out_ref[...] = term.astype(out_ref.dtype)


def run(nz, ahead, rows, row_e, col_e, cols, before=None):
    more, width = before is not None, col_e.shape[1]
    vmem = pl.BlockSpec(memory_space=pltpu.VMEM)
    anywhere = pl.BlockSpec(memory_space=pl.ANY)
    work = 4 * rows.size * width
    return pl.pallas_call(
        lambda *refs: density_kernel(ahead, nz, more, *refs),
        out_shape=jax.ShapeDtypeStruct(rows.shape, jnp.bfloat16 if more else jnp.float32),
        in_specs=[vmem] * 3 + [anywhere] * len(cols) + [vmem] * more,
        out_specs=vmem,
        scratch_shapes=[
            pltpu.VMEM((width, rows.shape[1]), jnp.bfloat16),
            pltpu.SemaphoreType.DMA((sum(len(parts) for parts in ahead),)),
        ],
        compiler_params=pltpu.CompilerParams(vmem_limit_bytes=24 * 1024 * 1024),
        cost_estimate=pl.CostEstimate(flops=work, bytes_accessed=work // 256, transcendentals=0),
    )(rows, row_e, col_e, *cols, *([before] if more else []))


def shards(integrals, occ_bins, vir_bins):
    nz, nh, nl, ny = (lax.axis_size(k) for k in ("z", "h", "l", "y"))
    z, h, l, y, c = (lax.axis_index(k) for k in ("z", "h", "l", "y", "c"))
    nj, slab, part = integrals.shape
    depth = nz * nh * part
    width = nj * slab
    own = integrals.astype(jnp.bfloat16)
    packed = jnp.concatenate([own[: nj // 2], own[nj // 2 :]], axis=2)
    there = lax.ppermute(packed, "h", SWAP)
    other = jnp.concatenate([there[:, :, :part], there[:, :, part:]], axis=0)
    first = h == 0
    wide = jnp.concatenate([jnp.where(first, own, other), jnp.where(first, other, own)], axis=2)
    wide = wide.reshape(width, nh * part)
    seeds = lax.all_to_all(own, ("z", "h"), 0, 0)
    seeds = jnp.transpose(seeds, (1, 0, 2)).reshape(slab, depth)
    seeds = jnp.broadcast_to(seeds[None], (nl * ny, slab, depth))

    def shift(block, by):
        return lax.ppermute(block, "z", [(k, (k + by) % nz) for k in range(nz)])

    up, down = shift(wide, 4), shift(wide, -4)
    up, down, seeds = lax.optimization_barrier((up, down, seeds))
    fours = jnp.stack([wide, up, down])
    below, above = shift(fours, 1), shift(fours, -1)
    last_above = shift(above[:, : width // 2], -1)
    last_below = shift(below[:, width // 2 :], 1)
    last = jnp.concatenate([last_above, last_below], axis=0)
    ones = jnp.concatenate([below, above], axis=0)
    here = [fours, below, above, last_above, last_below]
    tops = lambda *steps: [(0, step) for step in steps]
    ends = [(width // 2, step) for step in (-2, -6, 2)]
    of_here = [tops(0, -4, 4), tops(-1, -5, 3), tops(1, -3, 5), tops(2, -2, 6), ends]
    of_there = [of_here[0], of_here[1] + of_here[2], of_here[3] + ends]
    rows = lax.all_to_all(seeds, ("l", "y"), 0, 0).reshape(nl * ny * slab, depth)
    fours_there, ones_there, last_there = (lax.ppermute(k, "c", SWAP) for k in (fours, ones, last))

    occupied = occupied_base - occupied_step * occ_bins.astype(jnp.float32)
    virtual = virtual_base + virtual_step * vir_bins.astype(jnp.float32)
    virtual = virtual.reshape(nl * ny, 2, slab)
    occ_own = lax.dynamic_index_in_dim(occupied, z * nh + h, 0, keepdims=False)
    row_e = (lax.dynamic_index_in_dim(virtual, c, 1, keepdims=False) - occ_own).reshape(-1, 1)
    of_chip = lax.dynamic_index_in_dim(virtual, l * ny + y, 0, keepdims=False)
    col_own = lax.dynamic_index_in_dim(of_chip, c, 0, keepdims=False)
    col_there = lax.dynamic_index_in_dim(of_chip, 1 - c, 0, keepdims=False)
    col_own = (col_own[None, :] - occupied[:, None]).reshape(1, -1)
    col_there = (col_there[None, :] - occupied[:, None]).reshape(1, -1)

    before = run(nz, of_here, rows, row_e, col_own, here)
    there = [fours_there, ones_there, last_there]
    partial_term = run(nz, of_there, rows, row_e, col_there, there, before)
    shares = lax.all_to_all(partial_term.reshape(nl * ny, slab, depth), ("l", "y"), 0, 0)
    density = jnp.sum(shares.astype(jnp.float32), axis=0)
    return density[:, None, :]


def solution(mesh):
    fine = Mesh(mesh.devices.reshape(12, 2, 2, 8, 2), ("z", "h", "l", "y", "c"))
    in_specs = (P(None, ("l", "y", "c"), ("z", "h")), P(), P())
    out_specs = P(("l", "y", "c"), ("z", "h"), None)
    return jax.shard_map(shards, mesh=fine, in_specs=in_specs, out_specs=out_specs, check_vma=False)
```

time: 144 us -> 141 us (0.979)
  blocking collectives: 85.8 us -> 36.8 us
  waiting for transfers between devices: 1.73 us -> 28.1 us
  starting transfers between devices: 42.5 us -> 58.6 us
  other arithmetic: 2.43 us -> 4.08 us
    all_gather x2 -> x0, blocking collectives: 48.7 us -> none  [the longest x1 24.8 us: shards(): cols_early = lax.all_gather(early, 'z', axis=0, tiled=False)]
    ppermute x2 -> x9, waiting for transfers between devices: 0.01 us -> 26.3 us  [the longest x6 26.3 us: shift(): return lax.ppermute(block, 'z', [(k, (k + by) % nz) for k in range(nz)])]
    ppermute x2 -> x9, starting transfers between devices: 13.9 us -> 30.2 us  [the longest x6 19.8 us: shift(): return lax.ppermute(block, 'z', [(k, (k + by) % nz) for k in range(nz)])]
    all_to_all x1, waiting for transfers between devices: 0.01 us -> 1.73 us  [shards(): seeds = lax.all_to_all(own, ('z', 'h'), 0, 0)]
    concatenate x1 -> x2, other arithmetic: 0.08 us -> 1.79 us  [the longest x1 0.99 us: shards(): ones = jnp.concatenate([below, above], axis=0)]
    ppermute x1, waiting for transfers between devices: 1.72 us -> 0.01 us  [shards(): there = lax.ppermute(packed, 'h', SWAP)]
  transfers between devices with their start and end apart: 5 -> 12, of which waited for: 1 -> 7; matrix products, arithmetic and copies ran while one was open for 1% -> 4% of each run, Pallas kernels for 3% -> 2%
where the time goes in v6:
time: 141 us; the launch traced here: 139 us
  starting transfers between devices  58.6 us (42%)
  blocking collectives  36.8 us (26%)
  waiting for transfers between devices  28.1 us (20%)
  Pallas kernels  7.14 us (5%)
  local copies, waits for them, and re-layouts  4.11 us (3%)
  other arithmetic  4.08 us (3%)
    all_to_all x1, blocking collectives, shards(): lax.all_to_all(partial_term.reshape(nl * ny, slab, depth), ('l', 'y'), 0, 0)  36.8 us
    ppermute x6, waiting for transfers between devices, shift(): return lax.ppermute(block, 'z', [(k, (k + by) % nz) for k in range(nz)])  26.3 us
    ppermute x6, starting transfers between devices, shift(): return lax.ppermute(block, 'z', [(k, (k + by) % nz) for k in range(nz)])  19.8 us
    all_to_all x1, starting transfers between devices, shards(): seeds = lax.all_to_all(own, ('z', 'h'), 0, 0)  15.1 us
    ppermute x3, starting transfers between devices, shards(): lax.ppermute(k, 'c', SWAP)  10.5 us
    all_to_all x1, starting transfers between devices, shards(): lax.all_to_all(seeds, ('l', 'y'), 0, 0).reshape(nl * ny * slab, depth)  7.8 us
    pallas_call x2, Pallas kernels, run(): pl.pallas_call(lambda *refs: density_kernel(ahead, nz, more, *refs), out_...  7.14 us
    ppermute x1, starting transfers between devices, shards(): there = lax.ppermute(packed, 'h', SWAP)  5.48 us
  transfers between devices with their start and end apart: 12, of which 7 were waited for; matrix products, arithmetic and copies ran while one was open for 4% of the time, Pallas kernels for 2%

profile of v6, /device:TPU:1, one launch (start us, length us, event | category | flops | bytes accessed | tf_op | source)
XLA Modules:
  0.0 139.2 jit_solution(13644128461001409459)
XLA Ops:
  0.0 1.1 convert_element_type.12
  1.1 0.1 pad_maximum_fusion.5
  1.2 5.5 %collective-permute-start = (bf16[12,24,128]{2,1,0:T(8,128)(2,1)S(1)}, bf16[12,24,128]{2,1,0:T(8,128)(2,1)S(1)}, u32[]{:S(2)}, u32[]{:S(2)}) collective-permute-start(bf16[12,24,128]{2,1,0:T(8,128)(2,1)S(1)} %pad_maximum_fusion.5), channel_id=1, source_target_pairs={{0,32},{32,0},{1,33},{33,1},{2,34},{34,2},{3,35},{35,3},{4,36},{36... | collective-permute-start | bytes 221192 | tf_op jit(solution)/shard_map/ppermute | solution.py:70
  6.7 0.8 reshape.88
  7.4 15.1 %all-to-all-start = ((bf16[24,2,768]{2,1,0:T(2,128)(2,1)}), bf16[24,2,768]{2,1,0:T(2,128)(2,1)S(1)}, u32[]{:S(2)}, u32[]{:S(2)}) async-start(bf16[24,2,768]{2,1,0:T(2,128)(2,1)} %reshape.88), calls=%async_computation | async-start | bytes 147456 | tf_op jit(solution)/shard_map/all_to_all | solution.py:75
  22.6 0.0 collective-permute-done
  22.6 0.1 fusion.3
  22.7 0.1 broadcast_select_fusion.1
  22.7 0.1 pad_maximum_fusion.4
  22.8 7.1 %collective-permute-start.1 = (bf16[576,128]{1,0:T(8,128)(2,1)S(1)}, bf16[576,128]{1,0:T(8,128)(2,1)S(1)}, u32[]{:S(2)}, u32[]{:S(2)}) collective-permute-start(bf16[576,128]{1,0:T(8,128)(2,1)S(1)} %bitcast.15), channel_id=1, source_target_pairs={{0,256},{64,320},{128,384},{192,448},{256,512},{320,576},{384,640}... | collective-permute-start | bytes 442376 | tf_op jit(solution)/shard_map/ppermute | solution.py:80
  30.0 2.1 %collective-permute-start.2 = (bf16[576,128]{1,0:T(8,128)(2,1)S(1)}, bf16[576,128]{1,0:T(8,128)(2,1)S(1)}, u32[]{:S(2)}, u32[]{:S(2)}) collective-permute-start(bf16[576,128]{1,0:T(8,128)(2,1)S(1)} %bitcast.16), channel_id=1, source_target_pairs={{0,512},{64,576},{128,640},{192,704},{256,0},{320,64},{384,128},{4... | collective-permute-start | bytes 442376 | tf_op jit(solution)/shard_map/ppermute | solution.py:80
  32.1 1.7 %all-to-all-done = bf16[24,2,768]{2,1,0:T(2,128)(2,1)S(1)} async-done(((bf16[24,2,768]{2,1,0:T(2,128)(2,1)}), bf16[24,2,768]{2,1,0:T(2,128)(2,1)S(1)}, u32[]{:S(2)}, u32[]{:S(2)}) %all-to-all-start) | async-done | bytes 73760 | tf_op jit(solution)/shard_map/all_to_all | solution.py:75
  33.8 0.1 reshape.89
  34.0 0.2 broadcast_in_dim.6
  34.1 3.2 %collective-permute-done.1 = bf16[576,128]{1,0:T(8,128)(2,1)S(1)} collective-permute-done((bf16[576,128]{1,0:T(8,128)(2,1)S(1)}, bf16[576,128]{1,0:T(8,128)(2,1)S(1)}, u32[]{:S(2)}, u32[]{:S(2)}) %collective-permute-start.1) | collective-permute-done | bytes 147488 | tf_op jit(solution)/shard_map/ppermute | solution.py:80
  37.3 8.9 %collective-permute-done.2 = bf16[576,128]{1,0:T(8,128)(2,1)S(1)} collective-permute-done((bf16[576,128]{1,0:T(8,128)(2,1)S(1)}, bf16[576,128]{1,0:T(8,128)(2,1)S(1)}, u32[]{:S(2)}, u32[]{:S(2)}) %collective-permute-start.2) | collective-permute-done | bytes 147488 | tf_op jit(solution)/shard_map/ppermute | solution.py:80
  46.2 1.1 broadcast_in_dim.7
  47.3 7.8 %all-to-all-start.1 = ((bf16[16,24,1536]{2,1,0:T(8,128)(2,1)}), bf16[16,24,1536]{2,1,0:T(8,128)(2,1)S(1)}, u32[]{:S(2)}, u32[]{:S(2)}) async-start(bf16[16,24,1536]{2,1,0:T(8,128)(2,1)} %broadcast_in_dim.7), calls=%async_computation.1 | async-start | bytes 2359296 | tf_op jit(solution)/shard_map/all_to_all | solution.py:95
  55.1 0.0 copy-start.1
  55.1 0.1 pad_maximum_fusion.1.refs_3_
  55.2 0.0 copy-start.2
  55.2 3.0 %collective-permute-start.5 = (bf16[3,576,128]{2,1,0:T(8,128)(2,1)S(1)}, bf16[3,576,128]{2,1,0:T(8,128)(2,1)S(1)}, u32[]{:S(2)}, u32[]{:S(2)}) collective-permute-start(bf16[3,576,128]{2,1,0:T(8,128)(2,1)S(1)} %pad_maximum_fusion.1.refs_3_), channel_id=1, source_target_pairs={{0,704},{64,0},{128,64},{192,128},{256,192},{320,256},{384,320},{4... | collective-permute-start | bytes 1327112 | tf_op jit(solution)/shard_map/ppermute | solution.py:80
  58.2 2.3 %collective-permute-start.4 = (bf16[3,576,128]{2,1,0:T(8,128)(2,1)S(1)}, bf16[3,576,128]{2,1,0:T(8,128)(2,1)S(1)}, u32[]{:S(2)}, u32[]{:S(2)}) collective-permute-start(bf16[3,576,128]{2,1,0:T(8,128)(2,1)S(1)} %pad_maximum_fusion.1.refs_3_), channel_id=1, source_target_pairs={{0,64},{64,128},{128,192},{192,256},{256,320},{320,384},{384,448},... | collective-permute-start | bytes 1327112 | tf_op jit(solution)/shard_map/ppermute | solution.py:80
  60.5 4.9 %collective-permute-done.5.refs_5_ = bf16[3,576,128]{2,1,0:T(8,128)(2,1)S(1)} collective-permute-done((bf16[3,576,128]{2,1,0:T(8,128)(2,1)S(1)}, bf16[3,576,128]{2,1,0:T(8,128)(2,1)S(1)}, u32[]{:S(2)}, u32[]{:S(2)}) %collective-permute-start.5) | collective-permute-done | bytes 442400 | tf_op jit(solution)/shard_map/ppermute | solution.py:80
  65.4 5.0 %collective-permute-done.4.refs_4_ = bf16[3,576,128]{2,1,0:T(8,128)(2,1)S(1)} collective-permute-done((bf16[3,576,128]{2,1,0:T(8,128)(2,1)S(1)}, bf16[3,576,128]{2,1,0:T(8,128)(2,1)S(1)}, u32[]{:S(2)}, u32[]{:S(2)}) %collective-permute-start.4) | collective-permute-done | bytes 442400 | tf_op jit(solution)/shard_map/ppermute | solution.py:80
  70.5 1.0 pad_maximum_fusion
  71.5 5.3 %collective-permute-start.6 = (bf16[6,576,128]{2,1,0:T(8,128)(2,1)}, bf16[6,576,128]{2,1,0:T(8,128)(2,1)}, u32[]{:S(2)}, u32[]{:S(2)}) collective-permute-start(bf16[6,576,128]{2,1,0:T(8,128)(2,1)} %pad_maximum_fusion), channel_id=1, source_target_pairs={{0,1},{1,0},{2,3},{3,2},{4,5},{5,4},{6,7},{7,6},{8,9},{9,8},{10,11... | collective-permute-start | bytes 2654216 | tf_op jit(solution)/shard_map/ppermute | solution.py:96
  76.8 0.1 reshape.79
  76.9 1.9 %collective-permute-start.7 = (bf16[3,288,128]{2,1,0:T(8,128)(2,1)S(1)}, bf16[3,288,128]{2,1,0:T(8,128)(2,1)S(1)}, u32[]{:S(2)}, u32[]{:S(2)}) collective-permute-start(bf16[3,288,128]{2,1,0:T(8,128)(2,1)S(1)} %slice.28), channel_id=1, source_target_pairs={{0,704},{64,0},{128,64},{192,128},{256,192},{320,256},{384,320},{4... | collective-permute-start | bytes 663560 | tf_op jit(solution)/shard_map/ppermute | solution.py:80
  78.9 3.4 %collective-permute-start.8 = (bf16[3,288,128]{2,1,0:T(8,128)(2,1)S(1)}, bf16[3,288,128]{2,1,0:T(8,128)(2,1)S(1)}, u32[]{:S(2)}, u32[]{:S(2)}) collective-permute-start(bf16[3,288,128]{2,1,0:T(8,128)(2,1)S(1)} %slice.29), channel_id=1, source_target_pairs={{0,64},{64,128},{128,192},{192,256},{256,320},{320,384},{384,448},... | collective-permute-start | bytes 663560 | tf_op jit(solution)/shard_map/ppermute | solution.py:80
  82.3 2.5 %collective-permute-start.3 = (bf16[3,576,128]{2,1,0:T(8,128)(2,1)S(1)}, bf16[3,576,128]{2,1,0:T(8,128)(2,1)}, u32[]{:S(2)}, u32[]{:S(2)}) collective-permute-start(bf16[3,576,128]{2,1,0:T(8,128)(2,1)S(1)} %pad_maximum_fusion.1.refs_3_), channel_id=1, source_target_pairs={{0,1},{1,0},{2,3},{3,2},{4,5},{5,4},{6,7},{7,6},{8,9},{9,8},{10,11... | collective-permute-start | bytes 1327112 | tf_op jit(solution)/shard_map/ppermute | solution.py:96
  84.8 1.1 collective-permute-done.7.refs_6_
  85.9 3.2 %collective-permute-done.8.refs_7_ = bf16[3,288,128]{2,1,0:T(8,128)(2,1)S(1)} collective-permute-done((bf16[3,288,128]{2,1,0:T(8,128)(2,1)S(1)}, bf16[3,288,128]{2,1,0:T(8,128)(2,1)S(1)}, u32[]{:S(2)}, u32[]{:S(2)}) %collective-permute-start.8) | collective-permute-done | bytes 221216 | tf_op jit(solution)/shard_map/ppermute | solution.py:80
  89.1 0.8 pad_maximum_fusion.2
  89.9 2.7 %collective-permute-start.9 = (bf16[6,288,128]{2,1,0:T(8,128)(2,1)}, bf16[6,288,128]{2,1,0:T(8,128)(2,1)}, u32[]{:S(2)}, u32[]{:S(2)}) collective-permute-start(bf16[6,288,128]{2,1,0:T(8,128)(2,1)} %pad_maximum_fusion.2), channel_id=1, source_target_pairs={{0,1},{1,0},{2,3},{3,2},{4,5},{5,4},{6,7},{7,6},{8,9},{9,8},{10,11... | collective-permute-start | bytes 1327112 | tf_op jit(solution)/shard_map/ppermute | solution.py:96
  92.6 0.1 broadcast_subtract_fusion
  92.6 0.1 sub.83.refs_2_
  92.8 0.6 dynamic_slice.18
  93.3 0.7 subtract_reduce_fusion
  94.0 0.1 sub.84.refs_1_
  94.1 0.1 sub.79.refs_2_
  94.2 0.0 all-to-all-done.1
  94.2 3.0 %shard_map.37.refs_6_ = f32[384,1536]{1,0:T(8,128)S(1)} custom-call(bf16[384,1536]{1,0:T(8,128)(2,1)S(1)} %bitcast.12, f32[384,1]{1,0:T(8,128)S(1)} %sub.84.refs_1_, f32[1,576]{1,0:T(1,128)S(1)} %sub.83.refs_2_, bf16[3,576,128]{2,1,0:T(8,128)(2,1)S(1)} %pad_maximum_fusion.1.refs_3_, bf16[3,576,128]{2,1,0:T(8,128)(2,1)S(1)} %collective-permute-done.4.refs_4_, ...), custom_call_target="tpu_custom_call" | custom-call | flops 1358954496 | bytes 5308416 | tf_op jit(solution)/shard_map/pallas_call | solution.py:48
  97.2 0.0 collective-permute-done.3.refs_3_
  97.3 4.2 %shard_map.38 = bf16[384,1536]{1,0:T(8,128)(2,1)S(1)} custom-call(bf16[384,1536]{1,0:T(8,128)(2,1)S(1)} %bitcast.13, f32[384,1]{1,0:T(8,128)S(1)} %sub.84.refs_1_, f32[1,576]{1,0:T(1,128)S(1)} %sub.79.refs_2_, bf16[3,576,128]{2,1,0:T(8,128)(2,1)} %collective-permute-done.3.refs_3_, bf16[6,576,128]{2,1,0:T(8,128)(2,1)} %collective-permute-done.6.refs_4_, ...), custom_call_target="tpu_custom_call" | custom-call | flops 1358954496 | bytes 5308416 | tf_op jit(solution)/shard_map/pallas_call | solution.py:48
  101.4 36.8 %all_to_all.15 = bf16[16,24,1536]{2,1,0:T(8,128)(2,1)S(1)} all-to-all(bf16[16,24,1536]{2,1,0:T(8,128)(2,1)S(1)} %bitcast.14), channel_id=1, replica_groups=mesh['z'=12,'h'=2,'l'=2,'y'=8,'c'=2] {'l','y'}, dimensions={0} | all-to-all | bytes 2359296 | tf_op jit(solution)/shard_map/all_to_all | solution.py:112
  138.3 0.2 convert_reduce_fusion
  138.4 0.8 broadcast_in_dim.16
  (13 shorter events, 0.1 us)
Async XLA Ops:
  0.0 22.7 %copy-start = (f32[24,24,64]{2,1,0:T(8,128)S(1)}, f32[24,24,64]{2,1,0:T(8,128)}, u32[]{:S(2)}) copy-start(f32[24,24,64]{2,1,0:T(8,128)} %param.3) | copy-start | bytes 442372
  1.2 21.4 %collective-permute-start = (bf16[12,24,128]{2,1,0:T(8,128)(2,1)S(1)}, bf16[12,24,128]{2,1,0:T(8,128)(2,1)S(1)}, u32[]{:S(2)}, u32[]{:S(2)}) collective-permute-start(bf16[12,24,128]{2,1,0:T(8,128)(2,1)S(1)} %pad_maximum_fusion.5), channel_id=1, source_target_pairs={{0,32},{32,0},{1,33},{33,1},{2,34},{34,2},{3,35},{35,3},{4,36},{36... | collective-permute-start | bytes 221192 | tf_op jit(solution)/shard_map/ppermute | solution.py:70
  7.4 26.3 %all-to-all-start = ((bf16[24,2,768]{2,1,0:T(2,128)(2,1)}), bf16[24,2,768]{2,1,0:T(2,128)(2,1)S(1)}, u32[]{:S(2)}, u32[]{:S(2)}) async-start(bf16[24,2,768]{2,1,0:T(2,128)(2,1)} %reshape.88), calls=%async_computation | async-start | bytes 147456 | tf_op jit(solution)/shard_map/all_to_all | solution.py:75
  22.8 14.5 %collective-permute-start.1 = (bf16[576,128]{1,0:T(8,128)(2,1)S(1)}, bf16[576,128]{1,0:T(8,128)(2,1)S(1)}, u32[]{:S(2)}, u32[]{:S(2)}) collective-permute-start(bf16[576,128]{1,0:T(8,128)(2,1)S(1)} %bitcast.15), channel_id=1, source_target_pairs={{0,256},{64,320},{128,384},{192,448},{256,512},{320,576},{384,640}... | collective-permute-start | bytes 442376 | tf_op jit(solution)/shard_map/ppermute | solution.py:80
  30.0 16.3 %collective-permute-start.2 = (bf16[576,128]{1,0:T(8,128)(2,1)S(1)}, bf16[576,128]{1,0:T(8,128)(2,1)S(1)}, u32[]{:S(2)}, u32[]{:S(2)}) collective-permute-start(bf16[576,128]{1,0:T(8,128)(2,1)S(1)} %bitcast.16), channel_id=1, source_target_pairs={{0,512},{64,576},{128,640},{192,704},{256,0},{320,64},{384,128},{4... | collective-permute-start | bytes 442376 | tf_op jit(solution)/shard_map/ppermute | solution.py:80
  47.3 46.9 %all-to-all-start.1 = ((bf16[16,24,1536]{2,1,0:T(8,128)(2,1)}), bf16[16,24,1536]{2,1,0:T(8,128)(2,1)S(1)}, u32[]{:S(2)}, u32[]{:S(2)}) async-start(bf16[16,24,1536]{2,1,0:T(8,128)(2,1)} %broadcast_in_dim.7), calls=%async_computation.1 | async-start | bytes 2359296 | tf_op jit(solution)/shard_map/all_to_all | solution.py:95
  55.1 21.7 %copy-start.1 = (s32[768]{0:T(1024)S(1)}, s32[768]{0:T(1024)}, u32[]{:S(2)}) copy-start(s32[768]{0:T(1024)} %param.5) | copy-start | bytes 9220
  55.2 27.1 %copy-start.2 = (s32[24]{0:T(128)S(1)}, s32[24]{0:T(128)}, u32[]{:S(2)}) copy-start(s32[24]{0:T(128)} %param.4) | copy-start | bytes 292
  55.2 10.2 %collective-permute-start.5 = (bf16[3,576,128]{2,1,0:T(8,128)(2,1)S(1)}, bf16[3,576,128]{2,1,0:T(8,128)(2,1)S(1)}, u32[]{:S(2)}, u32[]{:S(2)}) collective-permute-start(bf16[3,576,128]{2,1,0:T(8,128)(2,1)S(1)} %pad_maximum_fusion.1.refs_3_), channel_id=1, source_target_pairs={{0,704},{64,0},{128,64},{192,128},{256,192},{320,256},{384,320},{4... | collective-permute-start | bytes 1327112 | tf_op jit(solution)/shard_map/ppermute | solution.py:80
  58.2 12.3 %collective-permute-start.4 = (bf16[3,576,128]{2,1,0:T(8,128)(2,1)S(1)}, bf16[3,576,128]{2,1,0:T(8,128)(2,1)S(1)}, u32[]{:S(2)}, u32[]{:S(2)}) collective-permute-start(bf16[3,576,128]{2,1,0:T(8,128)(2,1)S(1)} %pad_maximum_fusion.1.refs_3_), channel_id=1, source_target_pairs={{0,64},{64,128},{128,192},{192,256},{256,320},{320,384},{384,448},... | collective-permute-start | bytes 1327112 | tf_op jit(solution)/shard_map/ppermute | solution.py:80
  71.5 25.8 %collective-permute-start.6 = (bf16[6,576,128]{2,1,0:T(8,128)(2,1)}, bf16[6,576,128]{2,1,0:T(8,128)(2,1)}, u32[]{:S(2)}, u32[]{:S(2)}) collective-permute-start(bf16[6,576,128]{2,1,0:T(8,128)(2,1)} %pad_maximum_fusion), channel_id=1, source_target_pairs={{0,1},{1,0},{2,3},{3,2},{4,5},{5,4},{6,7},{7,6},{8,9},{9,8},{10,11... | collective-permute-start | bytes 2654216 | tf_op jit(solution)/shard_map/ppermute | solution.py:96
  76.9 8.9 %collective-permute-start.7 = (bf16[3,288,128]{2,1,0:T(8,128)(2,1)S(1)}, bf16[3,288,128]{2,1,0:T(8,128)(2,1)S(1)}, u32[]{:S(2)}, u32[]{:S(2)}) collective-permute-start(bf16[3,288,128]{2,1,0:T(8,128)(2,1)S(1)} %slice.28), channel_id=1, source_target_pairs={{0,704},{64,0},{128,64},{192,128},{256,192},{320,256},{384,320},{4... | collective-permute-start | bytes 663560 | tf_op jit(solution)/shard_map/ppermute | solution.py:80
  78.9 10.2 %collective-permute-start.8 = (bf16[3,288,128]{2,1,0:T(8,128)(2,1)S(1)}, bf16[3,288,128]{2,1,0:T(8,128)(2,1)S(1)}, u32[]{:S(2)}, u32[]{:S(2)}) collective-permute-start(bf16[3,288,128]{2,1,0:T(8,128)(2,1)S(1)} %slice.29), channel_id=1, source_target_pairs={{0,64},{64,128},{128,192},{192,256},{256,320},{320,384},{384,448},... | collective-permute-start | bytes 663560 | tf_op jit(solution)/shard_map/ppermute | solution.py:80
  82.3 14.9 %collective-permute-start.3 = (bf16[3,576,128]{2,1,0:T(8,128)(2,1)S(1)}, bf16[3,576,128]{2,1,0:T(8,128)(2,1)}, u32[]{:S(2)}, u32[]{:S(2)}) collective-permute-start(bf16[3,576,128]{2,1,0:T(8,128)(2,1)S(1)} %pad_maximum_fusion.1.refs_3_), channel_id=1, source_target_pairs={{0,1},{1,0},{2,3},{3,2},{4,5},{5,4},{6,7},{7,6},{8,9},{9,8},{10,11... | collective-permute-start | bytes 1327112 | tf_op jit(solution)/shard_map/ppermute | solution.py:96
  89.9 7.4 %collective-permute-start.9 = (bf16[6,288,128]{2,1,0:T(8,128)(2,1)}, bf16[6,288,128]{2,1,0:T(8,128)(2,1)}, u32[]{:S(2)}, u32[]{:S(2)}) collective-permute-start(bf16[6,288,128]{2,1,0:T(8,128)(2,1)} %pad_maximum_fusion.2), channel_id=1, source_target_pairs={{0,1},{1,0},{2,3},{3,2},{4,5},{5,4},{6,7},{7,6},{8,9},{9,8},{10,11... | collective-permute-start | bytes 1327112 | tf_op jit(solution)/shard_map/ppermute | solution.py:96

commit v7 on v4

v7 whole, which is shorter than its diff:
```python
import jax
import jax.numpy as jnp
from jax import lax
from jax.experimental import pallas as pl
from jax.experimental.pallas import tpu as pltpu
from jax.sharding import Mesh, PartitionSpec as P

occupied_base = -0.4
occupied_step = 0.01
virtual_base = 0.1
virtual_step = 0.01
spin_scale = 1.3

SWAP = [(0, 1), (1, 0)]


def density_kernel(blocks, kinds, more, there_ref, there_e, own_ref, own_e, col_e, *refs):
    cols_refs, refs = refs[:blocks], refs[blocks:]
    befores, refs = (refs[:2], refs[2:]) if more else ((None, None), refs)
    outs, (full, sem) = refs[:2], refs[2:]
    copies, first, left = [], 0, 0
    for cols_ref in cols_refs:
        chunks, width, lanes = cols_ref.shape
        for k in range(chunks):
            there = full.at[pl.ds(first, width), pl.ds(left, lanes)]
            copies.append(pltpu.make_async_copy(cols_ref.at[k], there, sem.at[len(copies)]))
            left += lanes
        if left == full.shape[1]:
            first, left = first + width, 0
    for copy in copies:
        copy.start()
    for copy in copies:
        copy.wait()
    sides = ((there_ref, there_e, befores[0], outs[0]), (own_ref, own_e, befores[1], outs[1]))
    for rows_ref, row_e, before_ref, out_ref in sides:
        pair = lax.dot_general(
            rows_ref[...], full[...], (((1,), (1,)), ((), ())), preferred_element_type=jnp.float32
        )
        amplitude = (spin_scale * pair / (row_e[...] + col_e[...])).astype(jnp.bfloat16)
        term = jnp.dot(amplitude, full[...], preferred_element_type=jnp.float32)
        if more:
            term = term + before_ref[...]
        out_ref[...] = term.astype(out_ref.dtype)


def run(kinds, there, there_e, own, own_e, col_e, cols, befores=()):
    vmem = pl.BlockSpec(memory_space=pltpu.VMEM)
    anywhere = pl.BlockSpec(memory_space=pl.ANY)
    width = col_e.shape[1]
    work = 8 * own.size * width
    return pl.pallas_call(
        lambda *refs: density_kernel(len(cols), kinds, len(befores) > 0, *refs),
        out_shape=[jax.ShapeDtypeStruct(own.shape, kind) for kind in kinds],
        in_specs=[vmem] * 5 + [anywhere] * len(cols) + [vmem] * len(befores),
        out_specs=[vmem, vmem],
        scratch_shapes=[
            pltpu.VMEM((width, own.shape[1]), jnp.bfloat16),
            pltpu.SemaphoreType.DMA((sum(block.shape[0] for block in cols),)),
        ],
        compiler_params=pltpu.CompilerParams(vmem_limit_bytes=24 * 1024 * 1024),
        cost_estimate=pl.CostEstimate(flops=work, bytes_accessed=work // 256, transcendentals=0),
    )(there, there_e, own, own_e, col_e, *cols, *befores)


def shards(integrals, occ_bins, vir_bins):
    nz, nh, nl, ny = (lax.axis_size(k) for k in ("z", "h", "l", "y"))
    z, h, l, y, c = (lax.axis_index(k) for k in ("z", "h", "l", "y", "c"))
    nj, slab, part = integrals.shape
    depth = nz * nh * part
    own = integrals.astype(jnp.bfloat16).reshape(nz, nh, slab, part)
    even, odd = own[:, 0], own[:, 1]
    first = h == 0
    mine = jnp.where(first, even, odd)
    there = lax.ppermute(jnp.where(first, odd, even), "h", SWAP)
    wide = jnp.concatenate([jnp.where(first, mine, there), jnp.where(first, there, mine)], axis=2)
    seeds = lax.all_to_all(wide, "z", 0, 0)
    here = lax.all_gather(wide.reshape(nz * slab, nh * part), "z", axis=0, tiled=False)
    here, seeds = lax.optimization_barrier((here, seeds))

    def shift(block, by):
        ring = [(k, (k + by) % (nh * nl)) for k in range(nh * nl)]
        return lax.ppermute(block, ("h", "l"), ring)

    left, right = shift(here, 1), shift(here, -1)
    far_low, far_high = shift(left[: nz // 2], 1), shift(right[nz // 2 :], -1)
    seeds = jnp.transpose(seeds, (1, 0, 2)).reshape(slab, depth)
    rows = lax.all_to_all(jnp.broadcast_to(seeds[None], (ny, slab, depth)), "y", 0, 0)
    rows = rows.reshape(ny * slab, depth)
    rows_there = lax.ppermute(rows, "c", SWAP)

    occupied = occupied_base - occupied_step * occ_bins.astype(jnp.float32)
    virtual = virtual_base + virtual_step * vir_bins.astype(jnp.float32)
    virtual = virtual.reshape(nl, ny, 2, slab)
    occ_own = lax.dynamic_slice_in_dim(occupied, z * nh + h, 1, 0)
    core0, low0 = c == 0, l == 0
    of_rows = jnp.where(low0, virtual[0], virtual[1]) - occ_own
    own_e = jnp.where(core0, of_rows[:, 0], of_rows[:, 1]).reshape(-1, 1)
    there_e = jnp.where(core0, of_rows[:, 1], of_rows[:, 0]).reshape(-1, 1)
    of_cols = lax.dynamic_slice_in_dim(virtual, y, 1, 1)[:, 0]
    of_cols = jnp.where(core0, of_cols[:, 0], of_cols[:, 1])
    low_own = jnp.where(low0, of_cols[0], of_cols[1])
    low_other = jnp.where(low0, of_cols[1], of_cols[0])
    evens, odds = occupied[0::2], occupied[1::2]

    def col_e(low, is_even):
        return (low[None, :] - jnp.where(is_even, evens, odds)[:, None]).reshape(1, -1)

    most_e = [col_e(low_own, h == 0), col_e(low_other, h != l), col_e(low_other, h == l)]
    rest_e = col_e(low_own, h != 0)
    f32, bf16 = jnp.float32, jnp.bfloat16
    rows_e = (rows_there, there_e, rows, own_e)
    most = run((f32, f32), *rows_e, jnp.concatenate(most_e, axis=1), [here, left, right])
    for_there, for_own = run((bf16, f32), *rows_e, rest_e, [far_low, far_high], most)
    arrived = lax.ppermute(for_there, "c", SWAP)
    pair_sum = (for_own + arrived.astype(jnp.float32)).astype(jnp.bfloat16)
    shares = lax.all_to_all(pair_sum.reshape(ny, slab, depth), "y", 0, 0)
    density = jnp.sum(shares.astype(jnp.float32), axis=0)
    return density[:, None, :]


def solution(mesh):
    fine = Mesh(mesh.devices.reshape(12, 2, 2, 8, 2), ("z", "h", "l", "y", "c"))
    in_specs = (P(None, ("l", "y", "c"), ("z", "h")), P(), P())
    out_specs = P(("l", "y", "c"), ("z", "h"), None)
    return jax.shard_map(shards, mesh=fine, in_specs=in_specs, out_specs=out_specs, check_vma=False)
```

time: 144 us -> 133 us (0.924)
  blocking collectives: 85.8 us -> 49.1 us
  starting transfers between devices: 42.5 us -> 55.3 us
  waiting for transfers between devices: 1.73 us -> 9.61 us
  local copies, waits for them, and re-layouts: 3.83 us -> 7.89 us
    all_gather x2 -> x1, blocking collectives: 48.7 us -> 24.5 us  [shards(): lax.all_gather(wide.reshape(nz * slab, nh * part), 'z', axis=0, tiled=False)]
    ppermute x3 -> x7, starting transfers between devices: 19.4 us -> 33.4 us  [the longest x4 12.9 us: shift(): return lax.ppermute(block, ('h', 'l'), ring)]
    all_to_all x1, blocking collectives: 37.1 us -> 24.6 us  [shards(): shares = lax.all_to_all(pair_sum.reshape(ny, slab, depth), 'y', 0, 0)]
    all_to_all x2, waiting for transfers between devices: 0.01 us -> 5.45 us  [the longest x1 5.45 us: shards(): lax.all_to_all(jnp.broadcast_to(seeds[None], (ny, slab, depth)), 'y', 0, 0)]
    slice x3 -> x4, local copies, waits for them, and re-layouts: 0.18 us -> 2.84 us  [the longest x2 2.65 us: shards(): far_low, far_high = (shift(left[:nz // 2], 1), shift(right[nz // 2:], -1))]
    ppermute x3 -> x7, waiting for transfers between devices: 1.72 us -> 4.16 us  [the longest x1 1.73 us: shards(): there = lax.ppermute(jnp.where(first, odd, even), 'h', SWAP)]
    unnamed x6 -> x8, local copies, waits for them, and re-layouts: 0.01 us -> 2.13 us
  transfers between devices with their start and end apart: 5 -> 9, of which waited for: 1 -> 4; matrix products, arithmetic and copies ran while one was open for 1% -> 4% of each run, Pallas kernels for 3% -> 4%
where the time goes in v7:
time: 133 us; the launch traced here: 132 us
  starting transfers between devices  55.3 us (42%)
  blocking collectives  49.1 us (37%)
  waiting for transfers between devices  9.61 us (7%)
  local copies, waits for them, and re-layouts  7.89 us (6%)
  Pallas kernels  7.14 us (5%)
  other arithmetic  2.83 us (2%)
    all_to_all x1, blocking collectives, shards(): shares = lax.all_to_all(pair_sum.reshape(ny, slab, depth), 'y', 0, 0)  24.6 us
    all_gather x1, blocking collectives, shards(): lax.all_gather(wide.reshape(nz * slab, nh * part), 'z', axis=0, tiled=False)  24.5 us
    all_to_all x1, starting transfers between devices, shards(): seeds = lax.all_to_all(wide, 'z', 0, 0)  15.1 us
    ppermute x4, starting transfers between devices, shift(): return lax.ppermute(block, ('h', 'l'), ring)  12.9 us
    ppermute x1, starting transfers between devices, shards(): rows_there = lax.ppermute(rows, 'c', SWAP)  10.2 us
    pallas_call x2, Pallas kernels, run(): pl.pallas_call(lambda *refs: density_kernel(len(cols), kinds, len(befores...  7.14 us
    all_to_all x1, starting transfers between devices, shards(): lax.all_to_all(jnp.broadcast_to(seeds[None], (ny, slab, depth)), 'y', 0, 0)  6.82 us
    ppermute x1, starting transfers between devices, shards(): there = lax.ppermute(jnp.where(first, odd, even), 'h', SWAP)  5.48 us
  transfers between devices with their start and end apart: 9, of which 4 were waited for; matrix products, arithmetic and copies ran while one was open for 4% of the time, Pallas kernels for 4%

profile of v7, /device:TPU:1, one launch (start us, length us, event | category | flops | bytes accessed | tf_op | source)
XLA Modules:
  0.0 132.2 jit_solution(10168925860507239386)
XLA Ops:
  0.0 1.0 convert_element_type.18
  1.0 5.5 %collective-permute-start = (bf16[12,24,64]{2,1,0:T(8,128)(2,1)S(1)}, bf16[12,24,64]{2,1,0:T(8,128)(2,1)S(1)}, u32[]{:S(2)}, u32[]{:S(2)}) collective-permute-start(bf16[12,24,64]{2,1,0:T(8,128)(2,1)S(1)} %fusion), channel_id=1, source_target_pairs={{0,32},{32,0},{1,33},{33,1},{2,34},{34,2},{3,35},{35,3},{4,36},{36... | collective-permute-start | bytes 110600 | tf_op jit(solution)/shard_map/ppermute | solution.py:74
  6.5 1.7 %collective-permute-done = bf16[12,24,64]{2,1,0:T(8,128)(2,1)S(1)} collective-permute-done((bf16[12,24,64]{2,1,0:T(8,128)(2,1)S(1)}, bf16[12,24,64]{2,1,0:T(8,128)(2,1)S(1)}, u32[]{:S(2)}, u32[]{:S(2)}) %collective-permute-start) | collective-permute-done | bytes 36896 | tf_op jit(solution)/shard_map/ppermute | solution.py:74
  8.2 0.7 pad_maximum_fusion
  9.0 15.1 %all-to-all-start = ((bf16[12,24,128]{2,1,0:T(8,128)(2,1)}), bf16[12,24,128]{2,1,0:T(8,128)(2,1)S(1)}, u32[]{:S(2)}, u32[]{:S(2)}) async-start(bf16[12,24,128]{2,1,0:T(8,128)(2,1)} %pad_maximum_fusion), calls=%async_computation | async-start | bytes 147456 | tf_op jit(solution)/shard_map/all_to_all | solution.py:76
  24.1 24.5 %all_gather.3.refs_5_ = bf16[12,288,128]{2,1,0:T(8,128)(2,1)S(1)} all-gather(bf16[1,288,128]{2,1,0:T(8,128)(2,1)} %bitcast.6), channel_id=1, replica_groups=mesh['z'=12,'h'=2,'l'=2,'y'=8,'c'=2] {'z'}, dimensions={0}, use_global_device_ids=true | all-gather | bytes 958464 | tf_op jit(solution)/shard_map/all_gather | solution.py:77
  48.6 0.0 all-to-all-done
  48.6 0.9 broadcast_in_dim.7
  49.5 6.8 %all-to-all-start.1 = ((bf16[8,24,1536]{2,1,0:T(8,128)(2,1)}), bf16[8,24,1536]{2,1,0:T(8,128)(2,1)S(1)}, u32[]{:S(2)}, u32[]{:S(2)}) async-start(bf16[8,24,1536]{2,1,0:T(8,128)(2,1)} %broadcast_in_dim.7), calls=%async_computation.1 | async-start | bytes 1179648 | tf_op jit(solution)/shard_map/all_to_all | solution.py:87
  56.3 0.0 copy-done.3
  56.4 0.1 slice.76
  56.5 0.1 slice.77
  56.6 0.0 copy-done.2
  56.6 0.1 reshape.190
  56.7 0.6 dynamic_slice.6
  57.3 3.1 %collective-permute-start.2 = (bf16[12,288,128]{2,1,0:T(8,128)(2,1)S(1)}, bf16[12,288,128]{2,1,0:T(8,128)(2,1)S(1)}, u32[]{:S(2)}, u32[]{:S(2)}) collective-permute-start(bf16[12,288,128]{2,1,0:T(8,128)(2,1)S(1)} %all_gather.3.refs_5_), channel_id=1, source_target_pairs={{0,16},{16,32},{32,48},{48,0},{1,17},{17,33},{33,49},{49,1},{2,18}... | collective-permute-start | bytes 2654216 | tf_op jit(solution)/shard_map/ppermute | solution.py:82
  60.4 3.4 %collective-permute-start.4 = (bf16[12,288,128]{2,1,0:T(8,128)(2,1)S(1)}, bf16[12,288,128]{2,1,0:T(8,128)(2,1)}, u32[]{:S(2)}, u32[]{:S(2)}) collective-permute-start(bf16[12,288,128]{2,1,0:T(8,128)(2,1)S(1)} %all_gather.3.refs_5_), channel_id=1, source_target_pairs={{0,48},{16,0},{32,16},{48,32},{1,49},{17,1},{33,17},{49,33},{2,50}... | collective-permute-start | bytes 2654216 | tf_op jit(solution)/shard_map/ppermute | solution.py:82
  63.8 5.4 %all-to-all-done.1 = bf16[8,24,1536]{2,1,0:T(8,128)(2,1)S(1)} async-done(((bf16[8,24,1536]{2,1,0:T(8,128)(2,1)}), bf16[8,24,1536]{2,1,0:T(8,128)(2,1)S(1)}, u32[]{:S(2)}, u32[]{:S(2)}) %all-to-all-start.1) | async-done | bytes 589856 | tf_op jit(solution)/shard_map/all_to_all | solution.py:87
  69.3 10.2 %collective-permute-start.1 = (bf16[192,1536]{1,0:T(8,128)(2,1)S(1)}, bf16[192,1536]{1,0:T(8,128)(2,1)S(1)}, u32[]{:S(2)}, u32[]{:S(2)}) collective-permute-start(bf16[192,1536]{1,0:T(8,128)(2,1)S(1)} %bitcast.45), channel_id=1, source_target_pairs={{0,1},{1,0},{2,3},{3,2},{4,5},{5,4},{6,7},{7,6},{8,9},{9,8},{10,11... | collective-permute-start | bytes 1769480 | tf_op jit(solution)/shard_map/ppermute | solution.py:89
  79.5 0.1 broadcast_subtract_fusion.1
  79.6 0.0 collective-permute-done.2.refs_6_
  79.6 0.8 slice.88
  80.4 1.0 copy-done
  81.4 3.1 %collective-permute-start.3 = (bf16[6,288,128]{2,1,0:T(8,128)(2,1)}, bf16[6,288,128]{2,1,0:T(8,128)(2,1)S(1)}, u32[]{:S(2)}, u32[]{:S(2)}) collective-permute-start(bf16[6,288,128]{2,1,0:T(8,128)(2,1)} %slice.88), channel_id=1, source_target_pairs={{0,16},{16,32},{32,48},{48,0},{1,17},{17,33},{33,49},{49,1},{2,18}... | collective-permute-start | bytes 1327112 | tf_op jit(solution)/shard_map/ppermute | solution.py:82
  84.5 0.0 collective-permute-done.4.refs_7_
  84.5 1.8 %slice.89 = bf16[6,288,128]{2,1,0:T(8,128)(2,1)} slice(bf16[12,288,128]{2,1,0:T(8,128)(2,1)} %collective-permute-done.4.refs_7_), slice={[6:12], [0:288], [0:128]} | slice | bytes 884736 | tf_op jit(solution)/shard_map/slice | solution.py:85
  86.3 3.4 %collective-permute-start.5 = (bf16[6,288,128]{2,1,0:T(8,128)(2,1)}, bf16[6,288,128]{2,1,0:T(8,128)(2,1)S(1)}, u32[]{:S(2)}, u32[]{:S(2)}) collective-permute-start(bf16[6,288,128]{2,1,0:T(8,128)(2,1)} %slice.89), channel_id=1, source_target_pairs={{0,48},{16,0},{32,16},{48,32},{1,49},{17,1},{33,17},{49,33},{2,50}... | collective-permute-start | bytes 1327112 | tf_op jit(solution)/shard_map/ppermute | solution.py:82
  89.7 0.7 select_subtract_fusion
  90.4 0.1 sub.120
  90.4 0.1 sub.125
  90.5 0.1 sub.128
  90.6 0.1 sub.112
  90.7 0.1 select_n.156.refs_1_
  90.8 0.1 select_n.157.refs_3_
  90.9 0.1 sub.117.refs_4_
  91.0 0.1 pad_maximum_fusion.1.refs_4_
  91.1 0.0 collective-permute-done.1.refs_0_
  91.1 1.2 copy-done.1
  92.3 5.0 %shard_map.37 = (f32[192,1536]{1,0:T(8,128)S(1)}, f32[192,1536]{1,0:T(8,128)S(1)}) custom-call(bf16[192,1536]{1,0:T(8,128)(2,1)S(1)} %collective-permute-done.1.refs_0_, f32[192,1]{1,0:T(8,128)S(1)} %select_n.156.refs_1_, bf16[192,1536]{1,0:T(8,128)(2,1)S(1)} %bitcast.46, f32[192,1]{1,0:T(8,128)S(1)} %select_n.157.refs_3_, ...), custom_call_target="tpu_custom_call" | custom-call | flops 2038431744 | bytes 7962624 | tf_op jit(solution)/shard_map/pallas_call | solution.py:51
  97.3 0.0 collective-permute-done.3.refs_5_
  97.3 0.8 collective-permute-done.5.refs_6_
  98.2 2.1 %shard_map.38 = (bf16[192,1536]{1,0:T(8,128)(2,1)S(1)}, f32[192,1536]{1,0:T(8,128)S(1)}) custom-call(bf16[192,1536]{1,0:T(8,128)(2,1)S(1)} %collective-permute-done.1.refs_0_, f32[192,1]{1,0:T(8,128)S(1)} %select_n.156.refs_1_, bf16[192,1536]{1,0:T(8,128)(2,1)S(1)} %bitcast.47, f32[192,1]{1,0:T(8,128)S(1)} %select_n.157.refs_3_, f32[1,288]{1,0:T(1,128)S(1)} %sub.117.refs_4_, ...), custom_call_target="tpu_custom_call" | custom-call | flops 679477248 | bytes 2654208 | tf_op jit(solution)/shard_map/pallas_call | solution.py:51
  100.3 4.8 %collective-permute-start.6 = (bf16[192,1536]{1,0:T(8,128)(2,1)S(1)}, bf16[192,1536]{1,0:T(8,128)(2,1)S(1)}, u32[]{:S(2)}, u32[]{:S(2)}) collective-permute-start(bf16[192,1536]{1,0:T(8,128)(2,1)S(1)} %get-tuple-element.16), channel_id=1, source_target_pairs={{0,1},{1,0},{2,3},{3,2},{4,5},{5,4},{6,7},{7,6},{8,9},{9,8},{10,11... | collective-permute-start | bytes 1769480 | tf_op jit(solution)/shard_map/ppermute | solution.py:114
  105.0 1.6 %collective-permute-done.6 = bf16[192,1536]{1,0:T(8,128)(2,1)S(1)} collective-permute-done((bf16[192,1536]{1,0:T(8,128)(2,1)S(1)}, bf16[192,1536]{1,0:T(8,128)(2,1)S(1)}, u32[]{:S(2)}, u32[]{:S(2)}) %collective-permute-start.6) | collective-permute-done | bytes 589856 | tf_op jit(solution)/shard_map/ppermute | solution.py:114
  106.6 0.1 add_convert_fusion
  106.8 24.6 %all_to_all.15 = bf16[8,24,1536]{2,1,0:T(8,128)(2,1)S(1)} all-to-all(bf16[8,24,1536]{2,1,0:T(8,128)(2,1)S(1)} %bitcast.48), channel_id=1, replica_groups=mesh['z'=12,'h'=2,'l'=2,'y'=8,'c'=2] {'y'}, dimensions={0} | all-to-all | bytes 1179648 | tf_op jit(solution)/shard_map/all_to_all | solution.py:116
  131.4 0.1 convert_reduce_fusion
  131.5 0.8 broadcast_in_dim.8
  (14 shorter events, 0.1 us)
Async XLA Ops:
  1.0 7.2 %collective-permute-start = (bf16[12,24,64]{2,1,0:T(8,128)(2,1)S(1)}, bf16[12,24,64]{2,1,0:T(8,128)(2,1)S(1)}, u32[]{:S(2)}, u32[]{:S(2)}) collective-permute-start(bf16[12,24,64]{2,1,0:T(8,128)(2,1)S(1)} %fusion), channel_id=1, source_target_pairs={{0,32},{32,0},{1,33},{33,1},{2,34},{34,2},{3,35},{35,3},{4,36},{36... | collective-permute-start | bytes 110600 | tf_op jit(solution)/shard_map/ppermute | solution.py:74
  9.0 39.6 %all-to-all-start = ((bf16[12,24,128]{2,1,0:T(8,128)(2,1)}), bf16[12,24,128]{2,1,0:T(8,128)(2,1)S(1)}, u32[]{:S(2)}, u32[]{:S(2)}) async-start(bf16[12,24,128]{2,1,0:T(8,128)(2,1)} %pad_maximum_fusion), calls=%async_computation | async-start | bytes 147456 | tf_op jit(solution)/shard_map/all_to_all | solution.py:76
  48.6 7.7 %copy-start.3 = (s32[24]{0:T(128)S(1)}, s32[24]{0:T(128)}, u32[]{:S(2)}) copy-start(s32[24]{0:T(128)} %param.4) | copy-start | bytes 292
  48.6 8.0 %copy-start.2 = (s32[768]{0:T(1024)S(1)}, s32[768]{0:T(1024)}, u32[]{:S(2)}) copy-start(s32[768]{0:T(1024)} %param.5) | copy-start | bytes 9220
  49.5 19.8 %all-to-all-start.1 = ((bf16[8,24,1536]{2,1,0:T(8,128)(2,1)}), bf16[8,24,1536]{2,1,0:T(8,128)(2,1)S(1)}, u32[]{:S(2)}, u32[]{:S(2)}) async-start(bf16[8,24,1536]{2,1,0:T(8,128)(2,1)} %broadcast_in_dim.7), calls=%async_computation.1 | async-start | bytes 1179648 | tf_op jit(solution)/shard_map/all_to_all | solution.py:87
  57.3 22.3 %collective-permute-start.2 = (bf16[12,288,128]{2,1,0:T(8,128)(2,1)S(1)}, bf16[12,288,128]{2,1,0:T(8,128)(2,1)S(1)}, u32[]{:S(2)}, u32[]{:S(2)}) collective-permute-start(bf16[12,288,128]{2,1,0:T(8,128)(2,1)S(1)} %all_gather.3.refs_5_), channel_id=1, source_target_pairs={{0,16},{16,32},{32,48},{48,0},{1,17},{17,33},{33,49},{49,1},{2,18}... | collective-permute-start | bytes 2654216 | tf_op jit(solution)/shard_map/ppermute | solution.py:82
  60.4 24.1 %collective-permute-start.4 = (bf16[12,288,128]{2,1,0:T(8,128)(2,1)S(1)}, bf16[12,288,128]{2,1,0:T(8,128)(2,1)}, u32[]{:S(2)}, u32[]{:S(2)}) collective-permute-start(bf16[12,288,128]{2,1,0:T(8,128)(2,1)S(1)} %all_gather.3.refs_5_), channel_id=1, source_target_pairs={{0,48},{16,0},{32,16},{48,32},{1,49},{17,1},{33,17},{49,33},{2,50}... | collective-permute-start | bytes 2654216 | tf_op jit(solution)/shard_map/ppermute | solution.py:82
  69.3 21.8 %collective-permute-start.1 = (bf16[192,1536]{1,0:T(8,128)(2,1)S(1)}, bf16[192,1536]{1,0:T(8,128)(2,1)S(1)}, u32[]{:S(2)}, u32[]{:S(2)}) collective-permute-start(bf16[192,1536]{1,0:T(8,128)(2,1)S(1)} %bitcast.45), channel_id=1, source_target_pairs={{0,1},{1,0},{2,3},{3,2},{4,5},{5,4},{6,7},{7,6},{8,9},{9,8},{10,11... | collective-permute-start | bytes 1769480 | tf_op jit(solution)/shard_map/ppermute | solution.py:89
  80.4 1.0 copy-start
  81.4 16.0 %collective-permute-start.3 = (bf16[6,288,128]{2,1,0:T(8,128)(2,1)}, bf16[6,288,128]{2,1,0:T(8,128)(2,1)S(1)}, u32[]{:S(2)}, u32[]{:S(2)}) collective-permute-start(bf16[6,288,128]{2,1,0:T(8,128)(2,1)} %slice.88), channel_id=1, source_target_pairs={{0,16},{16,32},{32,48},{48,0},{1,17},{17,33},{33,49},{49,1},{2,18}... | collective-permute-start | bytes 1327112 | tf_op jit(solution)/shard_map/ppermute | solution.py:82
  86.3 11.8 %collective-permute-start.5 = (bf16[6,288,128]{2,1,0:T(8,128)(2,1)}, bf16[6,288,128]{2,1,0:T(8,128)(2,1)S(1)}, u32[]{:S(2)}, u32[]{:S(2)}) collective-permute-start(bf16[6,288,128]{2,1,0:T(8,128)(2,1)} %slice.89), channel_id=1, source_target_pairs={{0,48},{16,0},{32,16},{48,32},{1,49},{17,1},{33,17},{49,33},{2,50}... | collective-permute-start | bytes 1327112 | tf_op jit(solution)/shard_map/ppermute | solution.py:82
  91.1 1.2 copy-start.1
  100.3 6.4 %collective-permute-start.6 = (bf16[192,1536]{1,0:T(8,128)(2,1)S(1)}, bf16[192,1536]{1,0:T(8,128)(2,1)S(1)}, u32[]{:S(2)}, u32[]{:S(2)}) collective-permute-start(bf16[192,1536]{1,0:T(8,128)(2,1)S(1)} %get-tuple-element.16), channel_id=1, source_target_pairs={{0,1},{1,0},{2,3},{3,2},{4,5},{5,4},{6,7},{7,6},{8,9},{9,8},{10,11... | collective-permute-start | bytes 1769480 | tf_op jit(solution)/shard_map/ppermute | solution.py:114

commit v8 on v7

v8 whole, which is shorter than its diff:
```python
import jax
import jax.numpy as jnp
from jax import lax
from jax.experimental import pallas as pl
from jax.experimental.pallas import tpu as pltpu
from jax.sharding import Mesh, PartitionSpec as P

occupied_base = -0.4
occupied_step = 0.01
virtual_base = 0.1
virtual_step = 0.01
spin_scale = 1.3

SWAP = [(0, 1), (1, 0)]


def density_kernel(halves, more, there_ref, there_e, own_ref, own_e, col_e, *refs):
    blocks, refs = refs[: len(halves)], refs[len(halves) :]
    befores, refs = (refs[:2], refs[2:]) if more else ((None, None), refs)
    outs, (full, sem) = refs[:2], refs[2:]
    h, l = lax.axis_index("h"), lax.axis_index("l")
    mixed = lax.rem(h + l, 2)
    parity = {"own": h, "far": 1 - h, "right": mixed, "left": 1 - mixed}
    copies = []
    for block, (side, first) in zip(blocks, halves):
        chunks, part, _ = block.shape
        for k in range(chunks):
            start = (first + k) * 2 * part + parity[side] * part
            place = full.at[pl.ds(pl.multiple_of(start, part), part)]
            copies.append(pltpu.make_async_copy(block.at[k], place, sem.at[len(copies)]))
    for copy in copies:
        copy.start()
    for copy in copies:
        copy.wait()
    sides = ((there_ref, there_e, befores[0], outs[0]), (own_ref, own_e, befores[1], outs[1]))
    for rows_ref, row_e, before_ref, out_ref in sides:
        pair = jnp.dot(rows_ref[...], full[...], preferred_element_type=jnp.float32)
        amplitude = (spin_scale * pair / (row_e[...] + col_e[...])).astype(jnp.bfloat16)
        term = lax.dot_general(
            amplitude, full[...], (((1,), (1,)), ((), ())), preferred_element_type=jnp.float32
        )
        if more:
            term = term + before_ref[...]
        out_ref[...] = term.astype(out_ref.dtype)


def run(kinds, there, there_e, own, own_e, col_e, halves, blocks, befores=()):
    vmem = pl.BlockSpec(memory_space=pltpu.VMEM)
    anywhere = pl.BlockSpec(memory_space=pl.ANY)
    width = col_e.shape[1]
    work = 8 * own.size * width
    return pl.pallas_call(
        lambda *refs: density_kernel(halves, len(befores) > 0, *refs),
        out_shape=[jax.ShapeDtypeStruct(own.shape, kind) for kind in kinds],
        in_specs=[vmem] * 5 + [anywhere] * len(blocks) + [vmem] * len(befores),
        out_specs=[vmem, vmem],
        scratch_shapes=[
            pltpu.VMEM((own.shape[1], width), jnp.bfloat16),
            pltpu.SemaphoreType.DMA((sum(block.shape[0] for block in blocks),)),
        ],
        compiler_params=pltpu.CompilerParams(vmem_limit_bytes=16 * 1024 * 1024),
        cost_estimate=pl.CostEstimate(flops=work, bytes_accessed=work // 256, transcendentals=0),
    )(there, there_e, own, own_e, col_e, *blocks, *befores)


def shards(integrals, occ_bins, vir_bins):
    nz, nh, nl, ny = (lax.axis_size(k) for k in ("z", "h", "l", "y"))
    z, h, l, y, c = (lax.axis_index(k) for k in ("z", "h", "l", "y", "c"))
    nj, slab, part = integrals.shape
    depth = nz * nh * part
    first, core0, low0 = h == 0, c == 0, l == 0
    rounded = integrals.astype(jnp.bfloat16)
    seeds = lax.all_to_all(rounded, ("z", "h"), 0, 0)
    own = jnp.transpose(rounded.reshape(nj * slab, part))
    here = lax.all_gather(own, "z", axis=0, tiled=False)
    here, seeds = lax.optimization_barrier((here, seeds))
    seeds = jnp.transpose(seeds, (1, 0, 2)).reshape(slab, depth)

    def shift(block, by):
        ring = [(k, (k + by) % (nh * nl)) for k in range(nh * nl)]
        return lax.ppermute(block, ("h", "l"), ring)

    mid = nz // 2
    low, high = here[:mid], here[mid:]
    left_low, right_high = shift(low, 1), shift(high, -1)
    left_high, right_low = shift(high, 1), shift(low, -1)
    far_low, far_high = shift(left_low, 1), shift(right_high, -1)
    rows = lax.all_to_all(jnp.broadcast_to(seeds[None], (ny, slab, depth)), "y", 0, 0)
    rows = rows.reshape(ny * slab, depth)
    rows_there = lax.ppermute(rows, "c", SWAP)

    occupied = occupied_base - occupied_step * occ_bins.astype(jnp.float32)
    virtual = virtual_base + virtual_step * vir_bins.astype(jnp.float32)
    virtual = virtual.reshape(nl, ny, 2, slab)
    occ_own = lax.dynamic_slice_in_dim(occupied, z * nh + h, 1, 0)
    of_rows = jnp.where(low0, virtual[0], virtual[1]) - occ_own
    own_e = jnp.where(core0, of_rows[:, 0], of_rows[:, 1]).reshape(-1, 1)
    there_e = jnp.where(core0, of_rows[:, 1], of_rows[:, 0]).reshape(-1, 1)
    of_cols = lax.dynamic_slice_in_dim(virtual, y, 1, 1)[:, 0]
    of_cols = jnp.where(core0, of_cols[:, 0], of_cols[:, 1])
    of_cols = (of_cols[:, None, :] - occupied[None, :, None]).reshape(nl, 1, nj * slab)
    col_own = jnp.where(low0, of_cols[0], of_cols[1])
    col_other = jnp.where(low0, of_cols[1], of_cols[0])

    f32, bf16 = jnp.float32, jnp.bfloat16
    rows_e = (rows_there, there_e, rows, own_e)
    sides = [("left", 0), ("right", mid), ("left", mid), ("right", 0)]
    blocks = [left_low, right_high, left_high, right_low]
    other = run((f32, f32), *rows_e, col_other, sides, blocks)
    sides = [("own", 0), ("far", 0), ("far", mid)]
    blocks = [here, far_low, far_high]
    for_there, for_own = run((bf16, f32), *rows_e, col_own, sides, blocks, other)
    arrived = lax.ppermute(for_there, "c", SWAP)
    pair_sum = (for_own + arrived.astype(jnp.float32)).astype(jnp.bfloat16)
    shares = lax.all_to_all(pair_sum.reshape(ny, slab, depth), "y", 0, 0)
    density = jnp.sum(shares.astype(jnp.float32), axis=0)
    return density[:, None, :]


def solution(mesh):
    fine = Mesh(mesh.devices.reshape(12, 2, 2, 8, 2), ("z", "h", "l", "y", "c"))
    in_specs = (P(None, ("l", "y", "c"), ("z", "h")), P(), P())
    out_specs = P(("l", "y", "c"), ("z", "h"), None)
    return jax.shard_map(shards, mesh=fine, in_specs=in_specs, out_specs=out_specs, check_vma=False)
```

time: 133 us -> 137 us (1.030)
  waiting for transfers between devices: 9.61 us -> 16.7 us
  blocking collectives: 49.1 us -> 46.2 us
  local copies, waits for them, and re-layouts: 7.89 us -> 5.1 us
  Pallas kernels: 7.14 us -> 9.44 us
    ppermute x4 -> x6, waiting for transfers between devices: 0.83 us -> 9.93 us  [shift(): return lax.ppermute(block, ('h', 'l'), ring)]
    ppermute x4 -> x6, starting transfers between devices: 12.9 us -> 19.5 us  [shift(): return lax.ppermute(block, ('h', 'l'), ring)]
    ppermute x1 -> x0, starting transfers between devices: 5.48 us -> none  [shards(): there = lax.ppermute(jnp.where(first, odd, even), 'h', SWAP)]
    all_to_all x1, starting transfers between devices: 15.1 us -> 18.4 us  [shards(): seeds = lax.all_to_all(rounded, ('z', 'h'), 0, 0)]
    all_to_all x1, blocking collectives: 24.6 us -> 21.8 us  [shards(): shares = lax.all_to_all(pair_sum.reshape(ny, slab, depth), 'y', 0, 0)]
    pallas_call x2, Pallas kernels: 7.14 us -> 9.44 us  [run(): pl.pallas_call(lambda *refs: density_kernel(halves, len(befores) > 0, *re...]
    ppermute x1, starting transfers between devices: 4.75 us -> 2.71 us  [shards(): arrived = lax.ppermute(for_there, 'c', SWAP)]
    slice x4 -> x1, local copies, waits for them, and re-layouts: 2.84 us -> 1.09 us  [shards(): low, high = (here[:mid], here[mid:])]
  transfers between devices with their start and end apart: 9 -> 10, of which waited for: 4 -> 6; matrix products, arithmetic and copies ran while one was open for 4% -> 2% of each run, Pallas kernels for 4% -> 3%
where the time goes in v8:
time: 137 us; the launch traced here: 136 us
  starting transfers between devices  56.6 us (41%)
  blocking collectives  46.2 us (34%)
  waiting for transfers between devices  16.7 us (12%)
  Pallas kernels  9.44 us (7%)
  local copies, waits for them, and re-layouts  5.1 us (4%)
  other arithmetic  1.98 us (1%)
    all_gather x1, blocking collectives, shards(): here = lax.all_gather(own, 'z', axis=0, tiled=False)  24.5 us
    all_to_all x1, blocking collectives, shards(): shares = lax.all_to_all(pair_sum.reshape(ny, slab, depth), 'y', 0, 0)  21.8 us
    ppermute x6, starting transfers between devices, shift(): return lax.ppermute(block, ('h', 'l'), ring)  19.5 us
    all_to_all x1, starting transfers between devices, shards(): seeds = lax.all_to_all(rounded, ('z', 'h'), 0, 0)  18.4 us
    ppermute x6, waiting for transfers between devices, shift(): return lax.ppermute(block, ('h', 'l'), ring)  9.93 us
    pallas_call x2, Pallas kernels, run(): pl.pallas_call(lambda *refs: density_kernel(halves, len(befores) > 0, *re...  9.44 us
    ppermute x1, starting transfers between devices, shards(): rows_there = lax.ppermute(rows, 'c', SWAP)  9.19 us
    all_to_all x1, starting transfers between devices, shards(): lax.all_to_all(jnp.broadcast_to(seeds[None], (ny, slab, depth)), 'y', 0, 0)  6.82 us
  transfers between devices with their start and end apart: 10, of which 6 were waited for; matrix products, arithmetic and copies ran while one was open for 2% of the time, Pallas kernels for 3%

profile of v8, /device:TPU:1, one launch (start us, length us, event | category | flops | bytes accessed | tf_op | source)
XLA Modules:
  0.0 136.3 jit_solution(18304115117681025568)
XLA Ops:
  0.0 1.0 convert_element_type.18
  1.0 0.8 reshape.145
  1.8 18.4 %all-to-all-start = ((bf16[24,2,768]{2,1,0:T(2,128)(2,1)}), bf16[24,2,768]{2,1,0:T(2,128)(2,1)S(1)}, u32[]{:S(2)}, u32[]{:S(2)}) async-start(bf16[24,2,768]{2,1,0:T(2,128)(2,1)} %reshape.145), calls=%async_computation | async-start | bytes 147456 | tf_op jit(solution)/shard_map/all_to_all | solution.py:73
  20.2 0.1 copy.5
  20.3 24.5 %all-gather = bf16[768,576]{1,0:T(8,128)(2,1)S(1)} all-gather(bf16[64,576]{1,0:T(8,128)(2,1)S(1)} %bitcast.18), channel_id=2, replica_groups=mesh['z'=12,'h'=2,'l'=2,'y'=8,'c'=2] {'z'}, dimensions={0}, use_global_device_ids=true | all-gather | bytes 958464 | tf_op jit(solution)/shard_map/all_gather | solution.py:75
  44.8 0.0 all-to-all-done
  44.8 0.2 reshape.146
  44.9 0.0 copy-start
  45.0 0.0 copy-start.1
  45.0 0.2 broadcast_in_dim.6
  45.2 0.9 broadcast_in_dim.14
  46.0 6.8 %all-to-all-start.1 = ((bf16[8,24,1536]{2,1,0:T(8,128)(2,1)}), bf16[8,24,1536]{2,1,0:T(8,128)(2,1)S(1)}, u32[]{:S(2)}, u32[]{:S(2)}) async-start(bf16[8,24,1536]{2,1,0:T(8,128)(2,1)} %broadcast_in_dim.14), calls=%async_computation.1 | async-start | bytes 1179648 | tf_op jit(solution)/shard_map/all_to_all | solution.py:88
  52.8 0.0 copy-done
  52.9 0.1 reshape.130
  53.0 0.0 copy-done.1
  53.0 1.1 fusion.2
  54.1 2.2 %collective-permute-start.1 = (bf16[6,64,576]{2,1,0:T(8,128)(2,1)}, bf16[6,64,576]{2,1,0:T(8,128)(2,1)}, u32[]{:S(2)}, u32[]{:S(2)}) collective-permute-start(bf16[6,64,576]{2,1,0:T(8,128)(2,1)} %get-tuple-element.20), channel_id=1, source_target_pairs={{0,16},{16,32},{32,48},{48,0},{1,17},{17,33},{33,49},{49,1},{2,18}... | collective-permute-start | bytes 1327112 | tf_op jit(solution)/shard_map/ppermute | solution.py:81
  56.3 4.3 %collective-permute-start.3 = (bf16[6,64,576]{2,1,0:T(8,128)(2,1)}, bf16[6,64,576]{2,1,0:T(8,128)(2,1)}, u32[]{:S(2)}, u32[]{:S(2)}) collective-permute-start(bf16[6,64,576]{2,1,0:T(8,128)(2,1)} %get-tuple-element.19), channel_id=1, source_target_pairs={{0,48},{16,0},{32,16},{48,32},{1,49},{17,1},{33,17},{49,33},{2,50}... | collective-permute-start | bytes 1327112 | tf_op jit(solution)/shard_map/ppermute | solution.py:81
  60.6 5.2 %all-to-all-done.1 = bf16[8,24,1536]{2,1,0:T(8,128)(2,1)S(1)} async-done(((bf16[8,24,1536]{2,1,0:T(8,128)(2,1)}), bf16[8,24,1536]{2,1,0:T(8,128)(2,1)S(1)}, u32[]{:S(2)}, u32[]{:S(2)}) %all-to-all-start.1) | async-done | bytes 589856 | tf_op jit(solution)/shard_map/all_to_all | solution.py:88
  65.8 9.2 %collective-permute-start = (bf16[192,1536]{1,0:T(8,128)(2,1)S(1)}, bf16[192,1536]{1,0:T(8,128)(2,1)S(1)}, u32[]{:S(2)}, u32[]{:S(2)}) collective-permute-start(bf16[192,1536]{1,0:T(8,128)(2,1)S(1)} %bitcast.12), channel_id=1, source_target_pairs={{0,1},{1,0},{2,3},{3,2},{4,5},{5,4},{6,7},{7,6},{8,9},{9,8},{10,11... | collective-permute-start | bytes 1769480 | tf_op jit(solution)/shard_map/ppermute | solution.py:90
  74.9 0.1 broadcast_subtract_fusion
  75.0 0.6 dynamic_slice.6
  75.6 2.2 %collective-permute-start.5 = (bf16[6,64,576]{2,1,0:T(8,128)(2,1)}, bf16[6,64,576]{2,1,0:T(8,128)(2,1)}, u32[]{:S(2)}, u32[]{:S(2)}) collective-permute-start(bf16[6,64,576]{2,1,0:T(8,128)(2,1)} %get-tuple-element.19), channel_id=1, source_target_pairs={{0,16},{16,32},{32,48},{48,0},{1,17},{17,33},{33,49},{49,1},{2,18}... | collective-permute-start | bytes 1327112 | tf_op jit(solution)/shard_map/ppermute | solution.py:81
  77.8 4.3 %collective-permute-start.6 = (bf16[6,64,576]{2,1,0:T(8,128)(2,1)}, bf16[6,64,576]{2,1,0:T(8,128)(2,1)}, u32[]{:S(2)}, u32[]{:S(2)}) collective-permute-start(bf16[6,64,576]{2,1,0:T(8,128)(2,1)} %get-tuple-element.20), channel_id=1, source_target_pairs={{0,48},{16,0},{32,16},{48,32},{1,49},{17,1},{33,17},{49,33},{2,50}... | collective-permute-start | bytes 1327112 | tf_op jit(solution)/shard_map/ppermute | solution.py:81
  82.1 0.7 select_subtract_fusion
  82.8 0.1 sub.35
  82.9 0.0 collective-permute-done.1.refs_5_
  82.9 1.9 %collective-permute-start.2 = (bf16[6,64,576]{2,1,0:T(8,128)(2,1)}, bf16[6,64,576]{2,1,0:T(8,128)(2,1)S(1)}, u32[]{:S(2)}, u32[]{:S(2)}) collective-permute-start(bf16[6,64,576]{2,1,0:T(8,128)(2,1)} %collective-permute-done.1.refs_5_), channel_id=1, source_target_pairs={{0,16},{16,32},{32,48},{48,0},{1,17},{17,33},{33,49},{49,1},{2,18}... | collective-permute-start | bytes 1327112 | tf_op jit(solution)/shard_map/ppermute | solution.py:81
  84.8 0.0 collective-permute-done.3.refs_6_
  84.8 4.6 %collective-permute-start.4 = (bf16[6,64,576]{2,1,0:T(8,128)(2,1)}, bf16[6,64,576]{2,1,0:T(8,128)(2,1)S(1)}, u32[]{:S(2)}, u32[]{:S(2)}) collective-permute-start(bf16[6,64,576]{2,1,0:T(8,128)(2,1)} %collective-permute-done.3.refs_6_), channel_id=1, source_target_pairs={{0,48},{16,0},{32,16},{48,32},{1,49},{17,1},{33,17},{49,33},{2,50}... | collective-permute-start | bytes 1327112 | tf_op jit(solution)/shard_map/ppermute | solution.py:81
  89.4 0.1 select_n.88.refs_1_
  89.5 0.1 select_n.89.refs_3_
  89.6 0.1 select_n.87.refs_4_
  89.7 0.1 select_n.85.refs_4_
  89.8 2.0 %collective-permute-done.5.refs_7_ = bf16[6,64,576]{2,1,0:T(8,128)(2,1)} collective-permute-done((bf16[6,64,576]{2,1,0:T(8,128)(2,1)}, bf16[6,64,576]{2,1,0:T(8,128)(2,1)}, u32[]{:S(2)}, u32[]{:S(2)}) %collective-permute-start.5) | collective-permute-done | bytes 442400 | tf_op jit(solution)/shard_map/ppermute | solution.py:81
  91.9 1.7 %collective-permute-done.6.refs_8_ = bf16[6,64,576]{2,1,0:T(8,128)(2,1)} collective-permute-done((bf16[6,64,576]{2,1,0:T(8,128)(2,1)}, bf16[6,64,576]{2,1,0:T(8,128)(2,1)}, u32[]{:S(2)}, u32[]{:S(2)}) %collective-permute-start.6) | collective-permute-done | bytes 442400 | tf_op jit(solution)/shard_map/ppermute | solution.py:81
  93.5 0.0 collective-permute-done.refs_0_
  93.5 4.2 %shard_map.37 = (f32[192,1536]{1,0:T(8,128)S(1)}, f32[192,1536]{1,0:T(8,128)S(1)}) custom-call(bf16[192,1536]{1,0:T(8,128)(2,1)S(1)} %collective-permute-done.refs_0_, f32[192,1]{1,0:T(8,128)S(1)} %select_n.88.refs_1_, bf16[192,1536]{1,0:T(8,128)(2,1)S(1)} %bitcast.13, f32[192,1]{1,0:T(8,128)S(1)} %select_n.89.refs_3_, f32[1,576]{1,0:T(1,128)S(1)} %select_n.87.refs_4_, ...), custom_call_target="tpu_custom_call" | custom-call | flops 1358954496 | bytes 5308416 | tf_op jit(solution)/shard_map/pallas_call | solution.py:52
  97.7 4.6 %collective-permute-done.2.refs_6_ = bf16[6,64,576]{2,1,0:T(8,128)(2,1)S(1)} collective-permute-done((bf16[6,64,576]{2,1,0:T(8,128)(2,1)}, bf16[6,64,576]{2,1,0:T(8,128)(2,1)S(1)}, u32[]{:S(2)}, u32[]{:S(2)}) %collective-permute-start.2) | collective-permute-done | bytes 442400 | tf_op jit(solution)/shard_map/ppermute | solution.py:81
  102.3 1.7 %collective-permute-done.4.refs_7_ = bf16[6,64,576]{2,1,0:T(8,128)(2,1)S(1)} collective-permute-done((bf16[6,64,576]{2,1,0:T(8,128)(2,1)}, bf16[6,64,576]{2,1,0:T(8,128)(2,1)S(1)}, u32[]{:S(2)}, u32[]{:S(2)}) %collective-permute-start.4) | collective-permute-done | bytes 442400 | tf_op jit(solution)/shard_map/ppermute | solution.py:81
  104.0 5.2 %shard_map.38 = (bf16[192,1536]{1,0:T(8,128)(2,1)S(1)}, f32[192,1536]{1,0:T(8,128)S(1)}) custom-call(bf16[192,1536]{1,0:T(8,128)(2,1)S(1)} %collective-permute-done.refs_0_, f32[192,1]{1,0:T(8,128)S(1)} %select_n.88.refs_1_, bf16[192,1536]{1,0:T(8,128)(2,1)S(1)} %bitcast.14, f32[192,1]{1,0:T(8,128)S(1)} %select_n.89.refs_3_, f32[1,576]{1,0:T(1,128)S(1)} %select_n.85.refs_4_, ...), custom_call_target="tpu_custom_call" | custom-call | flops 1358954496 | bytes 5308416 | tf_op jit(solution)/shard_map/pallas_call | solution.py:52
  109.2 2.7 %collective-permute-start.7 = (bf16[192,1536]{1,0:T(8,128)(2,1)S(1)}, bf16[192,1536]{1,0:T(8,128)(2,1)S(1)}, u32[]{:S(2)}, u32[]{:S(2)}) collective-permute-start(bf16[192,1536]{1,0:T(8,128)(2,1)S(1)} %get-tuple-element.16), channel_id=1, source_target_pairs={{0,1},{1,0},{2,3},{3,2},{4,5},{5,4},{6,7},{7,6},{8,9},{9,8},{10,11... | collective-permute-start | bytes 1769480 | tf_op jit(solution)/shard_map/ppermute | solution.py:113
  111.9 1.6 %collective-permute-done.7 = bf16[192,1536]{1,0:T(8,128)(2,1)S(1)} collective-permute-done((bf16[192,1536]{1,0:T(8,128)(2,1)S(1)}, bf16[192,1536]{1,0:T(8,128)(2,1)S(1)}, u32[]{:S(2)}, u32[]{:S(2)}) %collective-permute-start.7) | collective-permute-done | bytes 589856 | tf_op jit(solution)/shard_map/ppermute | solution.py:113
  113.5 0.1 add_convert_fusion
  113.7 21.8 %all_to_all.15 = bf16[8,24,1536]{2,1,0:T(8,128)(2,1)S(1)} all-to-all(bf16[8,24,1536]{2,1,0:T(8,128)(2,1)S(1)} %bitcast.15), channel_id=1, replica_groups=mesh['z'=12,'h'=2,'l'=2,'y'=8,'c'=2] {'y'}, dimensions={0} | all-to-all | bytes 1179648 | tf_op jit(solution)/shard_map/all_to_all | solution.py:115
  135.4 0.1 convert_reduce_fusion
  135.5 0.8 broadcast_in_dim.15
  (7 shorter events, 0.1 us)
Async XLA Ops:
  1.8 43.0 %all-to-all-start = ((bf16[24,2,768]{2,1,0:T(2,128)(2,1)}), bf16[24,2,768]{2,1,0:T(2,128)(2,1)S(1)}, u32[]{:S(2)}, u32[]{:S(2)}) async-start(bf16[24,2,768]{2,1,0:T(2,128)(2,1)} %reshape.145), calls=%async_computation | async-start | bytes 147456 | tf_op jit(solution)/shard_map/all_to_all | solution.py:73
  44.9 7.9 %copy-start = (s32[768]{0:T(1024)S(1)}, s32[768]{0:T(1024)}, u32[]{:S(2)}) copy-start(s32[768]{0:T(1024)} %param.5) | copy-start | bytes 9220
  45.0 8.0 %copy-start.1 = (s32[24]{0:T(128)S(1)}, s32[24]{0:T(128)}, u32[]{:S(2)}) copy-start(s32[24]{0:T(128)} %param.4) | copy-start | bytes 292
  46.0 19.7 %all-to-all-start.1 = ((bf16[8,24,1536]{2,1,0:T(8,128)(2,1)}), bf16[8,24,1536]{2,1,0:T(8,128)(2,1)S(1)}, u32[]{:S(2)}, u32[]{:S(2)}) async-start(bf16[8,24,1536]{2,1,0:T(8,128)(2,1)} %broadcast_in_dim.14), calls=%async_computation.1 | async-start | bytes 1179648 | tf_op jit(solution)/shard_map/all_to_all | solution.py:88
  54.1 28.8 %collective-permute-start.1 = (bf16[6,64,576]{2,1,0:T(8,128)(2,1)}, bf16[6,64,576]{2,1,0:T(8,128)(2,1)}, u32[]{:S(2)}, u32[]{:S(2)}) collective-permute-start(bf16[6,64,576]{2,1,0:T(8,128)(2,1)} %get-tuple-element.20), channel_id=1, source_target_pairs={{0,16},{16,32},{32,48},{48,0},{1,17},{17,33},{33,49},{49,1},{2,18}... | collective-permute-start | bytes 1327112 | tf_op jit(solution)/shard_map/ppermute | solution.py:81
  56.3 28.5 %collective-permute-start.3 = (bf16[6,64,576]{2,1,0:T(8,128)(2,1)}, bf16[6,64,576]{2,1,0:T(8,128)(2,1)}, u32[]{:S(2)}, u32[]{:S(2)}) collective-permute-start(bf16[6,64,576]{2,1,0:T(8,128)(2,1)} %get-tuple-element.19), channel_id=1, source_target_pairs={{0,48},{16,0},{32,16},{48,32},{1,49},{17,1},{33,17},{49,33},{2,50}... | collective-permute-start | bytes 1327112 | tf_op jit(solution)/shard_map/ppermute | solution.py:81
  65.8 27.8 %collective-permute-start = (bf16[192,1536]{1,0:T(8,128)(2,1)S(1)}, bf16[192,1536]{1,0:T(8,128)(2,1)S(1)}, u32[]{:S(2)}, u32[]{:S(2)}) collective-permute-start(bf16[192,1536]{1,0:T(8,128)(2,1)S(1)} %bitcast.12), channel_id=1, source_target_pairs={{0,1},{1,0},{2,3},{3,2},{4,5},{5,4},{6,7},{7,6},{8,9},{9,8},{10,11... | collective-permute-start | bytes 1769480 | tf_op jit(solution)/shard_map/ppermute | solution.py:90
  75.6 16.3 %collective-permute-start.5 = (bf16[6,64,576]{2,1,0:T(8,128)(2,1)}, bf16[6,64,576]{2,1,0:T(8,128)(2,1)}, u32[]{:S(2)}, u32[]{:S(2)}) collective-permute-start(bf16[6,64,576]{2,1,0:T(8,128)(2,1)} %get-tuple-element.19), channel_id=1, source_target_pairs={{0,16},{16,32},{32,48},{48,0},{1,17},{17,33},{33,49},{49,1},{2,18}... | collective-permute-start | bytes 1327112 | tf_op jit(solution)/shard_map/ppermute | solution.py:81
  77.8 15.7 %collective-permute-start.6 = (bf16[6,64,576]{2,1,0:T(8,128)(2,1)}, bf16[6,64,576]{2,1,0:T(8,128)(2,1)}, u32[]{:S(2)}, u32[]{:S(2)}) collective-permute-start(bf16[6,64,576]{2,1,0:T(8,128)(2,1)} %get-tuple-element.20), channel_id=1, source_target_pairs={{0,48},{16,0},{32,16},{48,32},{1,49},{17,1},{33,17},{49,33},{2,50}... | collective-permute-start | bytes 1327112 | tf_op jit(solution)/shard_map/ppermute | solution.py:81
  82.9 19.4 %collective-permute-start.2 = (bf16[6,64,576]{2,1,0:T(8,128)(2,1)}, bf16[6,64,576]{2,1,0:T(8,128)(2,1)S(1)}, u32[]{:S(2)}, u32[]{:S(2)}) collective-permute-start(bf16[6,64,576]{2,1,0:T(8,128)(2,1)} %collective-permute-done.1.refs_5_), channel_id=1, source_target_pairs={{0,16},{16,32},{32,48},{48,0},{1,17},{17,33},{33,49},{49,1},{2,18}... | collective-permute-start | bytes 1327112 | tf_op jit(solution)/shard_map/ppermute | solution.py:81
  84.8 19.1 %collective-permute-start.4 = (bf16[6,64,576]{2,1,0:T(8,128)(2,1)}, bf16[6,64,576]{2,1,0:T(8,128)(2,1)S(1)}, u32[]{:S(2)}, u32[]{:S(2)}) collective-permute-start(bf16[6,64,576]{2,1,0:T(8,128)(2,1)} %collective-permute-done.3.refs_6_), channel_id=1, source_target_pairs={{0,48},{16,0},{32,16},{48,32},{1,49},{17,1},{33,17},{49,33},{2,50}... | collective-permute-start | bytes 1327112 | tf_op jit(solution)/shard_map/ppermute | solution.py:81
  109.2 4.3 %collective-permute-start.7 = (bf16[192,1536]{1,0:T(8,128)(2,1)S(1)}, bf16[192,1536]{1,0:T(8,128)(2,1)S(1)}, u32[]{:S(2)}, u32[]{:S(2)}) collective-permute-start(bf16[192,1536]{1,0:T(8,128)(2,1)S(1)} %get-tuple-element.16), channel_id=1, source_target_pairs={{0,1},{1,0},{2,3},{3,2},{4,5},{5,4},{6,7},{7,6},{8,9},{9,8},{10,11... | collective-permute-start | bytes 1769480 | tf_op jit(solution)/shard_map/ppermute | solution.py:113

commit v9 on v7

--- a/solution.py
+++ b/solution.py
@@ -31,13 +31,15 @@
         copy.start()
     for copy in copies:
         copy.wait()
-    sides = ((there_ref, there_e, befores[0], outs[0]), (own_ref, own_e, befores[1], outs[1]))
-    for rows_ref, row_e, before_ref, out_ref in sides:
-        pair = lax.dot_general(
-            rows_ref[...], full[...], (((1,), (1,)), ((), ())), preferred_element_type=jnp.float32
-        )
-        amplitude = (spin_scale * pair / (row_e[...] + col_e[...])).astype(jnp.bfloat16)
-        term = jnp.dot(amplitude, full[...], preferred_element_type=jnp.float32)
+    rows = jnp.concatenate([there_ref[...], own_ref[...]], axis=0)
+    row_e = jnp.concatenate([there_e[...], own_e[...]], axis=0)
+    pair = lax.dot_general(
+        rows, full[...], (((1,), (1,)), ((), ())), preferred_element_type=jnp.float32
+    )
+    amplitude = (spin_scale * pair / (row_e + col_e[...])).astype(jnp.bfloat16)
+    terms = jnp.dot(amplitude, full[...], preferred_element_type=jnp.float32)
+    count = own_ref.shape[0]
+    for term, before_ref, out_ref in zip((terms[:count], terms[count:]), befores, outs):
         if more:
             term = term + before_ref[...]
         out_ref[...] = term.astype(out_ref.dtype)
@@ -57,7 +59,7 @@
             pltpu.VMEM((width, own.shape[1]), jnp.bfloat16),
             pltpu.SemaphoreType.DMA((sum(block.shape[0] for block in cols),)),
         ],
-        compiler_params=pltpu.CompilerParams(vmem_limit_bytes=24 * 1024 * 1024),
+        compiler_params=pltpu.CompilerParams(vmem_limit_bytes=14 * 1024 * 1024),
         cost_estimate=pl.CostEstimate(flops=work, bytes_accessed=work // 256, transcendentals=0),
     )(there, there_e, own, own_e, col_e, *cols, *befores)
 
@@ -73,21 +75,6 @@
     mine = jnp.where(first, even, odd)
     there = lax.ppermute(jnp.where(first, odd, even), "h", SWAP)
     wide = jnp.concatenate([jnp.where(first, mine, there), jnp.where(first, there, mine)], axis=2)
-    seeds = lax.all_to_all(wide, "z", 0, 0)
-    here = lax.all_gather(wide.reshape(nz * slab, nh * part), "z", axis=0, tiled=False)
-    here, seeds = lax.optimization_barrier((here, seeds))
-
-    def shift(block, by):
-        ring = [(k, (k + by) % (nh * nl)) for k in range(nh * nl)]
-        return lax.ppermute(block, ("h", "l"), ring)
-
-    left, right = shift(here, 1), shift(here, -1)
-    far_low, far_high = shift(left[: nz // 2], 1), shift(right[nz // 2 :], -1)
-    seeds = jnp.transpose(seeds, (1, 0, 2)).reshape(slab, depth)
-    rows = lax.all_to_all(jnp.broadcast_to(seeds[None], (ny, slab, depth)), "y", 0, 0)
-    rows = rows.reshape(ny * slab, depth)
-    rows_there = lax.ppermute(rows, "c", SWAP)
-
     occupied = occupied_base - occupied_step * occ_bins.astype(jnp.float32)
     virtual = virtual_base + virtual_step * vir_bins.astype(jnp.float32)
     virtual = virtual.reshape(nl, ny, 2, slab)
@@ -107,9 +94,26 @@
 
     most_e = [col_e(low_own, h == 0), col_e(low_other, h != l), col_e(low_other, h == l)]
     rest_e = col_e(low_own, h != 0)
+    wide, own_e, there_e, most_e, rest_e = lax.optimization_barrier(
+        (wide, own_e, there_e, jnp.concatenate(most_e, axis=1), rest_e)
+    )
+    here = lax.all_gather(wide.reshape(nz * slab, nh * part), "z", axis=0, tiled=False)
+
+    def shift(block, by):
+        ring = [(k, (k + by) % (nh * nl)) for k in range(nh * nl)]
+        return lax.ppermute(block, ("h", "l"), ring)
+
+    left, right = shift(here, 1), shift(here, -1)
+    far_low, far_high = shift(left[: nz // 2], 1), shift(right[nz // 2 :], -1)
+    seeds = lax.dynamic_slice_in_dim(here, z * slab, slab, 1)
+    seeds = jnp.transpose(seeds, (1, 0, 2)).reshape(slab, depth)
+    rows = lax.all_to_all(jnp.broadcast_to(seeds[None], (ny, slab, depth)), "y", 0, 0)
+    rows = rows.reshape(ny * slab, depth)
+    rows_there = lax.ppermute(rows, "c", SWAP)
+
     f32, bf16 = jnp.float32, jnp.bfloat16
     rows_e = (rows_there, there_e, rows, own_e)
-    most = run((f32, f32), *rows_e, jnp.concatenate(most_e, axis=1), [here, left, right])
+    most = run((f32, f32), *rows_e, most_e, [here, left, right])
     for_there, for_own = run((bf16, f32), *rows_e, rest_e, [far_low, far_high], most)
     arrived = lax.ppermute(for_there, "c", SWAP)
     pair_sum = (for_own + arrived.astype(jnp.float32)).astype(jnp.bfloat16)

time: 133 us -> 126 us (0.947)
  starting transfers between devices: 55.3 us -> 40.3 us
  blocking collectives: 49.1 us -> 57 us
    all_to_all x1 -> x0, starting transfers between devices: 15.1 us -> none  [shards(): seeds = lax.all_to_all(wide, 'z', 0, 0)]
    all_gather x1, blocking collectives: 24.5 us -> 32.9 us  [shards(): lax.all_gather(wide.reshape(nz * slab, nh * part), 'z', axis=0, tiled=False)]
    ppermute x1, waiting for transfers between devices: 1.73 us -> 0.01 us  [shards(): there = lax.ppermute(jnp.where(first, odd, even), 'h', SWAP)]
  transfers between devices with their start and end apart: 9 -> 8, of which waited for: 4 -> 3; matrix products, arithmetic and copies ran while one was open for 4% -> 5% of each run, Pallas kernels for 4% -> 4%
where the time goes in v9:
time: 126 us; the launch traced here: 124 us
  blocking collectives  57 us (45%)
  starting transfers between devices  40.3 us (32%)
  waiting for transfers between devices  8.66 us (7%)
  local copies, waits for them, and re-layouts  8.07 us (6%)
  Pallas kernels  6.28 us (5%)
  other arithmetic  3.54 us (3%)
    all_gather x1, blocking collectives, shards(): lax.all_gather(wide.reshape(nz * slab, nh * part), 'z', axis=0, tiled=False)  32.9 us
    all_to_all x1, blocking collectives, shards(): shares = lax.all_to_all(pair_sum.reshape(ny, slab, depth), 'y', 0, 0)  24.1 us
    ppermute x4, starting transfers between devices, shift(): return lax.ppermute(block, ('h', 'l'), ring)  12.9 us
    ppermute x1, starting transfers between devices, shards(): rows_there = lax.ppermute(rows, 'c', SWAP)  9.01 us
    all_to_all x1, starting transfers between devices, shards(): lax.all_to_all(jnp.broadcast_to(seeds[None], (ny, slab, depth)), 'y', 0, 0)  6.82 us
    all_to_all x1, waiting for transfers between devices, shards(): lax.all_to_all(jnp.broadcast_to(seeds[None], (ny, slab, depth)), 'y', 0, 0)  6.42 us
    pallas_call x2, Pallas kernels, run(): pl.pallas_call(lambda *refs: density_kernel(len(cols), kinds, len(befores...  6.28 us
    ppermute x1, starting transfers between devices, shards(): arrived = lax.ppermute(for_there, 'c', SWAP)  6.01 us
  transfers between devices with their start and end apart: 8, of which 3 were waited for; matrix products, arithmetic and copies ran while one was open for 5% of the time, Pallas kernels for 4%

profile of v9, /device:TPU:1, one launch (start us, length us, event | category | flops | bytes accessed | tf_op | source)
XLA Modules:
  0.0 124.1 jit_solution(13020501016385663618)
XLA Ops:
  0.0 1.0 convert_element_type.18
  1.0 5.5 %collective-permute-start = (bf16[12,24,64]{2,1,0:T(8,128)(2,1)S(1)}, bf16[12,24,64]{2,1,0:T(8,128)(2,1)S(1)}, u32[]{:S(2)}, u32[]{:S(2)}) collective-permute-start(bf16[12,24,64]{2,1,0:T(8,128)(2,1)S(1)} %select_bitcast_fusion), channel_id=1, source_target_pairs={{0,32},{32,0},{1,33},{33,1},{2,34},{34,2},{3,35},{35,3},{4,36},{36... | collective-permute-start | bytes 110600 | tf_op jit(solution)/shard_map/ppermute | solution.py:76
  6.5 0.7 multiply_subtract_fusion
  7.2 0.1 slice.76
  7.3 0.1 slice.77
  7.4 0.7 multiply_add_fusion
  8.1 0.1 reshape.189
  8.2 0.1 broadcast_subtract_fusion
  8.3 0.1 sub.117
  8.4 0.1 sub.122
  8.5 0.1 sub.125
  8.6 0.6 dynamic_slice.9
  9.2 0.6 select_subtract_fusion
  9.8 0.1 sub.112
  10.0 0.1 pad_maximum_fusion.1.refs_4_
  10.0 0.1 sub.128.refs_4_
  10.1 0.1 select_n.142
  10.2 0.1 select_n.144
  10.3 0.0 collective-permute-done
  10.3 0.1 pad_maximum_fusion
  10.4 32.9 %all_gather.3.refs_5_ = bf16[12,288,128]{2,1,0:T(8,128)(2,1)S(1)} all-gather(bf16[1,288,128]{2,1,0:T(8,128)(2,1)S(1)} %bitcast.48), channel_id=1, replica_groups=mesh['z'=12,'h'=2,'l'=2,'y'=8,'c'=2] {'z'}, dimensions={0}, use_global_device_ids=true | all-gather | bytes 958464 | tf_op jit(solution)/shard_map/all_gather | solution.py:100
  43.4 0.9 broadcast_in_dim.7
  44.2 6.8 %all-to-all-start = ((bf16[8,24,1536]{2,1,0:T(8,128)(2,1)}), bf16[8,24,1536]{2,1,0:T(8,128)(2,1)S(1)}, u32[]{:S(2)}, u32[]{:S(2)}) async-start(bf16[8,24,1536]{2,1,0:T(8,128)(2,1)} %broadcast_in_dim.7), calls=%async_computation | async-start | bytes 1179648 | tf_op jit(solution)/shard_map/all_to_all | solution.py:110
  51.0 2.2 %collective-permute-start.2 = (bf16[12,288,128]{2,1,0:T(8,128)(2,1)S(1)}, bf16[12,288,128]{2,1,0:T(8,128)(2,1)S(1)}, u32[]{:S(2)}, u32[]{:S(2)}) collective-permute-start(bf16[12,288,128]{2,1,0:T(8,128)(2,1)S(1)} %all_gather.3.refs_5_), channel_id=1, source_target_pairs={{0,16},{16,32},{32,48},{48,0},{1,17},{17,33},{33,49},{49,1},{2,18}... | collective-permute-start | bytes 2654216 | tf_op jit(solution)/shard_map/ppermute | solution.py:104
  53.3 4.3 %collective-permute-start.4 = (bf16[12,288,128]{2,1,0:T(8,128)(2,1)S(1)}, bf16[12,288,128]{2,1,0:T(8,128)(2,1)}, u32[]{:S(2)}, u32[]{:S(2)}) collective-permute-start(bf16[12,288,128]{2,1,0:T(8,128)(2,1)S(1)} %all_gather.3.refs_5_), channel_id=1, source_target_pairs={{0,48},{16,0},{32,16},{48,32},{1,49},{17,1},{33,17},{49,33},{2,50}... | collective-permute-start | bytes 2654216 | tf_op jit(solution)/shard_map/ppermute | solution.py:104
  57.5 6.4 %all-to-all-done = bf16[8,24,1536]{2,1,0:T(8,128)(2,1)S(1)} async-done(((bf16[8,24,1536]{2,1,0:T(8,128)(2,1)}), bf16[8,24,1536]{2,1,0:T(8,128)(2,1)S(1)}, u32[]{:S(2)}, u32[]{:S(2)}) %all-to-all-start) | async-done | bytes 589856 | tf_op jit(solution)/shard_map/all_to_all | solution.py:110
  64.0 9.0 %collective-permute-start.1 = (bf16[192,1536]{1,0:T(8,128)(2,1)S(1)}, bf16[192,1536]{1,0:T(8,128)(2,1)S(1)}, u32[]{:S(2)}, u32[]{:S(2)}) collective-permute-start(bf16[192,1536]{1,0:T(8,128)(2,1)S(1)} %bitcast.42), channel_id=1, source_target_pairs={{0,1},{1,0},{2,3},{3,2},{4,5},{5,4},{6,7},{7,6},{8,9},{9,8},{10,11... | collective-permute-start | bytes 1769480 | tf_op jit(solution)/shard_map/ppermute | solution.py:112
  73.0 0.0 collective-permute-done.2.refs_6_
  73.0 0.8 slice.88
  73.8 0.9 copy-done
  74.8 2.2 %collective-permute-start.3 = (bf16[6,288,128]{2,1,0:T(8,128)(2,1)}, bf16[6,288,128]{2,1,0:T(8,128)(2,1)S(1)}, u32[]{:S(2)}, u32[]{:S(2)}) collective-permute-start(bf16[6,288,128]{2,1,0:T(8,128)(2,1)} %slice.88), channel_id=1, source_target_pairs={{0,16},{16,32},{32,48},{48,0},{1,17},{17,33},{33,49},{49,1},{2,18}... | collective-permute-start | bytes 1327112 | tf_op jit(solution)/shard_map/ppermute | solution.py:104
  77.0 0.0 collective-permute-done.4.refs_7_
  77.0 1.8 %slice.89 = bf16[6,288,128]{2,1,0:T(8,128)(2,1)} slice(bf16[12,288,128]{2,1,0:T(8,128)(2,1)} %collective-permute-done.4.refs_7_), slice={[6:12], [0:288], [0:128]} | slice | bytes 884736 | tf_op jit(solution)/shard_map/slice | solution.py:107
  78.8 4.3 %collective-permute-start.5 = (bf16[6,288,128]{2,1,0:T(8,128)(2,1)}, bf16[6,288,128]{2,1,0:T(8,128)(2,1)S(1)}, u32[]{:S(2)}, u32[]{:S(2)}) collective-permute-start(bf16[6,288,128]{2,1,0:T(8,128)(2,1)} %slice.89), channel_id=1, source_target_pairs={{0,48},{16,0},{32,16},{48,32},{1,49},{17,1},{33,17},{49,33},{2,50}... | collective-permute-start | bytes 1327112 | tf_op jit(solution)/shard_map/ppermute | solution.py:104
  83.1 0.1 copy.18.refs_1_
  83.2 0.1 copy.19.refs_3_
  83.3 0.0 collective-permute-done.1.refs_0_
  83.3 1.2 copy-done.1
  84.5 4.5 %shard_map.37 = (f32[192,1536]{1,0:T(8,128)S(1)}, f32[192,1536]{1,0:T(8,128)S(1)}) custom-call(bf16[192,1536]{1,0:T(8,128)(2,1)S(1)} %collective-permute-done.1.refs_0_, f32[192,1]{1,0:T(8,128)S(1)} %copy.18.refs_1_, bf16[192,1536]{1,0:T(8,128)(2,1)S(1)} %bitcast.43, f32[192,1]{1,0:T(8,128)S(1)} %copy.19.refs_3_, f32[1,864]{1,0:T(1,128)S(1)} %pad_maximum_fusion.1.refs_4_, ...), custom_call_target="tpu_custom_call" | custom-call | flops 2038431744 | bytes 7962624 | tf_op jit(solution)/shard_map/pallas_call | solution.py:53
  89.0 0.0 collective-permute-done.3.refs_5_
  89.0 0.6 collective-permute-done.5.refs_6_
  89.6 1.8 %shard_map.38 = (bf16[192,1536]{1,0:T(8,128)(2,1)S(1)}, f32[192,1536]{1,0:T(8,128)S(1)}) custom-call(bf16[192,1536]{1,0:T(8,128)(2,1)S(1)} %collective-permute-done.1.refs_0_, f32[192,1]{1,0:T(8,128)S(1)} %copy.18.refs_1_, bf16[192,1536]{1,0:T(8,128)(2,1)S(1)} %bitcast.44, f32[192,1]{1,0:T(8,128)S(1)} %copy.19.refs_3_, f32[1,288]{1,0:T(1,128)S(1)} %sub.128.refs_4_, ...), custom_call_target="tpu_custom_call" | custom-call | flops 679477248 | bytes 2654208 | tf_op jit(solution)/shard_map/pallas_call | solution.py:53
  91.4 6.0 %collective-permute-start.6 = (bf16[192,1536]{1,0:T(8,128)(2,1)S(1)}, bf16[192,1536]{1,0:T(8,128)(2,1)S(1)}, u32[]{:S(2)}, u32[]{:S(2)}) collective-permute-start(bf16[192,1536]{1,0:T(8,128)(2,1)S(1)} %get-tuple-element.22), channel_id=1, source_target_pairs={{0,1},{1,0},{2,3},{3,2},{4,5},{5,4},{6,7},{7,6},{8,9},{9,8},{10,11... | collective-permute-start | bytes 1769480 | tf_op jit(solution)/shard_map/ppermute | solution.py:118
  97.4 1.6 %collective-permute-done.6 = bf16[192,1536]{1,0:T(8,128)(2,1)S(1)} collective-permute-done((bf16[192,1536]{1,0:T(8,128)(2,1)S(1)}, bf16[192,1536]{1,0:T(8,128)(2,1)S(1)}, u32[]{:S(2)}, u32[]{:S(2)}) %collective-permute-start.6) | collective-permute-done | bytes 589856 | tf_op jit(solution)/shard_map/ppermute | solution.py:118
  99.0 0.1 add_convert_fusion
  99.2 24.1 %all_to_all.10 = bf16[8,24,1536]{2,1,0:T(8,128)(2,1)S(1)} all-to-all(bf16[8,24,1536]{2,1,0:T(8,128)(2,1)S(1)} %bitcast.45), channel_id=1, replica_groups=mesh['z'=12,'h'=2,'l'=2,'y'=8,'c'=2] {'y'}, dimensions={0} | all-to-all | bytes 1179648 | tf_op jit(solution)/shard_map/all_to_all | solution.py:120
  123.2 0.1 convert_reduce_fusion
  123.3 0.8 broadcast_in_dim.8
  (10 shorter events, 0.1 us)
Async XLA Ops:
  1.0 9.3 %collective-permute-start = (bf16[12,24,64]{2,1,0:T(8,128)(2,1)S(1)}, bf16[12,24,64]{2,1,0:T(8,128)(2,1)S(1)}, u32[]{:S(2)}, u32[]{:S(2)}) collective-permute-start(bf16[12,24,64]{2,1,0:T(8,128)(2,1)S(1)} %select_bitcast_fusion), channel_id=1, source_target_pairs={{0,32},{32,0},{1,33},{33,1},{2,34},{34,2},{3,35},{35,3},{4,36},{36... | collective-permute-start | bytes 110600 | tf_op jit(solution)/shard_map/ppermute | solution.py:76
  44.2 19.7 %all-to-all-start = ((bf16[8,24,1536]{2,1,0:T(8,128)(2,1)}), bf16[8,24,1536]{2,1,0:T(8,128)(2,1)S(1)}, u32[]{:S(2)}, u32[]{:S(2)}) async-start(bf16[8,24,1536]{2,1,0:T(8,128)(2,1)} %broadcast_in_dim.7), calls=%async_computation | async-start | bytes 1179648 | tf_op jit(solution)/shard_map/all_to_all | solution.py:110
  51.0 21.9 %collective-permute-start.2 = (bf16[12,288,128]{2,1,0:T(8,128)(2,1)S(1)}, bf16[12,288,128]{2,1,0:T(8,128)(2,1)S(1)}, u32[]{:S(2)}, u32[]{:S(2)}) collective-permute-start(bf16[12,288,128]{2,1,0:T(8,128)(2,1)S(1)} %all_gather.3.refs_5_), channel_id=1, source_target_pairs={{0,16},{16,32},{32,48},{48,0},{1,17},{17,33},{33,49},{49,1},{2,18}... | collective-permute-start | bytes 2654216 | tf_op jit(solution)/shard_map/ppermute | solution.py:104
  53.3 23.7 %collective-permute-start.4 = (bf16[12,288,128]{2,1,0:T(8,128)(2,1)S(1)}, bf16[12,288,128]{2,1,0:T(8,128)(2,1)}, u32[]{:S(2)}, u32[]{:S(2)}) collective-permute-start(bf16[12,288,128]{2,1,0:T(8,128)(2,1)S(1)} %all_gather.3.refs_5_), channel_id=1, source_target_pairs={{0,48},{16,0},{32,16},{48,32},{1,49},{17,1},{33,17},{49,33},{2,50}... | collective-permute-start | bytes 2654216 | tf_op jit(solution)/shard_map/ppermute | solution.py:104
  64.0 19.4 %collective-permute-start.1 = (bf16[192,1536]{1,0:T(8,128)(2,1)S(1)}, bf16[192,1536]{1,0:T(8,128)(2,1)S(1)}, u32[]{:S(2)}, u32[]{:S(2)}) collective-permute-start(bf16[192,1536]{1,0:T(8,128)(2,1)S(1)} %bitcast.42), channel_id=1, source_target_pairs={{0,1},{1,0},{2,3},{3,2},{4,5},{5,4},{6,7},{7,6},{8,9},{9,8},{10,11... | collective-permute-start | bytes 1769480 | tf_op jit(solution)/shard_map/ppermute | solution.py:112
  73.8 0.9 copy-start
  74.8 14.3 %collective-permute-start.3 = (bf16[6,288,128]{2,1,0:T(8,128)(2,1)}, bf16[6,288,128]{2,1,0:T(8,128)(2,1)S(1)}, u32[]{:S(2)}, u32[]{:S(2)}) collective-permute-start(bf16[6,288,128]{2,1,0:T(8,128)(2,1)} %slice.88), channel_id=1, source_target_pairs={{0,16},{16,32},{32,48},{48,0},{1,17},{17,33},{33,49},{49,1},{2,18}... | collective-permute-start | bytes 1327112 | tf_op jit(solution)/shard_map/ppermute | solution.py:104
  78.8 10.8 %collective-permute-start.5 = (bf16[6,288,128]{2,1,0:T(8,128)(2,1)}, bf16[6,288,128]{2,1,0:T(8,128)(2,1)S(1)}, u32[]{:S(2)}, u32[]{:S(2)}) collective-permute-start(bf16[6,288,128]{2,1,0:T(8,128)(2,1)} %slice.89), channel_id=1, source_target_pairs={{0,48},{16,0},{32,16},{48,32},{1,49},{17,1},{33,17},{49,33},{2,50}... | collective-permute-start | bytes 1327112 | tf_op jit(solution)/shard_map/ppermute | solution.py:104
  83.3 1.2 copy-start.1
  91.4 7.6 %collective-permute-start.6 = (bf16[192,1536]{1,0:T(8,128)(2,1)S(1)}, bf16[192,1536]{1,0:T(8,128)(2,1)S(1)}, u32[]{:S(2)}, u32[]{:S(2)}) collective-permute-start(bf16[192,1536]{1,0:T(8,128)(2,1)S(1)} %get-tuple-element.22), channel_id=1, source_target_pairs={{0,1},{1,0},{2,3},{3,2},{4,5},{5,4},{6,7},{7,6},{8,9},{9,8},{10,11... | collective-permute-start | bytes 1769480 | tf_op jit(solution)/shard_map/ppermute | solution.py:118

commit v10 on v9

--- a/solution.py
+++ b/solution.py
@@ -49,7 +49,6 @@
     vmem = pl.BlockSpec(memory_space=pltpu.VMEM)
     anywhere = pl.BlockSpec(memory_space=pl.ANY)
     width = col_e.shape[1]
-    work = 8 * own.size * width
     return pl.pallas_call(
         lambda *refs: density_kernel(len(cols), kinds, len(befores) > 0, *refs),
         out_shape=[jax.ShapeDtypeStruct(own.shape, kind) for kind in kinds],
@@ -60,7 +59,7 @@
             pltpu.SemaphoreType.DMA((sum(block.shape[0] for block in cols),)),
         ],
         compiler_params=pltpu.CompilerParams(vmem_limit_bytes=14 * 1024 * 1024),
-        cost_estimate=pl.CostEstimate(flops=work, bytes_accessed=work // 256, transcendentals=0),
+        cost_estimate=pl.CostEstimate(flops=1024, bytes_accessed=1024, transcendentals=0),
     )(there, there_e, own, own_e, col_e, *cols, *befores)
 
 

time: 126 us -> 126 us (level)
  local copies, waits for them, and re-layouts: 8.07 us -> 5.95 us
    unnamed x4 -> x0, local copies, waits for them, and re-layouts: 2.1 us -> none
    ppermute x4, waiting for transfers between devices: 0.63 us -> 1.89 us  [shift(): return lax.ppermute(block, ('h', 'l'), ring)]
where the time goes in v10:
time: 126 us; the launch traced here: 124 us
  blocking collectives  57 us (45%)
  starting transfers between devices  40.2 us (32%)
  waiting for transfers between devices  9.92 us (8%)
  Pallas kernels  7.35 us (6%)
  local copies, waits for them, and re-layouts  5.95 us (5%)
  other arithmetic  3.54 us (3%)
    all_gather x1, blocking collectives, shards(): lax.all_gather(wide.reshape(nz * slab, nh * part), 'z', axis=0, tiled=False)  32.9 us
    all_to_all x1, blocking collectives, shards(): shares = lax.all_to_all(pair_sum.reshape(ny, slab, depth), 'y', 0, 0)  24.1 us
    ppermute x4, starting transfers between devices, shift(): return lax.ppermute(block, ('h', 'l'), ring)  13 us
    ppermute x1, starting transfers between devices, shards(): rows_there = lax.ppermute(rows, 'c', SWAP)  9.01 us
    pallas_call x2, Pallas kernels, run(): pl.pallas_call(lambda *refs: density_kernel(len(cols), kinds, len(befores...  7.35 us
    all_to_all x1, starting transfers between devices, shards(): lax.all_to_all(jnp.broadcast_to(seeds[None], (ny, slab, depth)), 'y', 0, 0)  6.82 us
    all_to_all x1, waiting for transfers between devices, shards(): lax.all_to_all(jnp.broadcast_to(seeds[None], (ny, slab, depth)), 'y', 0, 0)  6.42 us
    ppermute x1, starting transfers between devices, shards(): arrived = lax.ppermute(for_there, 'c', SWAP)  5.9 us
  transfers between devices with their start and end apart: 8, of which 3 were waited for; matrix products, arithmetic and copies ran while one was open for 5% of the time, Pallas kernels for 4%

profile of v10, /device:TPU:1, one launch (start us, length us, event | category | flops | bytes accessed | tf_op | source)
XLA Modules:
  0.0 124.2 jit_solution(15230465068661012786)
XLA Ops:
  0.0 1.0 convert_element_type.18
  1.0 5.5 %collective-permute-start = (bf16[12,24,64]{2,1,0:T(8,128)(2,1)S(1)}, bf16[12,24,64]{2,1,0:T(8,128)(2,1)S(1)}, u32[]{:S(2)}, u32[]{:S(2)}) collective-permute-start(bf16[12,24,64]{2,1,0:T(8,128)(2,1)S(1)} %select_bitcast_fusion), channel_id=1, source_target_pairs={{0,32},{32,0},{1,33},{33,1},{2,34},{34,2},{3,35},{35,3},{4,36},{36... | collective-permute-start | bytes 110600 | tf_op jit(solution)/shard_map/ppermute | solution.py:75
  6.5 0.7 multiply_subtract_fusion
  7.2 0.1 slice.76
  7.3 0.1 slice.77
  7.4 0.7 multiply_add_fusion
  8.1 0.1 reshape.189
  8.2 0.1 broadcast_subtract_fusion
  8.3 0.1 sub.117
  8.4 0.1 sub.122
  8.5 0.1 sub.125
  8.6 0.6 dynamic_slice.9
  9.2 0.6 select_subtract_fusion
  9.8 0.1 sub.112
  10.0 0.1 pad_maximum_fusion.1.refs_4_
  10.0 0.1 sub.128.refs_4_
  10.1 0.1 select_n.142
  10.2 0.1 select_n.144
  10.3 0.0 collective-permute-done
  10.3 0.1 pad_maximum_fusion
  10.4 32.9 %all_gather.3.refs_5_ = bf16[12,288,128]{2,1,0:T(8,128)(2,1)S(1)} all-gather(bf16[1,288,128]{2,1,0:T(8,128)(2,1)S(1)} %bitcast.48), channel_id=1, replica_groups=mesh['z'=12,'h'=2,'l'=2,'y'=8,'c'=2] {'z'}, dimensions={0}, use_global_device_ids=true | all-gather | bytes 958464 | tf_op jit(solution)/shard_map/all_gather | solution.py:99
  43.4 0.9 broadcast_in_dim.7
  44.2 6.8 %all-to-all-start = ((bf16[8,24,1536]{2,1,0:T(8,128)(2,1)}), bf16[8,24,1536]{2,1,0:T(8,128)(2,1)S(1)}, u32[]{:S(2)}, u32[]{:S(2)}) async-start(bf16[8,24,1536]{2,1,0:T(8,128)(2,1)} %broadcast_in_dim.7), calls=%async_computation | async-start | bytes 1179648 | tf_op jit(solution)/shard_map/all_to_all | solution.py:109
  51.0 2.2 %collective-permute-start.2 = (bf16[12,288,128]{2,1,0:T(8,128)(2,1)S(1)}, bf16[12,288,128]{2,1,0:T(8,128)(2,1)S(1)}, u32[]{:S(2)}, u32[]{:S(2)}) collective-permute-start(bf16[12,288,128]{2,1,0:T(8,128)(2,1)S(1)} %all_gather.3.refs_5_), channel_id=1, source_target_pairs={{0,16},{16,32},{32,48},{48,0},{1,17},{17,33},{33,49},{49,1},{2,18}... | collective-permute-start | bytes 2654216 | tf_op jit(solution)/shard_map/ppermute | solution.py:103
  53.3 4.3 %collective-permute-start.4 = (bf16[12,288,128]{2,1,0:T(8,128)(2,1)S(1)}, bf16[12,288,128]{2,1,0:T(8,128)(2,1)}, u32[]{:S(2)}, u32[]{:S(2)}) collective-permute-start(bf16[12,288,128]{2,1,0:T(8,128)(2,1)S(1)} %all_gather.3.refs_5_), channel_id=1, source_target_pairs={{0,48},{16,0},{32,16},{48,32},{1,49},{17,1},{33,17},{49,33},{2,50}... | collective-permute-start | bytes 2654216 | tf_op jit(solution)/shard_map/ppermute | solution.py:103
  57.5 6.4 %all-to-all-done = bf16[8,24,1536]{2,1,0:T(8,128)(2,1)S(1)} async-done(((bf16[8,24,1536]{2,1,0:T(8,128)(2,1)}), bf16[8,24,1536]{2,1,0:T(8,128)(2,1)S(1)}, u32[]{:S(2)}, u32[]{:S(2)}) %all-to-all-start) | async-done | bytes 589856 | tf_op jit(solution)/shard_map/all_to_all | solution.py:109
  64.0 9.0 %collective-permute-start.1 = (bf16[192,1536]{1,0:T(8,128)(2,1)S(1)}, bf16[192,1536]{1,0:T(8,128)(2,1)S(1)}, u32[]{:S(2)}, u32[]{:S(2)}) collective-permute-start(bf16[192,1536]{1,0:T(8,128)(2,1)S(1)} %bitcast.42), channel_id=1, source_target_pairs={{0,1},{1,0},{2,3},{3,2},{4,5},{5,4},{6,7},{7,6},{8,9},{9,8},{10,11... | collective-permute-start | bytes 1769480 | tf_op jit(solution)/shard_map/ppermute | solution.py:111
  73.0 0.0 collective-permute-done.2.refs_6_
  73.0 0.8 slice.88
  73.8 2.2 %collective-permute-start.3 = (bf16[6,288,128]{2,1,0:T(8,128)(2,1)}, bf16[6,288,128]{2,1,0:T(8,128)(2,1)}, u32[]{:S(2)}, u32[]{:S(2)}) collective-permute-start(bf16[6,288,128]{2,1,0:T(8,128)(2,1)} %slice.88), channel_id=1, source_target_pairs={{0,16},{16,32},{32,48},{48,0},{1,17},{17,33},{33,49},{49,1},{2,18}... | collective-permute-start | bytes 1327112 | tf_op jit(solution)/shard_map/ppermute | solution.py:103
  76.0 0.0 collective-permute-done.4.refs_7_
  76.0 1.8 %slice.89 = bf16[6,288,128]{2,1,0:T(8,128)(2,1)} slice(bf16[12,288,128]{2,1,0:T(8,128)(2,1)} %collective-permute-done.4.refs_7_), slice={[6:12], [0:288], [0:128]} | slice | bytes 884736 | tf_op jit(solution)/shard_map/slice | solution.py:106
  77.8 4.3 %collective-permute-start.5 = (bf16[6,288,128]{2,1,0:T(8,128)(2,1)}, bf16[6,288,128]{2,1,0:T(8,128)(2,1)}, u32[]{:S(2)}, u32[]{:S(2)}) collective-permute-start(bf16[6,288,128]{2,1,0:T(8,128)(2,1)} %slice.89), channel_id=1, source_target_pairs={{0,48},{16,0},{32,16},{48,32},{1,49},{17,1},{33,17},{49,33},{2,50}... | collective-permute-start | bytes 1327112 | tf_op jit(solution)/shard_map/ppermute | solution.py:103
  82.1 0.1 copy.18.refs_1_
  82.2 0.1 copy.19.refs_3_
  82.4 0.0 collective-permute-done.1.refs_0_
  82.4 4.5 %shard_map.37 = (f32[192,1536]{1,0:T(8,128)S(1)}, f32[192,1536]{1,0:T(8,128)S(1)}) custom-call(bf16[192,1536]{1,0:T(8,128)(2,1)S(1)} %collective-permute-done.1.refs_0_, f32[192,1]{1,0:T(8,128)S(1)} %copy.18.refs_1_, bf16[192,1536]{1,0:T(8,128)(2,1)S(1)} %bitcast.43, f32[192,1]{1,0:T(8,128)S(1)} %copy.19.refs_3_, f32[1,864]{1,0:T(1,128)S(1)} %pad_maximum_fusion.1.refs_4_, ...), custom_call_target="tpu_custom_call" | custom-call | flops 1024 | bytes 1024 | tf_op jit(solution)/shard_map/pallas_call | solution.py:52
  86.9 0.0 collective-permute-done.3.refs_5_
  86.9 1.9 %collective-permute-done.5.refs_6_ = bf16[6,288,128]{2,1,0:T(8,128)(2,1)} collective-permute-done((bf16[6,288,128]{2,1,0:T(8,128)(2,1)}, bf16[6,288,128]{2,1,0:T(8,128)(2,1)}, u32[]{:S(2)}, u32[]{:S(2)}) %collective-permute-start.5) | collective-permute-done | bytes 442400 | tf_op jit(solution)/shard_map/ppermute | solution.py:103
  88.8 2.8 %shard_map.38 = (bf16[192,1536]{1,0:T(8,128)(2,1)S(1)}, f32[192,1536]{1,0:T(8,128)S(1)}) custom-call(bf16[192,1536]{1,0:T(8,128)(2,1)S(1)} %collective-permute-done.1.refs_0_, f32[192,1]{1,0:T(8,128)S(1)} %copy.18.refs_1_, bf16[192,1536]{1,0:T(8,128)(2,1)S(1)} %bitcast.44, f32[192,1]{1,0:T(8,128)S(1)} %copy.19.refs_3_, f32[1,288]{1,0:T(1,128)S(1)} %sub.128.refs_4_, ...), custom_call_target="tpu_custom_call" | custom-call | flops 1024 | bytes 1024 | tf_op jit(solution)/shard_map/pallas_call | solution.py:52
  91.6 5.9 %collective-permute-start.6 = (bf16[192,1536]{1,0:T(8,128)(2,1)S(1)}, bf16[192,1536]{1,0:T(8,128)(2,1)S(1)}, u32[]{:S(2)}, u32[]{:S(2)}) collective-permute-start(bf16[192,1536]{1,0:T(8,128)(2,1)S(1)} %get-tuple-element.22), channel_id=1, source_target_pairs={{0,1},{1,0},{2,3},{3,2},{4,5},{5,4},{6,7},{7,6},{8,9},{9,8},{10,11... | collective-permute-start | bytes 1769480 | tf_op jit(solution)/shard_map/ppermute | solution.py:117
  97.5 1.6 %collective-permute-done.6 = bf16[192,1536]{1,0:T(8,128)(2,1)S(1)} collective-permute-done((bf16[192,1536]{1,0:T(8,128)(2,1)S(1)}, bf16[192,1536]{1,0:T(8,128)(2,1)S(1)}, u32[]{:S(2)}, u32[]{:S(2)}) %collective-permute-start.6) | collective-permute-done | bytes 589856 | tf_op jit(solution)/shard_map/ppermute | solution.py:117
  99.1 0.1 add_convert_fusion
  99.3 24.1 %all_to_all.10 = bf16[8,24,1536]{2,1,0:T(8,128)(2,1)S(1)} all-to-all(bf16[8,24,1536]{2,1,0:T(8,128)(2,1)S(1)} %bitcast.45), channel_id=1, replica_groups=mesh['z'=12,'h'=2,'l'=2,'y'=8,'c'=2] {'y'}, dimensions={0} | all-to-all | bytes 1179648 | tf_op jit(solution)/shard_map/all_to_all | solution.py:119
  123.3 0.1 convert_reduce_fusion
  123.4 0.8 broadcast_in_dim.8
  (8 shorter events, 0.1 us)
Async XLA Ops:
  1.0 9.3 %collective-permute-start = (bf16[12,24,64]{2,1,0:T(8,128)(2,1)S(1)}, bf16[12,24,64]{2,1,0:T(8,128)(2,1)S(1)}, u32[]{:S(2)}, u32[]{:S(2)}) collective-permute-start(bf16[12,24,64]{2,1,0:T(8,128)(2,1)S(1)} %select_bitcast_fusion), channel_id=1, source_target_pairs={{0,32},{32,0},{1,33},{33,1},{2,34},{34,2},{3,35},{35,3},{4,36},{36... | collective-permute-start | bytes 110600 | tf_op jit(solution)/shard_map/ppermute | solution.py:75
  44.2 19.7 %all-to-all-start = ((bf16[8,24,1536]{2,1,0:T(8,128)(2,1)}), bf16[8,24,1536]{2,1,0:T(8,128)(2,1)S(1)}, u32[]{:S(2)}, u32[]{:S(2)}) async-start(bf16[8,24,1536]{2,1,0:T(8,128)(2,1)} %broadcast_in_dim.7), calls=%async_computation | async-start | bytes 1179648 | tf_op jit(solution)/shard_map/all_to_all | solution.py:109
  51.0 21.9 %collective-permute-start.2 = (bf16[12,288,128]{2,1,0:T(8,128)(2,1)S(1)}, bf16[12,288,128]{2,1,0:T(8,128)(2,1)S(1)}, u32[]{:S(2)}, u32[]{:S(2)}) collective-permute-start(bf16[12,288,128]{2,1,0:T(8,128)(2,1)S(1)} %all_gather.3.refs_5_), channel_id=1, source_target_pairs={{0,16},{16,32},{32,48},{48,0},{1,17},{17,33},{33,49},{49,1},{2,18}... | collective-permute-start | bytes 2654216 | tf_op jit(solution)/shard_map/ppermute | solution.py:103
  53.3 22.8 %collective-permute-start.4 = (bf16[12,288,128]{2,1,0:T(8,128)(2,1)S(1)}, bf16[12,288,128]{2,1,0:T(8,128)(2,1)}, u32[]{:S(2)}, u32[]{:S(2)}) collective-permute-start(bf16[12,288,128]{2,1,0:T(8,128)(2,1)S(1)} %all_gather.3.refs_5_), channel_id=1, source_target_pairs={{0,48},{16,0},{32,16},{48,32},{1,49},{17,1},{33,17},{49,33},{2,50}... | collective-permute-start | bytes 2654216 | tf_op jit(solution)/shard_map/ppermute | solution.py:103
  64.0 18.4 %collective-permute-start.1 = (bf16[192,1536]{1,0:T(8,128)(2,1)S(1)}, bf16[192,1536]{1,0:T(8,128)(2,1)S(1)}, u32[]{:S(2)}, u32[]{:S(2)}) collective-permute-start(bf16[192,1536]{1,0:T(8,128)(2,1)S(1)} %bitcast.42), channel_id=1, source_target_pairs={{0,1},{1,0},{2,3},{3,2},{4,5},{5,4},{6,7},{7,6},{8,9},{9,8},{10,11... | collective-permute-start | bytes 1769480 | tf_op jit(solution)/shard_map/ppermute | solution.py:111
  73.8 13.1 %collective-permute-start.3 = (bf16[6,288,128]{2,1,0:T(8,128)(2,1)}, bf16[6,288,128]{2,1,0:T(8,128)(2,1)}, u32[]{:S(2)}, u32[]{:S(2)}) collective-permute-start(bf16[6,288,128]{2,1,0:T(8,128)(2,1)} %slice.88), channel_id=1, source_target_pairs={{0,16},{16,32},{32,48},{48,0},{1,17},{17,33},{33,49},{49,1},{2,18}... | collective-permute-start | bytes 1327112 | tf_op jit(solution)/shard_map/ppermute | solution.py:103
  77.8 11.0 %collective-permute-start.5 = (bf16[6,288,128]{2,1,0:T(8,128)(2,1)}, bf16[6,288,128]{2,1,0:T(8,128)(2,1)}, u32[]{:S(2)}, u32[]{:S(2)}) collective-permute-start(bf16[6,288,128]{2,1,0:T(8,128)(2,1)} %slice.89), channel_id=1, source_target_pairs={{0,48},{16,0},{32,16},{48,32},{1,49},{17,1},{33,17},{49,33},{2,50}... | collective-permute-start | bytes 1327112 | tf_op jit(solution)/shard_map/ppermute | solution.py:103
  91.6 7.5 %collective-permute-start.6 = (bf16[192,1536]{1,0:T(8,128)(2,1)S(1)}, bf16[192,1536]{1,0:T(8,128)(2,1)S(1)}, u32[]{:S(2)}, u32[]{:S(2)}) collective-permute-start(bf16[192,1536]{1,0:T(8,128)(2,1)S(1)} %get-tuple-element.22), channel_id=1, source_target_pairs={{0,1},{1,0},{2,3},{3,2},{4,5},{5,4},{6,7},{7,6},{8,9},{9,8},{10,11... | collective-permute-start | bytes 1769480 | tf_op jit(solution)/shard_map/ppermute | solution.py:117

commit v11 on v9

--- a/solution.py
+++ b/solution.py
@@ -14,10 +14,12 @@
 SWAP = [(0, 1), (1, 0)]
 
 
-def density_kernel(blocks, kinds, more, there_ref, there_e, own_ref, own_e, col_e, *refs):
+def density_kernel(sides, blocks, more, col_e, *refs):
+    rows_refs, refs = refs[:sides], refs[sides:]
+    row_es, refs = refs[:sides], refs[sides:]
     cols_refs, refs = refs[:blocks], refs[blocks:]
-    befores, refs = (refs[:2], refs[2:]) if more else ((None, None), refs)
-    outs, (full, sem) = refs[:2], refs[2:]
+    befores, refs = (refs[:sides], refs[sides:]) if more else ([None] * sides, refs)
+    outs, (full, sem) = refs[:sides], refs[sides:]
     copies, first, left = [], 0, 0
     for cols_ref in cols_refs:
         chunks, width, lanes = cols_ref.shape
@@ -31,37 +33,37 @@
         copy.start()
     for copy in copies:
         copy.wait()
-    rows = jnp.concatenate([there_ref[...], own_ref[...]], axis=0)
-    row_e = jnp.concatenate([there_e[...], own_e[...]], axis=0)
+    rows = jnp.concatenate([ref[...] for ref in rows_refs], axis=0)
+    row_e = jnp.concatenate([ref[...] for ref in row_es], axis=0)
     pair = lax.dot_general(
         rows, full[...], (((1,), (1,)), ((), ())), preferred_element_type=jnp.float32
     )
     amplitude = (spin_scale * pair / (row_e + col_e[...])).astype(jnp.bfloat16)
     terms = jnp.dot(amplitude, full[...], preferred_element_type=jnp.float32)
-    count = own_ref.shape[0]
-    for term, before_ref, out_ref in zip((terms[:count], terms[count:]), befores, outs):
+    count = outs[0].shape[0]
+    for k, (before_ref, out_ref) in enumerate(zip(befores, outs)):
+        term = terms[k * count : (k + 1) * count]
         if more:
             term = term + before_ref[...]
         out_ref[...] = term.astype(out_ref.dtype)
 
 
-def run(kinds, there, there_e, own, own_e, col_e, cols, befores=()):
+def run(kind, work, rows, row_es, col_e, cols, befores=()):
     vmem = pl.BlockSpec(memory_space=pltpu.VMEM)
     anywhere = pl.BlockSpec(memory_space=pl.ANY)
-    width = col_e.shape[1]
-    work = 8 * own.size * width
+    sides, blocks = len(rows), len(cols)
     return pl.pallas_call(
-        lambda *refs: density_kernel(len(cols), kinds, len(befores) > 0, *refs),
-        out_shape=[jax.ShapeDtypeStruct(own.shape, kind) for kind in kinds],
-        in_specs=[vmem] * 5 + [anywhere] * len(cols) + [vmem] * len(befores),
-        out_specs=[vmem, vmem],
+        lambda *refs: density_kernel(sides, blocks, len(befores) > 0, *refs),
+        out_shape=[jax.ShapeDtypeStruct(side.shape, kind) for side in rows],
+        in_specs=[vmem] * (1 + 2 * sides) + [anywhere] * blocks + [vmem] * len(befores),
+        out_specs=[vmem] * sides,
         scratch_shapes=[
-            pltpu.VMEM((width, own.shape[1]), jnp.bfloat16),
+            pltpu.VMEM((col_e.shape[1], rows[0].shape[1]), jnp.bfloat16),
             pltpu.SemaphoreType.DMA((sum(block.shape[0] for block in cols),)),
         ],
         compiler_params=pltpu.CompilerParams(vmem_limit_bytes=14 * 1024 * 1024),
         cost_estimate=pl.CostEstimate(flops=work, bytes_accessed=work // 256, transcendentals=0),
-    )(there, there_e, own, own_e, col_e, *cols, *befores)
+    )(col_e, *rows, *row_es, *cols, *befores)
 
 
 def shards(integrals, occ_bins, vir_bins):
@@ -78,11 +80,7 @@
     occupied = occupied_base - occupied_step * occ_bins.astype(jnp.float32)
     virtual = virtual_base + virtual_step * vir_bins.astype(jnp.float32)
     virtual = virtual.reshape(nl, ny, 2, slab)
-    occ_own = lax.dynamic_slice_in_dim(occupied, z * nh + h, 1, 0)
     core0, low0 = c == 0, l == 0
-    of_rows = jnp.where(low0, virtual[0], virtual[1]) - occ_own
-    own_e = jnp.where(core0, of_rows[:, 0], of_rows[:, 1]).reshape(-1, 1)
-    there_e = jnp.where(core0, of_rows[:, 1], of_rows[:, 0]).reshape(-1, 1)
     of_cols = lax.dynamic_slice_in_dim(virtual, y, 1, 1)[:, 0]
     of_cols = jnp.where(core0, of_cols[:, 0], of_cols[:, 1])
     low_own = jnp.where(low0, of_cols[0], of_cols[1])
@@ -94,9 +92,7 @@
 
     most_e = [col_e(low_own, h == 0), col_e(low_other, h != l), col_e(low_other, h == l)]
     rest_e = col_e(low_own, h != 0)
-    wide, own_e, there_e, most_e, rest_e = lax.optimization_barrier(
-        (wide, own_e, there_e, jnp.concatenate(most_e, axis=1), rest_e)
-    )
+    wide, most_e, rest_e = lax.optimization_barrier((wide, jnp.concatenate(most_e, axis=1), rest_e))
     here = lax.all_gather(wide.reshape(nz * slab, nh * part), "z", axis=0, tiled=False)
 
     def shift(block, by):
@@ -109,13 +105,20 @@
     seeds = jnp.transpose(seeds, (1, 0, 2)).reshape(slab, depth)
     rows = lax.all_to_all(jnp.broadcast_to(seeds[None], (ny, slab, depth)), "y", 0, 0)
     rows = rows.reshape(ny * slab, depth)
+    rows, virtual, occupied = lax.optimization_barrier((rows, virtual, occupied))
     rows_there = lax.ppermute(rows, "c", SWAP)
+    occ_own = lax.dynamic_slice_in_dim(occupied, z * nh + h, 1, 0)
+    of_rows = jnp.where(low0, virtual[0], virtual[1]) - occ_own
+    own_e = jnp.where(core0, of_rows[:, 0], of_rows[:, 1]).reshape(-1, 1)
+    there_e = jnp.where(core0, of_rows[:, 1], of_rows[:, 0]).reshape(-1, 1)
 
     f32, bf16 = jnp.float32, jnp.bfloat16
-    rows_e = (rows_there, there_e, rows, own_e)
-    most = run((f32, f32), *rows_e, most_e, [here, left, right])
-    for_there, for_own = run((bf16, f32), *rows_e, rest_e, [far_low, far_high], most)
+    both, both_e = [rows_there, rows], [there_e, own_e]
+    far, work = [far_low, far_high], 4 * rest_e.size * rows.size
+    most = run(f32, 1024, both, both_e, most_e, [here, left, right])
+    (for_there,) = run(bf16, work, both[:1], both_e[:1], rest_e, far, most[:1])
     arrived = lax.ppermute(for_there, "c", SWAP)
+    (for_own,) = run(f32, work, both[1:], both_e[1:], rest_e, far, most[1:])
     pair_sum = (for_own + arrived.astype(jnp.float32)).astype(jnp.bfloat16)
     shares = lax.all_to_all(pair_sum.reshape(ny, slab, depth), "y", 0, 0)
     density = jnp.sum(shares.astype(jnp.float32), axis=0)

time: 126 us -> 126 us (level)
  Pallas kernels: 6.28 us -> 9.14 us
  waiting for transfers between devices: 8.66 us -> 7.37 us
    pallas_call x2 -> x3, Pallas kernels: 6.28 us -> 9.14 us  [run(): pl.pallas_call(lambda *refs: density_kernel(sides, blocks, len(befores) >...]
    ppermute x1, waiting for transfers between devices: 1.61 us -> 0.01 us  [shards(): arrived = lax.ppermute(for_there, 'c', SWAP)]
    ppermute x1, starting transfers between devices: 6.01 us -> 4.44 us  [shards(): arrived = lax.ppermute(for_there, 'c', SWAP)]
  transfers between devices with their start and end apart: 8 -> 8, of which waited for: 3 -> 2; matrix products, arithmetic and copies ran while one was open for 5% -> 5% of each run, Pallas kernels for 4% -> 5%
where the time goes in v11:
time: 126 us; the launch traced here: 125 us
  blocking collectives  57.5 us (46%)
  starting transfers between devices  39.9 us (32%)
  Pallas kernels  9.14 us (7%)
  waiting for transfers between devices  7.37 us (6%)
  local copies, waits for them, and re-layouts  7.2 us (6%)
  other arithmetic  3.51 us (3%)
    all_gather x1, blocking collectives, shards(): lax.all_gather(wide.reshape(nz * slab, nh * part), 'z', axis=0, tiled=False)  32.5 us
    all_to_all x1, blocking collectives, shards(): shares = lax.all_to_all(pair_sum.reshape(ny, slab, depth), 'y', 0, 0)  25 us
    ppermute x4, starting transfers between devices, shift(): return lax.ppermute(block, ('h', 'l'), ring)  13 us
    ppermute x1, starting transfers between devices, shards(): rows_there = lax.ppermute(rows, 'c', SWAP)  10.2 us
    pallas_call x3, Pallas kernels, run(): pl.pallas_call(lambda *refs: density_kernel(sides, blocks, len(befores) >...  9.14 us
    all_to_all x1, starting transfers between devices, shards(): lax.all_to_all(jnp.broadcast_to(seeds[None], (ny, slab, depth)), 'y', 0, 0)  6.82 us
    all_to_all x1, waiting for transfers between devices, shards(): lax.all_to_all(jnp.broadcast_to(seeds[None], (ny, slab, depth)), 'y', 0, 0)  6.45 us
    ppermute x1, starting transfers between devices, shards(): there = lax.ppermute(jnp.where(first, odd, even), 'h', SWAP)  5.48 us
  transfers between devices with their start and end apart: 8, of which 2 were waited for; matrix products, arithmetic and copies ran while one was open for 5% of the time, Pallas kernels for 5%

profile of v11, /device:TPU:1, one launch (start us, length us, event | category | flops | bytes accessed | tf_op | source)
XLA Modules:
  0.0 124.9 jit_solution(10855461420387389728)
XLA Ops:
  0.0 1.0 convert_element_type.18
  1.0 5.5 %collective-permute-start = (bf16[12,24,64]{2,1,0:T(8,128)(2,1)S(1)}, bf16[12,24,64]{2,1,0:T(8,128)(2,1)S(1)}, u32[]{:S(2)}, u32[]{:S(2)}) collective-permute-start(bf16[12,24,64]{2,1,0:T(8,128)(2,1)S(1)} %select_bitcast_fusion), channel_id=1, source_target_pairs={{0,32},{32,0},{1,33},{33,1},{2,34},{34,2},{3,35},{35,3},{4,36},{36... | collective-permute-start | bytes 110600 | tf_op jit(solution)/shard_map/ppermute | solution.py:78
  6.5 0.7 multiply_subtract_fusion
  7.2 0.1 slice.54
  7.3 0.1 slice.55
  7.4 0.7 multiply_add_fusion
  8.1 0.1 reshape.169
  8.2 0.1 broadcast_subtract_fusion
  8.3 0.1 sub.113
  8.4 0.1 sub.118
  8.5 0.1 sub.121
  8.6 0.1 pad_maximum_fusion.1.refs_0_
  8.7 0.1 sub.124.refs_0_
  8.8 0.0 collective-permute-done
  8.8 0.1 pad_maximum_fusion
  8.9 32.5 %all_gather.3.refs_5_ = bf16[12,288,128]{2,1,0:T(8,128)(2,1)S(1)} all-gather(bf16[1,288,128]{2,1,0:T(8,128)(2,1)S(1)} %bitcast.50), channel_id=1, replica_groups=mesh['z'=12,'h'=2,'l'=2,'y'=8,'c'=2] {'z'}, dimensions={0}, use_global_device_ids=true | all-gather | bytes 958464 | tf_op jit(solution)/shard_map/all_gather | solution.py:96
  41.4 0.9 broadcast_in_dim.7
  42.3 6.8 %all-to-all-start = ((bf16[8,24,1536]{2,1,0:T(8,128)(2,1)}), bf16[8,24,1536]{2,1,0:T(8,128)(2,1)S(1)}, u32[]{:S(2)}, u32[]{:S(2)}) async-start(bf16[8,24,1536]{2,1,0:T(8,128)(2,1)} %broadcast_in_dim.7), calls=%async_computation | async-start | bytes 1179648 | tf_op jit(solution)/shard_map/all_to_all | solution.py:106
  49.1 3.2 %collective-permute-start.1 = (bf16[12,288,128]{2,1,0:T(8,128)(2,1)S(1)}, bf16[12,288,128]{2,1,0:T(8,128)(2,1)S(1)}, u32[]{:S(2)}, u32[]{:S(2)}) collective-permute-start(bf16[12,288,128]{2,1,0:T(8,128)(2,1)S(1)} %all_gather.3.refs_5_), channel_id=1, source_target_pairs={{0,16},{16,32},{32,48},{48,0},{1,17},{17,33},{33,49},{49,1},{2,18}... | collective-permute-start | bytes 2654216 | tf_op jit(solution)/shard_map/ppermute | solution.py:100
  52.3 3.3 %collective-permute-start.3 = (bf16[12,288,128]{2,1,0:T(8,128)(2,1)S(1)}, bf16[12,288,128]{2,1,0:T(8,128)(2,1)}, u32[]{:S(2)}, u32[]{:S(2)}) collective-permute-start(bf16[12,288,128]{2,1,0:T(8,128)(2,1)S(1)} %all_gather.3.refs_5_), channel_id=1, source_target_pairs={{0,48},{16,0},{32,16},{48,32},{1,49},{17,1},{33,17},{49,33},{2,50}... | collective-permute-start | bytes 2654216 | tf_op jit(solution)/shard_map/ppermute | solution.py:100
  55.6 6.5 %all-to-all-done = bf16[8,24,1536]{2,1,0:T(8,128)(2,1)S(1)} async-done(((bf16[8,24,1536]{2,1,0:T(8,128)(2,1)}), bf16[8,24,1536]{2,1,0:T(8,128)(2,1)S(1)}, u32[]{:S(2)}, u32[]{:S(2)}) %all-to-all-start) | async-done | bytes 589856 | tf_op jit(solution)/shard_map/all_to_all | solution.py:106
  62.0 10.2 %collective-permute-start.5 = (bf16[192,1536]{1,0:T(8,128)(2,1)S(1)}, bf16[192,1536]{1,0:T(8,128)(2,1)S(1)}, u32[]{:S(2)}, u32[]{:S(2)}) collective-permute-start(bf16[192,1536]{1,0:T(8,128)(2,1)S(1)} %bitcast.44), channel_id=1, source_target_pairs={{0,1},{1,0},{2,3},{3,2},{4,5},{5,4},{6,7},{7,6},{8,9},{9,8},{10,11... | collective-permute-start | bytes 1769480 | tf_op jit(solution)/shard_map/ppermute | solution.py:109
  72.2 0.0 collective-permute-done.1.refs_6_
  72.2 0.8 slice.70
  73.0 2.7 %collective-permute-start.2 = (bf16[6,288,128]{2,1,0:T(8,128)(2,1)}, bf16[6,288,128]{2,1,0:T(8,128)(2,1)S(1)}, u32[]{:S(2)}, u32[]{:S(2)}) collective-permute-start(bf16[6,288,128]{2,1,0:T(8,128)(2,1)} %slice.70), channel_id=1, source_target_pairs={{0,16},{16,32},{32,48},{48,0},{1,17},{17,33},{33,49},{49,1},{2,18}... | collective-permute-start | bytes 1327112 | tf_op jit(solution)/shard_map/ppermute | solution.py:100
  75.7 0.0 collective-permute-done.3.refs_7_
  75.7 1.8 %slice.71 = bf16[6,288,128]{2,1,0:T(8,128)(2,1)} slice(bf16[12,288,128]{2,1,0:T(8,128)(2,1)} %collective-permute-done.3.refs_7_), slice={[6:12], [0:288], [0:128]} | slice | bytes 884736 | tf_op jit(solution)/shard_map/slice | solution.py:103
  77.5 3.8 %collective-permute-start.4 = (bf16[6,288,128]{2,1,0:T(8,128)(2,1)}, bf16[6,288,128]{2,1,0:T(8,128)(2,1)}, u32[]{:S(2)}, u32[]{:S(2)}) collective-permute-start(bf16[6,288,128]{2,1,0:T(8,128)(2,1)} %slice.71), channel_id=1, source_target_pairs={{0,48},{16,0},{32,16},{48,32},{1,49},{17,1},{33,17},{49,33},{2,50}... | collective-permute-start | bytes 1327112 | tf_op jit(solution)/shard_map/ppermute | solution.py:100
  81.3 0.6 dynamic_slice.11
  81.9 0.7 subtract_bitcast_fusion
  82.6 0.1 select_n.160.refs_4_.refs_2_
  82.7 0.7 select_n.161.refs_3_.refs_2_
  83.5 0.0 collective-permute-done.5.refs_1_
  83.5 0.0 copy-start
  83.5 0.9 copy-done
  84.4 4.5 %shard_map.37 = (f32[192,1536]{1,0:T(8,128)S(1)}, f32[192,1536]{1,0:T(8,128)S(1)}) custom-call(f32[1,864]{1,0:T(1,128)S(1)} %pad_maximum_fusion.1.refs_0_, bf16[192,1536]{1,0:T(8,128)(2,1)S(1)} %collective-permute-done.5.refs_1_, bf16[192,1536]{1,0:T(8,128)(2,1)S(1)} %bitcast.45, f32[192,1]{1,0:T(8,128)S(1)} %copy-done, ...), custom_call_target="tpu_custom_call" | custom-call | flops 1024 | bytes 4 | tf_op jit(solution)/shard_map/pallas_call | solution.py:55
  88.9 0.0 collective-permute-done.2.refs_3_
  88.9 0.9 collective-permute-done.4.refs_4_
  89.8 2.3 %shard_map.39 = bf16[192,1536]{1,0:T(8,128)(2,1)S(1)} custom-call(f32[1,288]{1,0:T(1,128)S(1)} %sub.124.refs_0_, bf16[192,1536]{1,0:T(8,128)(2,1)S(1)} %collective-permute-done.5.refs_1_, f32[192,1]{1,0:T(8,128)S(1)} %copy-done, bf16[6,288,128]{2,1,0:T(8,128)(2,1)S(1)} %collective-permute-done.2.refs_3_, ...), custom_call_target="tpu_custom_call" | custom-call | flops 339738624 | bytes 1327104 | tf_op jit(solution)/shard_map/pallas_call | solution.py:55
  92.1 4.4 %collective-permute-start.6 = (bf16[192,1536]{1,0:T(8,128)(2,1)S(1)}, bf16[192,1536]{1,0:T(8,128)(2,1)S(1)}, u32[]{:S(2)}, u32[]{:S(2)}) collective-permute-start(bf16[192,1536]{1,0:T(8,128)(2,1)S(1)} %shard_map.39), channel_id=1, source_target_pairs={{0,1},{1,0},{2,3},{3,2},{4,5},{5,4},{6,7},{7,6},{8,9},{9,8},{10,11... | collective-permute-start | bytes 1769480 | tf_op jit(solution)/shard_map/ppermute | solution.py:120
  96.6 2.3 %shard_map.38 = f32[192,1536]{1,0:T(8,128)S(1)} custom-call(f32[1,288]{1,0:T(1,128)S(1)} %sub.124.refs_0_, bf16[192,1536]{1,0:T(8,128)(2,1)S(1)} %bitcast.46, f32[192,1]{1,0:T(8,128)S(1)} %select_n.160.refs_4_.refs_2_, bf16[6,288,128]{2,1,0:T(8,128)(2,1)S(1)} %collective-permute-done.2.refs_3_, bf16[6,288,128]{2,1,0:T(8,128)(2,1)} %collective-permute-done.4.refs_4_, ...), custom_call_target="tpu_custom_call" | custom-call | flops 339738624 | bytes 1327104 | tf_op jit(solution)/shard_map/pallas_call | solution.py:55
  98.9 0.0 collective-permute-done.6
  98.9 0.1 add_convert_fusion
  99.0 25.0 %all_to_all.10 = bf16[8,24,1536]{2,1,0:T(8,128)(2,1)S(1)} all-to-all(bf16[8,24,1536]{2,1,0:T(8,128)(2,1)S(1)} %bitcast.47), channel_id=1, replica_groups=mesh['z'=12,'h'=2,'l'=2,'y'=8,'c'=2] {'y'}, dimensions={0} | all-to-all | bytes 1179648 | tf_op jit(solution)/shard_map/all_to_all | solution.py:123
  124.0 0.1 convert_reduce_fusion
  124.1 0.8 broadcast_in_dim.8
  (8 shorter events, 0.1 us)
Async XLA Ops:
  1.0 7.8 %collective-permute-start = (bf16[12,24,64]{2,1,0:T(8,128)(2,1)S(1)}, bf16[12,24,64]{2,1,0:T(8,128)(2,1)S(1)}, u32[]{:S(2)}, u32[]{:S(2)}) collective-permute-start(bf16[12,24,64]{2,1,0:T(8,128)(2,1)S(1)} %select_bitcast_fusion), channel_id=1, source_target_pairs={{0,32},{32,0},{1,33},{33,1},{2,34},{34,2},{3,35},{35,3},{4,36},{36... | collective-permute-start | bytes 110600 | tf_op jit(solution)/shard_map/ppermute | solution.py:78
  42.3 19.8 %all-to-all-start = ((bf16[8,24,1536]{2,1,0:T(8,128)(2,1)}), bf16[8,24,1536]{2,1,0:T(8,128)(2,1)S(1)}, u32[]{:S(2)}, u32[]{:S(2)}) async-start(bf16[8,24,1536]{2,1,0:T(8,128)(2,1)} %broadcast_in_dim.7), calls=%async_computation | async-start | bytes 1179648 | tf_op jit(solution)/shard_map/all_to_all | solution.py:106
  49.1 23.1 %collective-permute-start.1 = (bf16[12,288,128]{2,1,0:T(8,128)(2,1)S(1)}, bf16[12,288,128]{2,1,0:T(8,128)(2,1)S(1)}, u32[]{:S(2)}, u32[]{:S(2)}) collective-permute-start(bf16[12,288,128]{2,1,0:T(8,128)(2,1)S(1)} %all_gather.3.refs_5_), channel_id=1, source_target_pairs={{0,16},{16,32},{32,48},{48,0},{1,17},{17,33},{33,49},{49,1},{2,18}... | collective-permute-start | bytes 2654216 | tf_op jit(solution)/shard_map/ppermute | solution.py:100
  52.3 23.4 %collective-permute-start.3 = (bf16[12,288,128]{2,1,0:T(8,128)(2,1)S(1)}, bf16[12,288,128]{2,1,0:T(8,128)(2,1)}, u32[]{:S(2)}, u32[]{:S(2)}) collective-permute-start(bf16[12,288,128]{2,1,0:T(8,128)(2,1)S(1)} %all_gather.3.refs_5_), channel_id=1, source_target_pairs={{0,48},{16,0},{32,16},{48,32},{1,49},{17,1},{33,17},{49,33},{2,50}... | collective-permute-start | bytes 2654216 | tf_op jit(solution)/shard_map/ppermute | solution.py:100
  62.0 21.4 %collective-permute-start.5 = (bf16[192,1536]{1,0:T(8,128)(2,1)S(1)}, bf16[192,1536]{1,0:T(8,128)(2,1)S(1)}, u32[]{:S(2)}, u32[]{:S(2)}) collective-permute-start(bf16[192,1536]{1,0:T(8,128)(2,1)S(1)} %bitcast.44), channel_id=1, source_target_pairs={{0,1},{1,0},{2,3},{3,2},{4,5},{5,4},{6,7},{7,6},{8,9},{9,8},{10,11... | collective-permute-start | bytes 1769480 | tf_op jit(solution)/shard_map/ppermute | solution.py:109
  73.0 15.9 %collective-permute-start.2 = (bf16[6,288,128]{2,1,0:T(8,128)(2,1)}, bf16[6,288,128]{2,1,0:T(8,128)(2,1)S(1)}, u32[]{:S(2)}, u32[]{:S(2)}) collective-permute-start(bf16[6,288,128]{2,1,0:T(8,128)(2,1)} %slice.70), channel_id=1, source_target_pairs={{0,16},{16,32},{32,48},{48,0},{1,17},{17,33},{33,49},{49,1},{2,18}... | collective-permute-start | bytes 1327112 | tf_op jit(solution)/shard_map/ppermute | solution.py:100
  77.5 12.2 %collective-permute-start.4 = (bf16[6,288,128]{2,1,0:T(8,128)(2,1)}, bf16[6,288,128]{2,1,0:T(8,128)(2,1)}, u32[]{:S(2)}, u32[]{:S(2)}) collective-permute-start(bf16[6,288,128]{2,1,0:T(8,128)(2,1)} %slice.71), channel_id=1, source_target_pairs={{0,48},{16,0},{32,16},{48,32},{1,49},{17,1},{33,17},{49,33},{2,50}... | collective-permute-start | bytes 1327112 | tf_op jit(solution)/shard_map/ppermute | solution.py:100
  83.5 0.9 copy-start
  92.1 6.8 %collective-permute-start.6 = (bf16[192,1536]{1,0:T(8,128)(2,1)S(1)}, bf16[192,1536]{1,0:T(8,128)(2,1)S(1)}, u32[]{:S(2)}, u32[]{:S(2)}) collective-permute-start(bf16[192,1536]{1,0:T(8,128)(2,1)S(1)} %shard_map.39), channel_id=1, source_target_pairs={{0,1},{1,0},{2,3},{3,2},{4,5},{5,4},{6,7},{7,6},{8,9},{9,8},{10,11... | collective-permute-start | bytes 1769480 | tf_op jit(solution)/shard_map/ppermute | solution.py:120

commit v12 on v11

--- a/solution.py
+++ b/solution.py
@@ -48,13 +48,13 @@
         out_ref[...] = term.astype(out_ref.dtype)
 
 
-def run(kind, work, rows, row_es, col_e, cols, befores=()):
+def run(kinds, work, rows, row_es, col_e, cols, befores=()):
     vmem = pl.BlockSpec(memory_space=pltpu.VMEM)
     anywhere = pl.BlockSpec(memory_space=pl.ANY)
     sides, blocks = len(rows), len(cols)
     return pl.pallas_call(
         lambda *refs: density_kernel(sides, blocks, len(befores) > 0, *refs),
-        out_shape=[jax.ShapeDtypeStruct(side.shape, kind) for side in rows],
+        out_shape=[jax.ShapeDtypeStruct(side.shape, kind) for side, kind in zip(rows, kinds)],
         in_specs=[vmem] * (1 + 2 * sides) + [anywhere] * blocks + [vmem] * len(befores),
         out_specs=[vmem] * sides,
         scratch_shapes=[
@@ -90,17 +90,20 @@
     def col_e(low, is_even):
         return (low[None, :] - jnp.where(is_even, evens, odds)[:, None]).reshape(1, -1)
 
-    most_e = [col_e(low_own, h == 0), col_e(low_other, h != l), col_e(low_other, h == l)]
+    near_even = (h != l) == core0
+    most_e = [col_e(low_own, h == 0), col_e(low_other, near_even), col_e(low_other, ~near_even)]
     rest_e = col_e(low_own, h != 0)
     wide, most_e, rest_e = lax.optimization_barrier((wide, jnp.concatenate(most_e, axis=1), rest_e))
     here = lax.all_gather(wide.reshape(nz * slab, nh * part), "z", axis=0, tiled=False)
 
     def shift(block, by):
-        ring = [(k, (k + by) % (nh * nl)) for k in range(nh * nl)]
-        return lax.ppermute(block, ("h", "l"), ring)
+        count = nh * nl
+        ring = [(2 * k, 2 * ((k + by) % count)) for k in range(count)]
+        ring += [(2 * k + 1, 2 * ((k - by) % count) + 1) for k in range(count)]
+        return lax.ppermute(block, ("h", "l", "c"), ring)
 
-    left, right = shift(here, 1), shift(here, -1)
-    far_low, far_high = shift(left[: nz // 2], 1), shift(right[nz // 2 :], -1)
+    near, off = shift(here, 1), shift(here, -1)
+    far = shift(near, 1)
     seeds = lax.dynamic_slice_in_dim(here, z * slab, slab, 1)
     seeds = jnp.transpose(seeds, (1, 0, 2)).reshape(slab, depth)
     rows = lax.all_to_all(jnp.broadcast_to(seeds[None], (ny, slab, depth)), "y", 0, 0)
@@ -114,11 +117,10 @@
 
     f32, bf16 = jnp.float32, jnp.bfloat16
     both, both_e = [rows_there, rows], [there_e, own_e]
-    far, work = [far_low, far_high], 4 * rest_e.size * rows.size
-    most = run(f32, 1024, both, both_e, most_e, [here, left, right])
-    (for_there,) = run(bf16, work, both[:1], both_e[:1], rest_e, far, most[:1])
+    work = 8 * rest_e.size * rows.size
+    most = run((f32, f32), 1024, both, both_e, most_e, [here, near, off])
+    for_there, for_own = run((bf16, f32), work, both, both_e, rest_e, [far], most)
     arrived = lax.ppermute(for_there, "c", SWAP)
-    (for_own,) = run(f32, work, both[1:], both_e[1:], rest_e, far, most[1:])
     pair_sum = (for_own + arrived.astype(jnp.float32)).astype(jnp.bfloat16)
     shares = lax.all_to_all(pair_sum.reshape(ny, slab, depth), "y", 0, 0)
     density = jnp.sum(shares.astype(jnp.float32), axis=0)

time: 126 us -> 119 us (0.944)
  local copies, waits for them, and re-layouts: 7.2 us -> 3.04 us
  Pallas kernels: 9.14 us -> 7.34 us
  starting transfers between devices: 39.9 us -> 38.4 us
    slice x2 -> x0, local copies, waits for them, and re-layouts: 2.63 us -> none  [shards(): far_low, far_high = (shift(left[:nz // 2], 1), shift(right[nz // 2:], -1))]
    pallas_call x3 -> x2, Pallas kernels: 9.14 us -> 7.34 us  [run(): pl.pallas_call(lambda *refs: density_kernel(sides, blocks, len(befores) >...]
    ppermute x1, waiting for transfers between devices: 0.01 us -> 1.61 us  [shards(): arrived = lax.ppermute(for_there, 'c', SWAP)]
    ppermute x4 -> x3, starting transfers between devices: 13 us -> 11.4 us  [shift(): return lax.ppermute(block, ('h', 'l', 'c'), ring)]
    ppermute x1, starting transfers between devices: 4.44 us -> 5.77 us  [shards(): arrived = lax.ppermute(for_there, 'c', SWAP)]
    ppermute x1, starting transfers between devices: 10.2 us -> 8.89 us  [shards(): rows_there = lax.ppermute(rows, 'c', SWAP)]
  transfers between devices with their start and end apart: 8 -> 7, of which waited for: 2 -> 4; matrix products, arithmetic and copies ran while one was open for 5% -> 4% of each run, Pallas kernels for 5% -> 4%
where the time goes in v12:
time: 119 us; the launch traced here: 118 us
  blocking collectives  57.7 us (48%)
  starting transfers between devices  38.4 us (32%)
  waiting for transfers between devices  7.65 us (6%)
  Pallas kernels  7.34 us (6%)
  other arithmetic  3.54 us (3%)
  local copies, waits for them, and re-layouts  3.04 us (3%)
    all_gather x1, blocking collectives, shards(): lax.all_gather(wide.reshape(nz * slab, nh * part), 'z', axis=0, tiled=False)  32.5 us
    all_to_all x1, blocking collectives, shards(): shares = lax.all_to_all(pair_sum.reshape(ny, slab, depth), 'y', 0, 0)  25.2 us
    ppermute x3, starting transfers between devices, shift(): return lax.ppermute(block, ('h', 'l', 'c'), ring)  11.4 us
    ppermute x1, starting transfers between devices, shards(): rows_there = lax.ppermute(rows, 'c', SWAP)  8.89 us
    pallas_call x2, Pallas kernels, run(): pl.pallas_call(lambda *refs: density_kernel(sides, blocks, len(befores) >...  7.34 us
    all_to_all x1, starting transfers between devices, shards(): lax.all_to_all(jnp.broadcast_to(seeds[None], (ny, slab, depth)), 'y', 0, 0)  6.82 us
    ppermute x1, starting transfers between devices, shards(): arrived = lax.ppermute(for_there, 'c', SWAP)  5.77 us
    all_to_all x1, waiting for transfers between devices, shards(): lax.all_to_all(jnp.broadcast_to(seeds[None], (ny, slab, depth)), 'y', 0, 0)  5.59 us
  transfers between devices with their start and end apart: 7, of which 4 were waited for; matrix products, arithmetic and copies ran while one was open for 4% of the time, Pallas kernels for 4%

profile of v12, /device:TPU:1, one launch (start us, length us, event | category | flops | bytes accessed | tf_op | source)
XLA Modules:
  0.0 117.9 jit_solution(4227996114066352377)
XLA Ops:
  0.0 1.0 convert_element_type.18
  1.0 5.5 %collective-permute-start = (bf16[12,24,64]{2,1,0:T(8,128)(2,1)S(1)}, bf16[12,24,64]{2,1,0:T(8,128)(2,1)S(1)}, u32[]{:S(2)}, u32[]{:S(2)}) collective-permute-start(bf16[12,24,64]{2,1,0:T(8,128)(2,1)S(1)} %select_bitcast_fusion), channel_id=1, source_target_pairs={{0,32},{32,0},{1,33},{33,1},{2,34},{34,2},{3,35},{35,3},{4,36},{36... | collective-permute-start | bytes 110600 | tf_op jit(solution)/shard_map/ppermute | solution.py:78
  6.5 0.7 multiply_subtract_fusion
  7.2 0.1 slice.49
  7.3 0.1 slice.48
  7.4 0.7 multiply_add_fusion
  8.1 0.1 reshape.169
  8.2 0.1 broadcast_subtract_fusion
  8.3 0.1 sub.113
  8.4 0.1 sub.121
  8.5 0.1 sub.118
  8.6 0.1 pad_maximum_fusion.1.refs_0_
  8.7 0.1 sub.124.refs_0_
  8.8 0.0 collective-permute-done
  8.8 0.1 pad_maximum_fusion
  8.9 32.5 %all_gather.3.refs_5_ = bf16[12,288,128]{2,1,0:T(8,128)(2,1)S(1)} all-gather(bf16[1,288,128]{2,1,0:T(8,128)(2,1)S(1)} %bitcast.50), channel_id=1, replica_groups=mesh['z'=12,'h'=2,'l'=2,'y'=8,'c'=2] {'z'}, dimensions={0}, use_global_device_ids=true | all-gather | bytes 958464 | tf_op jit(solution)/shard_map/all_gather | solution.py:97
  41.4 4.5 %collective-permute-start.2 = (bf16[12,288,128]{2,1,0:T(8,128)(2,1)S(1)}, bf16[12,288,128]{2,1,0:T(8,128)(2,1)S(1)}, u32[]{:S(2)}, u32[]{:S(2)}) collective-permute-start(bf16[12,288,128]{2,1,0:T(8,128)(2,1)S(1)} %all_gather.3.refs_5_), channel_id=1, source_target_pairs={{0,16},{16,32},{32,48},{48,0},{1,49},{17,1},{33,17},{49,33},{2,18}... | collective-permute-start | bytes 2654216 | tf_op jit(solution)/shard_map/ppermute | solution.py:103
  45.9 0.9 broadcast_in_dim.7
  46.8 6.8 %all-to-all-start = ((bf16[8,24,1536]{2,1,0:T(8,128)(2,1)}), bf16[8,24,1536]{2,1,0:T(8,128)(2,1)S(1)}, u32[]{:S(2)}, u32[]{:S(2)}) async-start(bf16[8,24,1536]{2,1,0:T(8,128)(2,1)} %broadcast_in_dim.7), calls=%async_computation | async-start | bytes 1179648 | tf_op jit(solution)/shard_map/all_to_all | solution.py:109
  53.6 1.9 %collective-permute-start.4 = (bf16[12,288,128]{2,1,0:T(8,128)(2,1)S(1)}, bf16[12,288,128]{2,1,0:T(8,128)(2,1)}, u32[]{:S(2)}, u32[]{:S(2)}) collective-permute-start(bf16[12,288,128]{2,1,0:T(8,128)(2,1)S(1)} %all_gather.3.refs_5_), channel_id=1, source_target_pairs={{0,48},{16,0},{32,16},{48,32},{1,17},{17,33},{33,49},{49,1},{2,50}... | collective-permute-start | bytes 2654216 | tf_op jit(solution)/shard_map/ppermute | solution.py:103
  55.5 0.3 collective-permute-done.2.refs_6_
  55.8 5.0 %collective-permute-start.3 = (bf16[12,288,128]{2,1,0:T(8,128)(2,1)S(1)}, bf16[12,288,128]{2,1,0:T(8,128)(2,1)}, u32[]{:S(2)}, u32[]{:S(2)}) collective-permute-start(bf16[12,288,128]{2,1,0:T(8,128)(2,1)S(1)} %collective-permute-done.2.refs_6_), channel_id=1, source_target_pairs={{0,16},{16,32},{32,48},{48,0},{1,49},{17,1},{33,17},{49,33},{2,18}... | collective-permute-start | bytes 2654216 | tf_op jit(solution)/shard_map/ppermute | solution.py:103
  60.8 5.6 %all-to-all-done = bf16[8,24,1536]{2,1,0:T(8,128)(2,1)S(1)} async-done(((bf16[8,24,1536]{2,1,0:T(8,128)(2,1)}), bf16[8,24,1536]{2,1,0:T(8,128)(2,1)S(1)}, u32[]{:S(2)}, u32[]{:S(2)}) %all-to-all-start) | async-done | bytes 589856 | tf_op jit(solution)/shard_map/all_to_all | solution.py:109
  66.4 8.9 %collective-permute-start.1 = (bf16[192,1536]{1,0:T(8,128)(2,1)S(1)}, bf16[192,1536]{1,0:T(8,128)(2,1)S(1)}, u32[]{:S(2)}, u32[]{:S(2)}) collective-permute-start(bf16[192,1536]{1,0:T(8,128)(2,1)S(1)} %bitcast.44), channel_id=1, source_target_pairs={{0,1},{1,0},{2,3},{3,2},{4,5},{5,4},{6,7},{7,6},{8,9},{9,8},{10,11... | collective-permute-start | bytes 1769480 | tf_op jit(solution)/shard_map/ppermute | solution.py:112
  75.3 0.6 dynamic_slice.11
  75.9 0.7 subtract_bitcast_fusion
  76.6 0.1 select_n.161.refs_4_
  76.7 0.1 select_n.160.refs_3_
  76.8 0.0 collective-permute-done.4.refs_7_
  76.8 0.1 collective-permute-done.1.refs_1_
  76.9 4.5 %shard_map.37 = (f32[192,1536]{1,0:T(8,128)S(1)}, f32[192,1536]{1,0:T(8,128)S(1)}) custom-call(f32[1,864]{1,0:T(1,128)S(1)} %pad_maximum_fusion.1.refs_0_, bf16[192,1536]{1,0:T(8,128)(2,1)S(1)} %collective-permute-done.1.refs_1_, bf16[192,1536]{1,0:T(8,128)(2,1)S(1)} %bitcast.45, f32[192,1]{1,0:T(8,128)S(1)} %select_n.160.refs_3_, ...), custom_call_target="tpu_custom_call" | custom-call | flops 1024 | bytes 4 | tf_op jit(solution)/shard_map/pallas_call | solution.py:55
  81.5 0.0 collective-permute-done.3.refs_5_
  81.5 2.8 %shard_map.38 = (bf16[192,1536]{1,0:T(8,128)(2,1)S(1)}, f32[192,1536]{1,0:T(8,128)S(1)}) custom-call(f32[1,288]{1,0:T(1,128)S(1)} %sub.124.refs_0_, bf16[192,1536]{1,0:T(8,128)(2,1)S(1)} %collective-permute-done.1.refs_1_, bf16[192,1536]{1,0:T(8,128)(2,1)S(1)} %bitcast.46, f32[192,1]{1,0:T(8,128)S(1)} %select_n.160.refs_3_, f32[192,1]{1,0:T(8,128)S(1)} %select_n.161.refs_4_, ...), custom_call_target="tpu_custom_call" | custom-call | flops 679477248 | bytes 2654208 | tf_op jit(solution)/shard_map/pallas_call | solution.py:55
  84.3 5.8 %collective-permute-start.5 = (bf16[192,1536]{1,0:T(8,128)(2,1)S(1)}, bf16[192,1536]{1,0:T(8,128)(2,1)S(1)}, u32[]{:S(2)}, u32[]{:S(2)}) collective-permute-start(bf16[192,1536]{1,0:T(8,128)(2,1)S(1)} %get-tuple-element.24), channel_id=1, source_target_pairs={{0,1},{1,0},{2,3},{3,2},{4,5},{5,4},{6,7},{7,6},{8,9},{9,8},{10,11... | collective-permute-start | bytes 1769480 | tf_op jit(solution)/shard_map/ppermute | solution.py:123
  90.1 1.6 %collective-permute-done.5 = bf16[192,1536]{1,0:T(8,128)(2,1)S(1)} collective-permute-done((bf16[192,1536]{1,0:T(8,128)(2,1)S(1)}, bf16[192,1536]{1,0:T(8,128)(2,1)S(1)}, u32[]{:S(2)}, u32[]{:S(2)}) %collective-permute-start.5) | collective-permute-done | bytes 589856 | tf_op jit(solution)/shard_map/ppermute | solution.py:123
  91.7 0.1 add_convert_fusion
  91.8 25.2 %all_to_all.10 = bf16[8,24,1536]{2,1,0:T(8,128)(2,1)S(1)} all-to-all(bf16[8,24,1536]{2,1,0:T(8,128)(2,1)S(1)} %bitcast.47), channel_id=1, replica_groups=mesh['z'=12,'h'=2,'l'=2,'y'=8,'c'=2] {'y'}, dimensions={0} | all-to-all | bytes 1179648 | tf_op jit(solution)/shard_map/all_to_all | solution.py:125
  117.0 0.1 convert_reduce_fusion
  117.1 0.8 broadcast_in_dim.8
  (8 shorter events, 0.1 us)
Async XLA Ops:
  1.0 7.7 %collective-permute-start = (bf16[12,24,64]{2,1,0:T(8,128)(2,1)S(1)}, bf16[12,24,64]{2,1,0:T(8,128)(2,1)S(1)}, u32[]{:S(2)}, u32[]{:S(2)}) collective-permute-start(bf16[12,24,64]{2,1,0:T(8,128)(2,1)S(1)} %select_bitcast_fusion), channel_id=1, source_target_pairs={{0,32},{32,0},{1,33},{33,1},{2,34},{34,2},{3,35},{35,3},{4,36},{36... | collective-permute-start | bytes 110600 | tf_op jit(solution)/shard_map/ppermute | solution.py:78
  41.4 14.4 %collective-permute-start.2 = (bf16[12,288,128]{2,1,0:T(8,128)(2,1)S(1)}, bf16[12,288,128]{2,1,0:T(8,128)(2,1)S(1)}, u32[]{:S(2)}, u32[]{:S(2)}) collective-permute-start(bf16[12,288,128]{2,1,0:T(8,128)(2,1)S(1)} %all_gather.3.refs_5_), channel_id=1, source_target_pairs={{0,16},{16,32},{32,48},{48,0},{1,49},{17,1},{33,17},{49,33},{2,18}... | collective-permute-start | bytes 2654216 | tf_op jit(solution)/shard_map/ppermute | solution.py:103
  46.8 19.7 %all-to-all-start = ((bf16[8,24,1536]{2,1,0:T(8,128)(2,1)}), bf16[8,24,1536]{2,1,0:T(8,128)(2,1)S(1)}, u32[]{:S(2)}, u32[]{:S(2)}) async-start(bf16[8,24,1536]{2,1,0:T(8,128)(2,1)} %broadcast_in_dim.7), calls=%async_computation | async-start | bytes 1179648 | tf_op jit(solution)/shard_map/all_to_all | solution.py:109
  53.6 23.2 %collective-permute-start.4 = (bf16[12,288,128]{2,1,0:T(8,128)(2,1)S(1)}, bf16[12,288,128]{2,1,0:T(8,128)(2,1)}, u32[]{:S(2)}, u32[]{:S(2)}) collective-permute-start(bf16[12,288,128]{2,1,0:T(8,128)(2,1)S(1)} %all_gather.3.refs_5_), channel_id=1, source_target_pairs={{0,48},{16,0},{32,16},{48,32},{1,17},{17,33},{33,49},{49,1},{2,50}... | collective-permute-start | bytes 2654216 | tf_op jit(solution)/shard_map/ppermute | solution.py:103
  55.8 25.6 %collective-permute-start.3 = (bf16[12,288,128]{2,1,0:T(8,128)(2,1)S(1)}, bf16[12,288,128]{2,1,0:T(8,128)(2,1)}, u32[]{:S(2)}, u32[]{:S(2)}) collective-permute-start(bf16[12,288,128]{2,1,0:T(8,128)(2,1)S(1)} %collective-permute-done.2.refs_6_), channel_id=1, source_target_pairs={{0,16},{16,32},{32,48},{48,0},{1,49},{17,1},{33,17},{49,33},{2,18}... | collective-permute-start | bytes 2654216 | tf_op jit(solution)/shard_map/ppermute | solution.py:103
  66.4 10.5 %collective-permute-start.1 = (bf16[192,1536]{1,0:T(8,128)(2,1)S(1)}, bf16[192,1536]{1,0:T(8,128)(2,1)S(1)}, u32[]{:S(2)}, u32[]{:S(2)}) collective-permute-start(bf16[192,1536]{1,0:T(8,128)(2,1)S(1)} %bitcast.44), channel_id=1, source_target_pairs={{0,1},{1,0},{2,3},{3,2},{4,5},{5,4},{6,7},{7,6},{8,9},{9,8},{10,11... | collective-permute-start | bytes 1769480 | tf_op jit(solution)/shard_map/ppermute | solution.py:112
  84.3 7.4 %collective-permute-start.5 = (bf16[192,1536]{1,0:T(8,128)(2,1)S(1)}, bf16[192,1536]{1,0:T(8,128)(2,1)S(1)}, u32[]{:S(2)}, u32[]{:S(2)}) collective-permute-start(bf16[192,1536]{1,0:T(8,128)(2,1)S(1)} %get-tuple-element.24), channel_id=1, source_target_pairs={{0,1},{1,0},{2,3},{3,2},{4,5},{5,4},{6,7},{7,6},{8,9},{9,8},{10,11... | collective-permute-start | bytes 1769480 | tf_op jit(solution)/shard_map/ppermute | solution.py:123

commit v13 on v12

--- a/solution.py
+++ b/solution.py
@@ -91,9 +91,10 @@
         return (low[None, :] - jnp.where(is_even, evens, odds)[:, None]).reshape(1, -1)
 
     near_even = (h != l) == core0
-    most_e = [col_e(low_own, h == 0), col_e(low_other, near_even), col_e(low_other, ~near_even)]
-    rest_e = col_e(low_own, h != 0)
-    wide, most_e, rest_e = lax.optimization_barrier((wide, jnp.concatenate(most_e, axis=1), rest_e))
+    most_e = [col_e(low_own, h == 0), col_e(low_other, near_even)]
+    rest_e = [col_e(low_other, ~near_even), col_e(low_own, h != 0)]
+    most_e, rest_e = jnp.concatenate(most_e, axis=1), jnp.concatenate(rest_e, axis=1)
+    wide, most_e, rest_e = lax.optimization_barrier((wide, most_e, rest_e))
     here = lax.all_gather(wide.reshape(nz * slab, nh * part), "z", axis=0, tiled=False)
 
     def shift(block, by):
@@ -118,8 +119,8 @@
     f32, bf16 = jnp.float32, jnp.bfloat16
     both, both_e = [rows_there, rows], [there_e, own_e]
     work = 8 * rest_e.size * rows.size
-    most = run((f32, f32), 1024, both, both_e, most_e, [here, near, off])
-    for_there, for_own = run((bf16, f32), work, both, both_e, rest_e, [far], most)
+    most = run((f32, f32), 1024, both, both_e, most_e, [here, near])
+    for_there, for_own = run((bf16, f32), work, both, both_e, rest_e, [off, far], most)
     arrived = lax.ppermute(for_there, "c", SWAP)
     pair_sum = (for_own + arrived.astype(jnp.float32)).astype(jnp.bfloat16)
     shares = lax.all_to_all(pair_sum.reshape(ny, slab, depth), "y", 0, 0)

time: 119 us -> 120 us (level)
  starting transfers between devices: 38.4 us -> 39.6 us
    ppermute x1, starting transfers between devices: 5.77 us -> 7.13 us  [shards(): arrived = lax.ppermute(for_there, 'c', SWAP)]
  transfers between devices with their start and end apart: 7 -> 7, of which waited for: 4 -> 4; matrix products, arithmetic and copies ran while one was open for 4% -> 4% of each run, Pallas kernels for 4% -> 3%
where the time goes in v13:
time: 120 us; the launch traced here: 119 us
  blocking collectives  57.7 us (48%)
  starting transfers between devices  39.6 us (33%)
  waiting for transfers between devices  7.66 us (6%)
  Pallas kernels  7.25 us (6%)
  other arithmetic  3.61 us (3%)
  local copies, waits for them, and re-layouts  3.04 us (3%)
    all_gather x1, blocking collectives, shards(): lax.all_gather(wide.reshape(nz * slab, nh * part), 'z', axis=0, tiled=False)  32.5 us
    all_to_all x1, blocking collectives, shards(): shares = lax.all_to_all(pair_sum.reshape(ny, slab, depth), 'y', 0, 0)  25.2 us
    ppermute x3, starting transfers between devices, shift(): return lax.ppermute(block, ('h', 'l', 'c'), ring)  11.3 us
    ppermute x1, starting transfers between devices, shards(): rows_there = lax.ppermute(rows, 'c', SWAP)  8.89 us
    pallas_call x2, Pallas kernels, run(): pl.pallas_call(lambda *refs: density_kernel(sides, blocks, len(befores) >...  7.25 us
    ppermute x1, starting transfers between devices, shards(): arrived = lax.ppermute(for_there, 'c', SWAP)  7.13 us
    all_to_all x1, starting transfers between devices, shards(): lax.all_to_all(jnp.broadcast_to(seeds[None], (ny, slab, depth)), 'y', 0, 0)  6.82 us
    all_to_all x1, waiting for transfers between devices, shards(): lax.all_to_all(jnp.broadcast_to(seeds[None], (ny, slab, depth)), 'y', 0, 0)  5.59 us
  transfers between devices with their start and end apart: 7, of which 4 were waited for; matrix products, arithmetic and copies ran while one was open for 4% of the time, Pallas kernels for 3%

profile of v13, /device:TPU:1, one launch (start us, length us, event | category | flops | bytes accessed | tf_op | source)
XLA Modules:
  0.0 119.2 jit_solution(14904836817212682297)
XLA Ops:
  0.0 1.0 convert_element_type.18
  1.0 5.5 %collective-permute-start = (bf16[12,24,64]{2,1,0:T(8,128)(2,1)S(1)}, bf16[12,24,64]{2,1,0:T(8,128)(2,1)S(1)}, u32[]{:S(2)}, u32[]{:S(2)}) collective-permute-start(bf16[12,24,64]{2,1,0:T(8,128)(2,1)S(1)} %select_bitcast_fusion), channel_id=1, source_target_pairs={{0,32},{32,0},{1,33},{33,1},{2,34},{34,2},{3,35},{35,3},{4,36},{36... | collective-permute-start | bytes 110600 | tf_op jit(solution)/shard_map/ppermute | solution.py:78
  6.5 0.7 multiply_subtract_fusion
  7.2 0.1 slice.48
  7.3 0.1 slice.49
  7.4 0.7 multiply_add_fusion
  8.1 0.1 reshape.169
  8.2 0.1 broadcast_subtract_fusion
  8.3 0.1 sub.113
  8.4 0.1 sub.118
  8.5 0.1 sub.121
  8.6 0.1 sub.124
  8.7 0.1 pad_maximum_fusion.1.refs_0_
  8.7 0.1 pad_maximum_fusion.2.refs_0_
  8.8 0.0 collective-permute-done
  8.8 0.1 pad_maximum_fusion
  8.9 32.5 %all_gather.3.refs_5_ = bf16[12,288,128]{2,1,0:T(8,128)(2,1)S(1)} all-gather(bf16[1,288,128]{2,1,0:T(8,128)(2,1)S(1)} %bitcast.50), channel_id=1, replica_groups=mesh['z'=12,'h'=2,'l'=2,'y'=8,'c'=2] {'z'}, dimensions={0}, use_global_device_ids=true | all-gather | bytes 958464 | tf_op jit(solution)/shard_map/all_gather | solution.py:98
  41.5 4.4 %collective-permute-start.3 = (bf16[12,288,128]{2,1,0:T(8,128)(2,1)S(1)}, bf16[12,288,128]{2,1,0:T(8,128)(2,1)S(1)}, u32[]{:S(2)}, u32[]{:S(2)}) collective-permute-start(bf16[12,288,128]{2,1,0:T(8,128)(2,1)S(1)} %all_gather.3.refs_5_), channel_id=1, source_target_pairs={{0,16},{16,32},{32,48},{48,0},{1,49},{17,1},{33,17},{49,33},{2,18}... | collective-permute-start | bytes 2654216 | tf_op jit(solution)/shard_map/ppermute | solution.py:104
  45.9 0.9 broadcast_in_dim.7
  46.8 6.8 %all-to-all-start = ((bf16[8,24,1536]{2,1,0:T(8,128)(2,1)}), bf16[8,24,1536]{2,1,0:T(8,128)(2,1)S(1)}, u32[]{:S(2)}, u32[]{:S(2)}) async-start(bf16[8,24,1536]{2,1,0:T(8,128)(2,1)} %broadcast_in_dim.7), calls=%async_computation | async-start | bytes 1179648 | tf_op jit(solution)/shard_map/all_to_all | solution.py:110
  53.6 1.9 %collective-permute-start.2 = (bf16[12,288,128]{2,1,0:T(8,128)(2,1)S(1)}, bf16[12,288,128]{2,1,0:T(8,128)(2,1)}, u32[]{:S(2)}, u32[]{:S(2)}) collective-permute-start(bf16[12,288,128]{2,1,0:T(8,128)(2,1)S(1)} %all_gather.3.refs_5_), channel_id=1, source_target_pairs={{0,48},{16,0},{32,16},{48,32},{1,17},{17,33},{33,49},{49,1},{2,50}... | collective-permute-start | bytes 2654216 | tf_op jit(solution)/shard_map/ppermute | solution.py:104
  55.5 0.3 collective-permute-done.3.refs_6_
  55.8 5.0 %collective-permute-start.4 = (bf16[12,288,128]{2,1,0:T(8,128)(2,1)S(1)}, bf16[12,288,128]{2,1,0:T(8,128)(2,1)}, u32[]{:S(2)}, u32[]{:S(2)}) collective-permute-start(bf16[12,288,128]{2,1,0:T(8,128)(2,1)S(1)} %collective-permute-done.3.refs_6_), channel_id=1, source_target_pairs={{0,16},{16,32},{32,48},{48,0},{1,49},{17,1},{33,17},{49,33},{2,18}... | collective-permute-start | bytes 2654216 | tf_op jit(solution)/shard_map/ppermute | solution.py:104
  60.8 5.6 %all-to-all-done = bf16[8,24,1536]{2,1,0:T(8,128)(2,1)S(1)} async-done(((bf16[8,24,1536]{2,1,0:T(8,128)(2,1)}), bf16[8,24,1536]{2,1,0:T(8,128)(2,1)S(1)}, u32[]{:S(2)}, u32[]{:S(2)}) %all-to-all-start) | async-done | bytes 589856 | tf_op jit(solution)/shard_map/all_to_all | solution.py:110
  66.4 8.9 %collective-permute-start.1 = (bf16[192,1536]{1,0:T(8,128)(2,1)S(1)}, bf16[192,1536]{1,0:T(8,128)(2,1)S(1)}, u32[]{:S(2)}, u32[]{:S(2)}) collective-permute-start(bf16[192,1536]{1,0:T(8,128)(2,1)S(1)} %bitcast.44), channel_id=1, source_target_pairs={{0,1},{1,0},{2,3},{3,2},{4,5},{5,4},{6,7},{7,6},{8,9},{9,8},{10,11... | collective-permute-start | bytes 1769480 | tf_op jit(solution)/shard_map/ppermute | solution.py:113
  75.3 0.6 dynamic_slice.11
  75.9 0.7 subtract_bitcast_fusion
  76.6 0.1 select_n.160.refs_3_
  76.7 0.1 select_n.161.refs_4_
  76.8 0.1 collective-permute-done.1.refs_1_
  76.9 3.0 %shard_map.37 = (f32[192,1536]{1,0:T(8,128)S(1)}, f32[192,1536]{1,0:T(8,128)S(1)}) custom-call(f32[1,576]{1,0:T(1,128)S(1)} %pad_maximum_fusion.1.refs_0_, bf16[192,1536]{1,0:T(8,128)(2,1)S(1)} %collective-permute-done.1.refs_1_, bf16[192,1536]{1,0:T(8,128)(2,1)S(1)} %bitcast.45, f32[192,1]{1,0:T(8,128)S(1)} %select_n.160.refs_3_, ...), custom_call_target="tpu_custom_call" | custom-call | flops 1024 | bytes 4 | tf_op jit(solution)/shard_map/pallas_call | solution.py:55
  80.0 0.0 collective-permute-done.2.refs_5_
  80.0 0.0 collective-permute-done.4.refs_6_
  80.0 4.2 %shard_map.38 = (bf16[192,1536]{1,0:T(8,128)(2,1)S(1)}, f32[192,1536]{1,0:T(8,128)S(1)}) custom-call(f32[1,576]{1,0:T(1,128)S(1)} %pad_maximum_fusion.2.refs_0_, bf16[192,1536]{1,0:T(8,128)(2,1)S(1)} %collective-permute-done.1.refs_1_, bf16[192,1536]{1,0:T(8,128)(2,1)S(1)} %bitcast.46, f32[192,1]{1,0:T(8,128)S(1)} %select_n.160.refs_3_, ...), custom_call_target="tpu_custom_call" | custom-call | flops 1358954496 | bytes 5308416 | tf_op jit(solution)/shard_map/pallas_call | solution.py:55
  84.2 7.1 %collective-permute-start.5 = (bf16[192,1536]{1,0:T(8,128)(2,1)S(1)}, bf16[192,1536]{1,0:T(8,128)(2,1)S(1)}, u32[]{:S(2)}, u32[]{:S(2)}) collective-permute-start(bf16[192,1536]{1,0:T(8,128)(2,1)S(1)} %get-tuple-element.24), channel_id=1, source_target_pairs={{0,1},{1,0},{2,3},{3,2},{4,5},{5,4},{6,7},{7,6},{8,9},{9,8},{10,11... | collective-permute-start | bytes 1769480 | tf_op jit(solution)/shard_map/ppermute | solution.py:124
  91.4 1.6 %collective-permute-done.5 = bf16[192,1536]{1,0:T(8,128)(2,1)S(1)} collective-permute-done((bf16[192,1536]{1,0:T(8,128)(2,1)S(1)}, bf16[192,1536]{1,0:T(8,128)(2,1)S(1)}, u32[]{:S(2)}, u32[]{:S(2)}) %collective-permute-start.5) | collective-permute-done | bytes 589856 | tf_op jit(solution)/shard_map/ppermute | solution.py:124
  93.0 0.1 add_convert_fusion
  93.1 25.2 %all_to_all.10 = bf16[8,24,1536]{2,1,0:T(8,128)(2,1)S(1)} all-to-all(bf16[8,24,1536]{2,1,0:T(8,128)(2,1)S(1)} %bitcast.47), channel_id=1, replica_groups=mesh['z'=12,'h'=2,'l'=2,'y'=8,'c'=2] {'y'}, dimensions={0} | all-to-all | bytes 1179648 | tf_op jit(solution)/shard_map/all_to_all | solution.py:126
  118.3 0.1 convert_reduce_fusion
  118.4 0.8 broadcast_in_dim.8
  (8 shorter events, 0.1 us)
Async XLA Ops:
  1.0 7.8 %collective-permute-start = (bf16[12,24,64]{2,1,0:T(8,128)(2,1)S(1)}, bf16[12,24,64]{2,1,0:T(8,128)(2,1)S(1)}, u32[]{:S(2)}, u32[]{:S(2)}) collective-permute-start(bf16[12,24,64]{2,1,0:T(8,128)(2,1)S(1)} %select_bitcast_fusion), channel_id=1, source_target_pairs={{0,32},{32,0},{1,33},{33,1},{2,34},{34,2},{3,35},{35,3},{4,36},{36... | collective-permute-start | bytes 110600 | tf_op jit(solution)/shard_map/ppermute | solution.py:78
  41.5 14.4 %collective-permute-start.3 = (bf16[12,288,128]{2,1,0:T(8,128)(2,1)S(1)}, bf16[12,288,128]{2,1,0:T(8,128)(2,1)S(1)}, u32[]{:S(2)}, u32[]{:S(2)}) collective-permute-start(bf16[12,288,128]{2,1,0:T(8,128)(2,1)S(1)} %all_gather.3.refs_5_), channel_id=1, source_target_pairs={{0,16},{16,32},{32,48},{48,0},{1,49},{17,1},{33,17},{49,33},{2,18}... | collective-permute-start | bytes 2654216 | tf_op jit(solution)/shard_map/ppermute | solution.py:104
  46.8 19.7 %all-to-all-start = ((bf16[8,24,1536]{2,1,0:T(8,128)(2,1)}), bf16[8,24,1536]{2,1,0:T(8,128)(2,1)S(1)}, u32[]{:S(2)}, u32[]{:S(2)}) async-start(bf16[8,24,1536]{2,1,0:T(8,128)(2,1)} %broadcast_in_dim.7), calls=%async_computation | async-start | bytes 1179648 | tf_op jit(solution)/shard_map/all_to_all | solution.py:110
  53.6 26.4 %collective-permute-start.2 = (bf16[12,288,128]{2,1,0:T(8,128)(2,1)S(1)}, bf16[12,288,128]{2,1,0:T(8,128)(2,1)}, u32[]{:S(2)}, u32[]{:S(2)}) collective-permute-start(bf16[12,288,128]{2,1,0:T(8,128)(2,1)S(1)} %all_gather.3.refs_5_), channel_id=1, source_target_pairs={{0,48},{16,0},{32,16},{48,32},{1,17},{17,33},{33,49},{49,1},{2,50}... | collective-permute-start | bytes 2654216 | tf_op jit(solution)/shard_map/ppermute | solution.py:104
  55.8 24.2 %collective-permute-start.4 = (bf16[12,288,128]{2,1,0:T(8,128)(2,1)S(1)}, bf16[12,288,128]{2,1,0:T(8,128)(2,1)}, u32[]{:S(2)}, u32[]{:S(2)}) collective-permute-start(bf16[12,288,128]{2,1,0:T(8,128)(2,1)S(1)} %collective-permute-done.3.refs_6_), channel_id=1, source_target_pairs={{0,16},{16,32},{32,48},{48,0},{1,49},{17,1},{33,17},{49,33},{2,18}... | collective-permute-start | bytes 2654216 | tf_op jit(solution)/shard_map/ppermute | solution.py:104
  66.4 10.5 %collective-permute-start.1 = (bf16[192,1536]{1,0:T(8,128)(2,1)S(1)}, bf16[192,1536]{1,0:T(8,128)(2,1)S(1)}, u32[]{:S(2)}, u32[]{:S(2)}) collective-permute-start(bf16[192,1536]{1,0:T(8,128)(2,1)S(1)} %bitcast.44), channel_id=1, source_target_pairs={{0,1},{1,0},{2,3},{3,2},{4,5},{5,4},{6,7},{7,6},{8,9},{9,8},{10,11... | collective-permute-start | bytes 1769480 | tf_op jit(solution)/shard_map/ppermute | solution.py:113
  84.2 8.7 %collective-permute-start.5 = (bf16[192,1536]{1,0:T(8,128)(2,1)S(1)}, bf16[192,1536]{1,0:T(8,128)(2,1)S(1)}, u32[]{:S(2)}, u32[]{:S(2)}) collective-permute-start(bf16[192,1536]{1,0:T(8,128)(2,1)S(1)} %get-tuple-element.24), channel_id=1, source_target_pairs={{0,1},{1,0},{2,3},{3,2},{4,5},{5,4},{6,7},{7,6},{8,9},{9,8},{10,11... | collective-permute-start | bytes 1769480 | tf_op jit(solution)/shard_map/ppermute | solution.py:124

commit v14 on v12

--- a/solution.py
+++ b/solution.py
@@ -103,6 +103,7 @@
         return lax.ppermute(block, ("h", "l", "c"), ring)
 
     near, off = shift(here, 1), shift(here, -1)
+    near, off = lax.optimization_barrier((near, off))
     far = shift(near, 1)
     seeds = lax.dynamic_slice_in_dim(here, z * slab, slab, 1)
     seeds = jnp.transpose(seeds, (1, 0, 2)).reshape(slab, depth)

time: 119 us -> 118 us (level)
  waiting for transfers between devices: 7.65 us -> 11 us
  starting transfers between devices: 38.4 us -> 35.1 us
    ppermute x3, waiting for transfers between devices: 0.34 us -> 8.4 us  [shift(): return lax.ppermute(block, ('h', 'l', 'c'), ring)]
    all_to_all x1, waiting for transfers between devices: 5.59 us -> 0.83 us  [shards(): lax.all_to_all(jnp.broadcast_to(seeds[None], (ny, slab, depth)), 'y', 0, 0)]
    ppermute x1, starting transfers between devices: 5.77 us -> 2.79 us  [shards(): arrived = lax.ppermute(for_there, 'c', SWAP)]
    ppermute x3, starting transfers between devices: 11.4 us -> 10.2 us  [shift(): return lax.ppermute(block, ('h', 'l', 'c'), ring)]
  transfers between devices with their start and end apart: 7 -> 7, of which waited for: 4 -> 5; matrix products, arithmetic and copies ran while one was open for 4% -> 4% of each run, Pallas kernels for 4% -> 4%
where the time goes in v14:
time: 118 us
  blocking collectives  57.5 us (49%)
  starting transfers between devices  35.1 us (30%)
  waiting for transfers between devices  11 us (9%)
  Pallas kernels  7.21 us (6%)
  other arithmetic  3.54 us (3%)
  local copies, waits for them, and re-layouts  3.04 us (3%)
    all_gather x1, blocking collectives, shards(): lax.all_gather(wide.reshape(nz * slab, nh * part), 'z', axis=0, tiled=False)  32.5 us
    all_to_all x1, blocking collectives, shards(): shares = lax.all_to_all(pair_sum.reshape(ny, slab, depth), 'y', 0, 0)  25 us
    ppermute x3, starting transfers between devices, shift(): return lax.ppermute(block, ('h', 'l', 'c'), ring)  10.2 us
    ppermute x1, starting transfers between devices, shards(): rows_there = lax.ppermute(rows, 'c', SWAP)  9.83 us
    ppermute x3, waiting for transfers between devices, shift(): return lax.ppermute(block, ('h', 'l', 'c'), ring)  8.4 us
    pallas_call x2, Pallas kernels, run(): pl.pallas_call(lambda *refs: density_kernel(sides, blocks, len(befores) >...  7.21 us
    all_to_all x1, starting transfers between devices, shards(): lax.all_to_all(jnp.broadcast_to(seeds[None], (ny, slab, depth)), 'y', 0, 0)  6.82 us
    ppermute x1, starting transfers between devices, shards(): there = lax.ppermute(jnp.where(first, odd, even), 'h', SWAP)  5.48 us
  transfers between devices with their start and end apart: 7, of which 5 were waited for; matrix products, arithmetic and copies ran while one was open for 4% of the time, Pallas kernels for 4%

profile of v14, /device:TPU:1, one launch (start us, length us, event | category | flops | bytes accessed | tf_op | source)
XLA Modules:
  0.0 117.6 jit_solution(1570974778365663148)
XLA Ops:
  0.0 1.0 convert_element_type.18
  1.0 5.5 %collective-permute-start = (bf16[12,24,64]{2,1,0:T(8,128)(2,1)S(1)}, bf16[12,24,64]{2,1,0:T(8,128)(2,1)S(1)}, u32[]{:S(2)}, u32[]{:S(2)}) collective-permute-start(bf16[12,24,64]{2,1,0:T(8,128)(2,1)S(1)} %select_bitcast_fusion), channel_id=1, source_target_pairs={{0,32},{32,0},{1,33},{33,1},{2,34},{34,2},{3,35},{35,3},{4,36},{36... | collective-permute-start | bytes 110600 | tf_op jit(solution)/shard_map/ppermute | solution.py:78
  6.5 0.7 multiply_subtract_fusion
  7.2 0.1 slice.49
  7.3 0.1 slice.48
  7.4 0.7 multiply_add_fusion
  8.1 0.1 reshape.169
  8.2 0.1 broadcast_subtract_fusion
  8.3 0.1 sub.113
  8.4 0.1 sub.121
  8.5 0.1 sub.118
  8.6 0.1 pad_maximum_fusion.1.refs_0_
  8.7 0.1 sub.124.refs_0_
  8.8 0.0 collective-permute-done
  8.8 0.1 pad_maximum_fusion
  8.9 32.5 %all_gather.3.refs_5_ = bf16[12,288,128]{2,1,0:T(8,128)(2,1)S(1)} all-gather(bf16[1,288,128]{2,1,0:T(8,128)(2,1)S(1)} %bitcast.50), channel_id=1, replica_groups=mesh['z'=12,'h'=2,'l'=2,'y'=8,'c'=2] {'z'}, dimensions={0}, use_global_device_ids=true | all-gather | bytes 958464 | tf_op jit(solution)/shard_map/all_gather | solution.py:97
  41.4 3.2 %collective-permute-start.3 = (bf16[12,288,128]{2,1,0:T(8,128)(2,1)S(1)}, bf16[12,288,128]{2,1,0:T(8,128)(2,1)S(1)}, u32[]{:S(2)}, u32[]{:S(2)}) collective-permute-start(bf16[12,288,128]{2,1,0:T(8,128)(2,1)S(1)} %all_gather.3.refs_5_), channel_id=1, source_target_pairs={{0,48},{16,0},{32,16},{48,32},{1,17},{17,33},{33,49},{49,1},{2,50}... | collective-permute-start | bytes 2654216 | tf_op jit(solution)/shard_map/ppermute | solution.py:103
  44.6 3.3 %collective-permute-start.2 = (bf16[12,288,128]{2,1,0:T(8,128)(2,1)S(1)}, bf16[12,288,128]{2,1,0:T(8,128)(2,1)}, u32[]{:S(2)}, u32[]{:S(2)}) collective-permute-start(bf16[12,288,128]{2,1,0:T(8,128)(2,1)S(1)} %all_gather.3.refs_5_), channel_id=1, source_target_pairs={{0,16},{16,32},{32,48},{48,0},{1,49},{17,1},{33,17},{49,33},{2,18}... | collective-permute-start | bytes 2654216 | tf_op jit(solution)/shard_map/ppermute | solution.py:103
  47.9 0.9 broadcast_in_dim.7
  48.8 6.8 %all-to-all-start = ((bf16[8,24,1536]{2,1,0:T(8,128)(2,1)}), bf16[8,24,1536]{2,1,0:T(8,128)(2,1)S(1)}, u32[]{:S(2)}, u32[]{:S(2)}) async-start(bf16[8,24,1536]{2,1,0:T(8,128)(2,1)} %broadcast_in_dim.7), calls=%async_computation | async-start | bytes 1179648 | tf_op jit(solution)/shard_map/all_to_all | solution.py:110
  55.6 0.8 collective-permute-done.3.refs_7_
  56.4 7.6 %collective-permute-done.2.refs_6_ = bf16[12,288,128]{2,1,0:T(8,128)(2,1)} collective-permute-done((bf16[12,288,128]{2,1,0:T(8,128)(2,1)S(1)}, bf16[12,288,128]{2,1,0:T(8,128)(2,1)}, u32[]{:S(2)}, u32[]{:S(2)}) %collective-permute-start.2) | collective-permute-done | bytes 884768 | tf_op jit(solution)/shard_map/ppermute | solution.py:103
  64.0 3.7 %collective-permute-start.4 = (bf16[12,288,128]{2,1,0:T(8,128)(2,1)}, bf16[12,288,128]{2,1,0:T(8,128)(2,1)}, u32[]{:S(2)}, u32[]{:S(2)}) collective-permute-start(bf16[12,288,128]{2,1,0:T(8,128)(2,1)} %collective-permute-done.2.refs_6_), channel_id=1, source_target_pairs={{0,16},{16,32},{32,48},{48,0},{1,49},{17,1},{33,17},{49,33},{2,18}... | collective-permute-start | bytes 2654216 | tf_op jit(solution)/shard_map/ppermute | solution.py:103
  67.7 0.8 all-to-all-done
  68.5 9.8 %collective-permute-start.1 = (bf16[192,1536]{1,0:T(8,128)(2,1)S(1)}, bf16[192,1536]{1,0:T(8,128)(2,1)S(1)}, u32[]{:S(2)}, u32[]{:S(2)}) collective-permute-start(bf16[192,1536]{1,0:T(8,128)(2,1)S(1)} %bitcast.44), channel_id=1, source_target_pairs={{0,1},{1,0},{2,3},{3,2},{4,5},{5,4},{6,7},{7,6},{8,9},{9,8},{10,11... | collective-permute-start | bytes 1769480 | tf_op jit(solution)/shard_map/ppermute | solution.py:113
  78.4 0.6 dynamic_slice.11
  79.0 0.7 subtract_bitcast_fusion
  79.7 0.1 select_n.161.refs_4_
  79.8 0.1 select_n.160.refs_3_
  79.9 0.1 collective-permute-done.1.refs_1_
  80.0 4.4 %shard_map.37 = (f32[192,1536]{1,0:T(8,128)S(1)}, f32[192,1536]{1,0:T(8,128)S(1)}) custom-call(f32[1,864]{1,0:T(1,128)S(1)} %pad_maximum_fusion.1.refs_0_, bf16[192,1536]{1,0:T(8,128)(2,1)S(1)} %collective-permute-done.1.refs_1_, bf16[192,1536]{1,0:T(8,128)(2,1)S(1)} %bitcast.45, f32[192,1]{1,0:T(8,128)S(1)} %select_n.160.refs_3_, ...), custom_call_target="tpu_custom_call" | custom-call | flops 1024 | bytes 4 | tf_op jit(solution)/shard_map/pallas_call | solution.py:55
  84.4 0.0 collective-permute-done.4.refs_5_
  84.4 2.8 %shard_map.38 = (bf16[192,1536]{1,0:T(8,128)(2,1)S(1)}, f32[192,1536]{1,0:T(8,128)S(1)}) custom-call(f32[1,288]{1,0:T(1,128)S(1)} %sub.124.refs_0_, bf16[192,1536]{1,0:T(8,128)(2,1)S(1)} %collective-permute-done.1.refs_1_, bf16[192,1536]{1,0:T(8,128)(2,1)S(1)} %bitcast.46, f32[192,1]{1,0:T(8,128)S(1)} %select_n.160.refs_3_, f32[192,1]{1,0:T(8,128)S(1)} %select_n.161.refs_4_, ...), custom_call_target="tpu_custom_call" | custom-call | flops 679477248 | bytes 2654208 | tf_op jit(solution)/shard_map/pallas_call | solution.py:55
  87.2 2.8 %collective-permute-start.5 = (bf16[192,1536]{1,0:T(8,128)(2,1)S(1)}, bf16[192,1536]{1,0:T(8,128)(2,1)S(1)}, u32[]{:S(2)}, u32[]{:S(2)}) collective-permute-start(bf16[192,1536]{1,0:T(8,128)(2,1)S(1)} %get-tuple-element.28), channel_id=1, source_target_pairs={{0,1},{1,0},{2,3},{3,2},{4,5},{5,4},{6,7},{7,6},{8,9},{9,8},{10,11... | collective-permute-start | bytes 1769480 | tf_op jit(solution)/shard_map/ppermute | solution.py:124
  90.0 1.6 %collective-permute-done.5 = bf16[192,1536]{1,0:T(8,128)(2,1)S(1)} collective-permute-done((bf16[192,1536]{1,0:T(8,128)(2,1)S(1)}, bf16[192,1536]{1,0:T(8,128)(2,1)S(1)}, u32[]{:S(2)}, u32[]{:S(2)}) %collective-permute-start.5) | collective-permute-done | bytes 589856 | tf_op jit(solution)/shard_map/ppermute | solution.py:124
  91.6 0.1 add_convert_fusion
  91.8 25.0 %all_to_all.10 = bf16[8,24,1536]{2,1,0:T(8,128)(2,1)S(1)} all-to-all(bf16[8,24,1536]{2,1,0:T(8,128)(2,1)S(1)} %bitcast.47), channel_id=1, replica_groups=mesh['z'=12,'h'=2,'l'=2,'y'=8,'c'=2] {'y'}, dimensions={0} | all-to-all | bytes 1179648 | tf_op jit(solution)/shard_map/all_to_all | solution.py:126
  116.8 0.1 convert_reduce_fusion
  116.9 0.8 broadcast_in_dim.8
  (8 shorter events, 0.1 us)
Async XLA Ops:
  1.0 7.7 %collective-permute-start = (bf16[12,24,64]{2,1,0:T(8,128)(2,1)S(1)}, bf16[12,24,64]{2,1,0:T(8,128)(2,1)S(1)}, u32[]{:S(2)}, u32[]{:S(2)}) collective-permute-start(bf16[12,24,64]{2,1,0:T(8,128)(2,1)S(1)} %select_bitcast_fusion), channel_id=1, source_target_pairs={{0,32},{32,0},{1,33},{33,1},{2,34},{34,2},{3,35},{35,3},{4,36},{36... | collective-permute-start | bytes 110600 | tf_op jit(solution)/shard_map/ppermute | solution.py:78
  41.4 15.0 %collective-permute-start.3 = (bf16[12,288,128]{2,1,0:T(8,128)(2,1)S(1)}, bf16[12,288,128]{2,1,0:T(8,128)(2,1)S(1)}, u32[]{:S(2)}, u32[]{:S(2)}) collective-permute-start(bf16[12,288,128]{2,1,0:T(8,128)(2,1)S(1)} %all_gather.3.refs_5_), channel_id=1, source_target_pairs={{0,48},{16,0},{32,16},{48,32},{1,17},{17,33},{33,49},{49,1},{2,50}... | collective-permute-start | bytes 2654216 | tf_op jit(solution)/shard_map/ppermute | solution.py:103
  44.6 19.4 %collective-permute-start.2 = (bf16[12,288,128]{2,1,0:T(8,128)(2,1)S(1)}, bf16[12,288,128]{2,1,0:T(8,128)(2,1)}, u32[]{:S(2)}, u32[]{:S(2)}) collective-permute-start(bf16[12,288,128]{2,1,0:T(8,128)(2,1)S(1)} %all_gather.3.refs_5_), channel_id=1, source_target_pairs={{0,16},{16,32},{32,48},{48,0},{1,49},{17,1},{33,17},{49,33},{2,18}... | collective-permute-start | bytes 2654216 | tf_op jit(solution)/shard_map/ppermute | solution.py:103
  48.8 19.8 %all-to-all-start = ((bf16[8,24,1536]{2,1,0:T(8,128)(2,1)}), bf16[8,24,1536]{2,1,0:T(8,128)(2,1)S(1)}, u32[]{:S(2)}, u32[]{:S(2)}) async-start(bf16[8,24,1536]{2,1,0:T(8,128)(2,1)} %broadcast_in_dim.7), calls=%async_computation | async-start | bytes 1179648 | tf_op jit(solution)/shard_map/all_to_all | solution.py:110
  64.0 20.4 %collective-permute-start.4 = (bf16[12,288,128]{2,1,0:T(8,128)(2,1)}, bf16[12,288,128]{2,1,0:T(8,128)(2,1)}, u32[]{:S(2)}, u32[]{:S(2)}) collective-permute-start(bf16[12,288,128]{2,1,0:T(8,128)(2,1)} %collective-permute-done.2.refs_6_), channel_id=1, source_target_pairs={{0,16},{16,32},{32,48},{48,0},{1,49},{17,1},{33,17},{49,33},{2,18}... | collective-permute-start | bytes 2654216 | tf_op jit(solution)/shard_map/ppermute | solution.py:103
  68.5 11.5 %collective-permute-start.1 = (bf16[192,1536]{1,0:T(8,128)(2,1)S(1)}, bf16[192,1536]{1,0:T(8,128)(2,1)S(1)}, u32[]{:S(2)}, u32[]{:S(2)}) collective-permute-start(bf16[192,1536]{1,0:T(8,128)(2,1)S(1)} %bitcast.44), channel_id=1, source_target_pairs={{0,1},{1,0},{2,3},{3,2},{4,5},{5,4},{6,7},{7,6},{8,9},{9,8},{10,11... | collective-permute-start | bytes 1769480 | tf_op jit(solution)/shard_map/ppermute | solution.py:113
  87.2 4.4 %collective-permute-start.5 = (bf16[192,1536]{1,0:T(8,128)(2,1)S(1)}, bf16[192,1536]{1,0:T(8,128)(2,1)S(1)}, u32[]{:S(2)}, u32[]{:S(2)}) collective-permute-start(bf16[192,1536]{1,0:T(8,128)(2,1)S(1)} %get-tuple-element.28), channel_id=1, source_target_pairs={{0,1},{1,0},{2,3},{3,2},{4,5},{5,4},{6,7},{7,6},{8,9},{9,8},{10,11... | collective-permute-start | bytes 1769480 | tf_op jit(solution)/shard_map/ppermute | solution.py:124

commit v15 on v14

--- a/solution.py
+++ b/solution.py
@@ -31,13 +31,23 @@
             first, left = first + width, 0
     for copy in copies:
         copy.start()
-    for copy in copies:
-        copy.wait()
     rows = jnp.concatenate([ref[...] for ref in rows_refs], axis=0)
     row_e = jnp.concatenate([ref[...] for ref in row_es], axis=0)
-    pair = lax.dot_general(
-        rows, full[...], (((1,), (1,)), ((), ())), preferred_element_type=jnp.float32
-    )
+    lanes = cols_refs[0].shape[2]
+    middle = full.shape[1] // lanes // 2 * lanes
+    starts = [k % (full.shape[1] // lanes) * lanes for k in range(len(copies))]
+    pair = None
+    for low, high in ((0, middle), (middle, full.shape[1])):
+        for copy, start in zip(copies, starts):
+            if low <= start < high:
+                copy.wait()
+        part = lax.dot_general(
+            rows[:, low:high],
+            full[:, low:high],
+            (((1,), (1,)), ((), ())),
+            preferred_element_type=jnp.float32,
+        )
+        pair = part if pair is None else pair + part
     amplitude = (spin_scale * pair / (row_e + col_e[...])).astype(jnp.bfloat16)
     terms = jnp.dot(amplitude, full[...], preferred_element_type=jnp.float32)
     count = outs[0].shape[0]
@@ -75,7 +85,10 @@
     even, odd = own[:, 0], own[:, 1]
     first = h == 0
     mine = jnp.where(first, even, odd)
-    there = lax.ppermute(jnp.where(first, odd, even), "h", SWAP)
+    sent = jnp.where(first, odd, even)
+    sent = jnp.concatenate([sent[: nz // 2], sent[nz // 2 :]], axis=2)
+    there = lax.ppermute(sent, "h", SWAP)
+    there = jnp.concatenate([there[:, :, :part], there[:, :, part:]], axis=0)
     wide = jnp.concatenate([jnp.where(first, mine, there), jnp.where(first, there, mine)], axis=2)
     occupied = occupied_base - occupied_step * occ_bins.astype(jnp.float32)
     virtual = virtual_base + virtual_step * vir_bins.astype(jnp.float32)

time: 118 us -> 118 us (level)
  waiting for transfers between devices: 11 us -> 9.52 us
    ppermute x3, starting transfers between devices: 10.2 us -> 11.8 us  [shift(): return lax.ppermute(block, ('h', 'l', 'c'), ring)]
  transfers between devices with their start and end apart: 7 -> 7, of which waited for: 5 -> 4; matrix products, arithmetic and copies ran while one was open for 4% -> 4% of each run, Pallas kernels for 4% -> 4%
where the time goes in v15:
time: 118 us
  blocking collectives  58.1 us (49%)
  starting transfers between devices  36 us (31%)
  waiting for transfers between devices  9.52 us (8%)
  Pallas kernels  7.15 us (6%)
  other arithmetic  3.64 us (3%)
  local copies, waits for them, and re-layouts  3.12 us (3%)
    all_gather x1, blocking collectives, shards(): lax.all_gather(wide.reshape(nz * slab, nh * part), 'z', axis=0, tiled=False)  33.1 us
    all_to_all x1, blocking collectives, shards(): shares = lax.all_to_all(pair_sum.reshape(ny, slab, depth), 'y', 0, 0)  25 us
    ppermute x3, starting transfers between devices, shift(): return lax.ppermute(block, ('h', 'l', 'c'), ring)  11.8 us
    ppermute x1, starting transfers between devices, shards(): rows_there = lax.ppermute(rows, 'c', SWAP)  8.8 us
    ppermute x3, waiting for transfers between devices, shift(): return lax.ppermute(block, ('h', 'l', 'c'), ring)  7.78 us
    pallas_call x2, Pallas kernels, run(): pl.pallas_call(lambda *refs: density_kernel(sides, blocks, len(befores) >...  7.15 us
    all_to_all x1, starting transfers between devices, shards(): lax.all_to_all(jnp.broadcast_to(seeds[None], (ny, slab, depth)), 'y', 0, 0)  6.82 us
    ppermute x1, starting transfers between devices, shards(): there = lax.ppermute(sent, 'h', SWAP)  5.48 us
  transfers between devices with their start and end apart: 7, of which 4 were waited for; matrix products, arithmetic and copies ran while one was open for 4% of the time, Pallas kernels for 4%

profile of v15, /device:TPU:1, one launch (start us, length us, event | category | flops | bytes accessed | tf_op | source)
XLA Modules:
  0.0 117.7 jit_solution(16673607292031666204)
XLA Ops:
  0.0 1.0 convert_element_type.18
  1.0 0.1 pad_maximum_fusion.2
  1.1 5.5 %collective-permute-start = (bf16[6,24,128]{2,1,0:T(8,128)(2,1)S(1)}, bf16[6,24,128]{2,1,0:T(8,128)(2,1)S(1)}, u32[]{:S(2)}, u32[]{:S(2)}) collective-permute-start(bf16[6,24,128]{2,1,0:T(8,128)(2,1)S(1)} %pad_maximum_fusion.2), channel_id=1, source_target_pairs={{0,32},{32,0},{1,33},{33,1},{2,34},{34,2},{3,35},{35,3},{4,36},{36... | collective-permute-start | bytes 110600 | tf_op jit(solution)/shard_map/ppermute | solution.py:90
  6.6 0.7 multiply_subtract_fusion
  7.3 0.1 slice.73
  7.4 0.1 slice.72
  7.5 0.7 multiply_add_fusion
  8.2 0.1 reshape.171
  8.4 0.1 broadcast_subtract_fusion
  8.4 0.1 sub.113
  8.5 0.1 sub.121
  8.6 0.1 sub.118
  8.7 0.1 pad_maximum_fusion.3.refs_0_
  8.8 0.1 sub.124.refs_0_
  8.9 0.0 collective-permute-done
  8.9 0.1 fusion.4
  9.0 0.1 pad_maximum_fusion.1
  9.1 33.1 %all_gather.3.refs_5_ = bf16[12,288,128]{2,1,0:T(8,128)(2,1)S(1)} all-gather(bf16[1,288,128]{2,1,0:T(8,128)(2,1)S(1)} %bitcast.52), channel_id=1, replica_groups=mesh['z'=12,'h'=2,'l'=2,'y'=8,'c'=2] {'z'}, dimensions={0}, use_global_device_ids=true | all-gather | bytes 958464 | tf_op jit(solution)/shard_map/all_gather | solution.py:110
  42.2 2.2 %collective-permute-start.3 = (bf16[12,288,128]{2,1,0:T(8,128)(2,1)S(1)}, bf16[12,288,128]{2,1,0:T(8,128)(2,1)S(1)}, u32[]{:S(2)}, u32[]{:S(2)}) collective-permute-start(bf16[12,288,128]{2,1,0:T(8,128)(2,1)S(1)} %all_gather.3.refs_5_), channel_id=1, source_target_pairs={{0,48},{16,0},{32,16},{48,32},{1,17},{17,33},{33,49},{49,1},{2,50}... | collective-permute-start | bytes 2654216 | tf_op jit(solution)/shard_map/ppermute | solution.py:116
  44.4 4.2 %collective-permute-start.2 = (bf16[12,288,128]{2,1,0:T(8,128)(2,1)S(1)}, bf16[12,288,128]{2,1,0:T(8,128)(2,1)}, u32[]{:S(2)}, u32[]{:S(2)}) collective-permute-start(bf16[12,288,128]{2,1,0:T(8,128)(2,1)S(1)} %all_gather.3.refs_5_), channel_id=1, source_target_pairs={{0,16},{16,32},{32,48},{48,0},{1,49},{17,1},{33,17},{49,33},{2,18}... | collective-permute-start | bytes 2654216 | tf_op jit(solution)/shard_map/ppermute | solution.py:116
  48.7 0.9 broadcast_in_dim.7
  49.5 6.8 %all-to-all-start = ((bf16[8,24,1536]{2,1,0:T(8,128)(2,1)}), bf16[8,24,1536]{2,1,0:T(8,128)(2,1)S(1)}, u32[]{:S(2)}, u32[]{:S(2)}) async-start(bf16[8,24,1536]{2,1,0:T(8,128)(2,1)} %broadcast_in_dim.7), calls=%async_computation | async-start | bytes 1179648 | tf_op jit(solution)/shard_map/all_to_all | solution.py:123
  56.4 0.8 collective-permute-done.3.refs_7_
  57.2 7.0 %collective-permute-done.2.refs_6_ = bf16[12,288,128]{2,1,0:T(8,128)(2,1)} collective-permute-done((bf16[12,288,128]{2,1,0:T(8,128)(2,1)S(1)}, bf16[12,288,128]{2,1,0:T(8,128)(2,1)}, u32[]{:S(2)}, u32[]{:S(2)}) %collective-permute-start.2) | collective-permute-done | bytes 884768 | tf_op jit(solution)/shard_map/ppermute | solution.py:116
  64.1 5.3 %collective-permute-start.4 = (bf16[12,288,128]{2,1,0:T(8,128)(2,1)}, bf16[12,288,128]{2,1,0:T(8,128)(2,1)}, u32[]{:S(2)}, u32[]{:S(2)}) collective-permute-start(bf16[12,288,128]{2,1,0:T(8,128)(2,1)} %collective-permute-done.2.refs_6_), channel_id=1, source_target_pairs={{0,16},{16,32},{32,48},{48,0},{1,49},{17,1},{33,17},{49,33},{2,18}... | collective-permute-start | bytes 2654216 | tf_op jit(solution)/shard_map/ppermute | solution.py:116
  69.5 0.0 all-to-all-done
  69.5 8.8 %collective-permute-start.1 = (bf16[192,1536]{1,0:T(8,128)(2,1)S(1)}, bf16[192,1536]{1,0:T(8,128)(2,1)S(1)}, u32[]{:S(2)}, u32[]{:S(2)}) collective-permute-start(bf16[192,1536]{1,0:T(8,128)(2,1)S(1)} %bitcast.46), channel_id=1, source_target_pairs={{0,1},{1,0},{2,3},{3,2},{4,5},{5,4},{6,7},{7,6},{8,9},{9,8},{10,11... | collective-permute-start | bytes 1769480 | tf_op jit(solution)/shard_map/ppermute | solution.py:126
  78.3 0.6 dynamic_slice.11
  78.9 0.7 subtract_bitcast_fusion
  79.6 0.1 select_n.158.refs_4_
  79.7 0.1 select_n.157.refs_3_
  79.8 0.1 collective-permute-done.1.refs_1_
  79.9 4.4 %shard_map.37 = (f32[192,1536]{1,0:T(8,128)S(1)}, f32[192,1536]{1,0:T(8,128)S(1)}) custom-call(f32[1,864]{1,0:T(1,128)S(1)} %pad_maximum_fusion.3.refs_0_, bf16[192,1536]{1,0:T(8,128)(2,1)S(1)} %collective-permute-done.1.refs_1_, bf16[192,1536]{1,0:T(8,128)(2,1)S(1)} %bitcast.47, f32[192,1]{1,0:T(8,128)S(1)} %select_n.157.refs_3_, ...), custom_call_target="tpu_custom_call" | custom-call | flops 1024 | bytes 4 | tf_op jit(solution)/shard_map/pallas_call | solution.py:65
  84.3 0.0 collective-permute-done.4.refs_5_
  84.3 2.8 %shard_map.38 = (bf16[192,1536]{1,0:T(8,128)(2,1)S(1)}, f32[192,1536]{1,0:T(8,128)S(1)}) custom-call(f32[1,288]{1,0:T(1,128)S(1)} %sub.124.refs_0_, bf16[192,1536]{1,0:T(8,128)(2,1)S(1)} %collective-permute-done.1.refs_1_, bf16[192,1536]{1,0:T(8,128)(2,1)S(1)} %bitcast.48, f32[192,1]{1,0:T(8,128)S(1)} %select_n.157.refs_3_, f32[192,1]{1,0:T(8,128)S(1)} %select_n.158.refs_4_, ...), custom_call_target="tpu_custom_call" | custom-call | flops 679477248 | bytes 2654208 | tf_op jit(solution)/shard_map/pallas_call | solution.py:65
  87.1 3.1 %collective-permute-start.5 = (bf16[192,1536]{1,0:T(8,128)(2,1)S(1)}, bf16[192,1536]{1,0:T(8,128)(2,1)S(1)}, u32[]{:S(2)}, u32[]{:S(2)}) collective-permute-start(bf16[192,1536]{1,0:T(8,128)(2,1)S(1)} %get-tuple-element.28), channel_id=1, source_target_pairs={{0,1},{1,0},{2,3},{3,2},{4,5},{5,4},{6,7},{7,6},{8,9},{9,8},{10,11... | collective-permute-start | bytes 1769480 | tf_op jit(solution)/shard_map/ppermute | solution.py:137
  90.1 1.6 %collective-permute-done.5 = bf16[192,1536]{1,0:T(8,128)(2,1)S(1)} collective-permute-done((bf16[192,1536]{1,0:T(8,128)(2,1)S(1)}, bf16[192,1536]{1,0:T(8,128)(2,1)S(1)}, u32[]{:S(2)}, u32[]{:S(2)}) %collective-permute-start.5) | collective-permute-done | bytes 589856 | tf_op jit(solution)/shard_map/ppermute | solution.py:137
  91.7 0.1 add_convert_fusion
  91.9 25.0 %all_to_all.10 = bf16[8,24,1536]{2,1,0:T(8,128)(2,1)S(1)} all-to-all(bf16[8,24,1536]{2,1,0:T(8,128)(2,1)S(1)} %bitcast.49), channel_id=1, replica_groups=mesh['z'=12,'h'=2,'l'=2,'y'=8,'c'=2] {'y'}, dimensions={0} | all-to-all | bytes 1179648 | tf_op jit(solution)/shard_map/all_to_all | solution.py:139
  116.9 0.1 convert_reduce_fusion
  117.0 0.8 broadcast_in_dim.8
  (9 shorter events, 0.1 us)
Async XLA Ops:
  1.1 7.7 %collective-permute-start = (bf16[6,24,128]{2,1,0:T(8,128)(2,1)S(1)}, bf16[6,24,128]{2,1,0:T(8,128)(2,1)S(1)}, u32[]{:S(2)}, u32[]{:S(2)}) collective-permute-start(bf16[6,24,128]{2,1,0:T(8,128)(2,1)S(1)} %pad_maximum_fusion.2), channel_id=1, source_target_pairs={{0,32},{32,0},{1,33},{33,1},{2,34},{34,2},{3,35},{35,3},{4,36},{36... | collective-permute-start | bytes 110600 | tf_op jit(solution)/shard_map/ppermute | solution.py:90
  42.2 15.0 %collective-permute-start.3 = (bf16[12,288,128]{2,1,0:T(8,128)(2,1)S(1)}, bf16[12,288,128]{2,1,0:T(8,128)(2,1)S(1)}, u32[]{:S(2)}, u32[]{:S(2)}) collective-permute-start(bf16[12,288,128]{2,1,0:T(8,128)(2,1)S(1)} %all_gather.3.refs_5_), channel_id=1, source_target_pairs={{0,48},{16,0},{32,16},{48,32},{1,17},{17,33},{33,49},{49,1},{2,50}... | collective-permute-start | bytes 2654216 | tf_op jit(solution)/shard_map/ppermute | solution.py:116
  44.4 19.7 %collective-permute-start.2 = (bf16[12,288,128]{2,1,0:T(8,128)(2,1)S(1)}, bf16[12,288,128]{2,1,0:T(8,128)(2,1)}, u32[]{:S(2)}, u32[]{:S(2)}) collective-permute-start(bf16[12,288,128]{2,1,0:T(8,128)(2,1)S(1)} %all_gather.3.refs_5_), channel_id=1, source_target_pairs={{0,16},{16,32},{32,48},{48,0},{1,49},{17,1},{33,17},{49,33},{2,18}... | collective-permute-start | bytes 2654216 | tf_op jit(solution)/shard_map/ppermute | solution.py:116
  49.5 19.9 %all-to-all-start = ((bf16[8,24,1536]{2,1,0:T(8,128)(2,1)}), bf16[8,24,1536]{2,1,0:T(8,128)(2,1)S(1)}, u32[]{:S(2)}, u32[]{:S(2)}) async-start(bf16[8,24,1536]{2,1,0:T(8,128)(2,1)} %broadcast_in_dim.7), calls=%async_computation | async-start | bytes 1179648 | tf_op jit(solution)/shard_map/all_to_all | solution.py:123
  64.1 20.1 %collective-permute-start.4 = (bf16[12,288,128]{2,1,0:T(8,128)(2,1)}, bf16[12,288,128]{2,1,0:T(8,128)(2,1)}, u32[]{:S(2)}, u32[]{:S(2)}) collective-permute-start(bf16[12,288,128]{2,1,0:T(8,128)(2,1)} %collective-permute-done.2.refs_6_), channel_id=1, source_target_pairs={{0,16},{16,32},{32,48},{48,0},{1,49},{17,1},{33,17},{49,33},{2,18}... | collective-permute-start | bytes 2654216 | tf_op jit(solution)/shard_map/ppermute | solution.py:116
  69.5 10.4 %collective-permute-start.1 = (bf16[192,1536]{1,0:T(8,128)(2,1)S(1)}, bf16[192,1536]{1,0:T(8,128)(2,1)S(1)}, u32[]{:S(2)}, u32[]{:S(2)}) collective-permute-start(bf16[192,1536]{1,0:T(8,128)(2,1)S(1)} %bitcast.46), channel_id=1, source_target_pairs={{0,1},{1,0},{2,3},{3,2},{4,5},{5,4},{6,7},{7,6},{8,9},{9,8},{10,11... | collective-permute-start | bytes 1769480 | tf_op jit(solution)/shard_map/ppermute | solution.py:126
  87.1 4.7 %collective-permute-start.5 = (bf16[192,1536]{1,0:T(8,128)(2,1)S(1)}, bf16[192,1536]{1,0:T(8,128)(2,1)S(1)}, u32[]{:S(2)}, u32[]{:S(2)}) collective-permute-start(bf16[192,1536]{1,0:T(8,128)(2,1)S(1)} %get-tuple-element.28), channel_id=1, source_target_pairs={{0,1},{1,0},{2,3},{3,2},{4,5},{5,4},{6,7},{7,6},{8,9},{9,8},{10,11... | collective-permute-start | bytes 1769480 | tf_op jit(solution)/shard_map/ppermute | solution.py:137

commit v16 on v15

--- a/solution.py
+++ b/solution.py
@@ -137,8 +137,19 @@
     arrived = lax.ppermute(for_there, "c", SWAP)
     pair_sum = (for_own + arrived.astype(jnp.float32)).astype(jnp.bfloat16)
     shares = lax.all_to_all(pair_sum.reshape(ny, slab, depth), "y", 0, 0)
-    density = jnp.sum(shares.astype(jnp.float32), axis=0)
-    return density[:, None, :]
+    def add_kernel(shares_ref, out_ref):
+        total = shares_ref[0].astype(jnp.float32)
+        for k in range(1, shares_ref.shape[0]):
+            total = total + shares_ref[k].astype(jnp.float32)
+        out_ref[...] = total[:, None, :]
+
+    vmem = pl.BlockSpec(memory_space=pltpu.VMEM)
+    return pl.pallas_call(
+        add_kernel,
+        out_shape=jax.ShapeDtypeStruct((slab, 1, depth), jnp.float32),
+        in_specs=[vmem],
+        out_specs=vmem,
+    )(shares)
 
 
 def solution(mesh):

time: 118 us -> 119 us (level)
  Pallas kernels: 7.15 us -> 8.97 us
    pallas_call x0 -> x1, Pallas kernels: none -> 1.82 us  [shards(): pl.pallas_call(add_kernel, out_shape=jax.ShapeDtypeStruct((slab, 1, depth...]
where the time goes in v16:
time: 119 us
  blocking collectives  58.2 us (49%)
  starting transfers between devices  36 us (30%)
  waiting for transfers between devices  9.53 us (8%)
  Pallas kernels  8.97 us (8%)
  other arithmetic  3.55 us (3%)
  local copies, waits for them, and re-layouts  2.34 us (2%)
    all_gather x1, blocking collectives, shards(): lax.all_gather(wide.reshape(nz * slab, nh * part), 'z', axis=0, tiled=False)  33.1 us
    all_to_all x1, blocking collectives, shards(): shares = lax.all_to_all(pair_sum.reshape(ny, slab, depth), 'y', 0, 0)  25.1 us
    ppermute x3, starting transfers between devices, shift(): return lax.ppermute(block, ('h', 'l', 'c'), ring)  11.8 us
    ppermute x1, starting transfers between devices, shards(): rows_there = lax.ppermute(rows, 'c', SWAP)  8.78 us
    ppermute x3, waiting for transfers between devices, shift(): return lax.ppermute(block, ('h', 'l', 'c'), ring)  7.79 us
    pallas_call x2, Pallas kernels, run(): pl.pallas_call(lambda *refs: density_kernel(sides, blocks, len(befores) >...  7.14 us
    all_to_all x1, starting transfers between devices, shards(): lax.all_to_all(jnp.broadcast_to(seeds[None], (ny, slab, depth)), 'y', 0, 0)  6.82 us
    ppermute x1, starting transfers between devices, shards(): there = lax.ppermute(sent, 'h', SWAP)  5.48 us
  transfers between devices with their start and end apart: 7, of which 4 were waited for; matrix products, arithmetic and copies ran while one was open for 4% of the time, Pallas kernels for 4%

profile of v16, /device:TPU:1, one launch (start us, length us, event | category | flops | bytes accessed | tf_op | source)
XLA Modules:
  0.0 118.8 jit_solution(12087588862549043913)
XLA Ops:
  0.0 1.0 convert_element_type.15
  1.0 0.1 pad_maximum_fusion.2
  1.1 5.5 %collective-permute-start = (bf16[6,24,128]{2,1,0:T(8,128)(2,1)S(1)}, bf16[6,24,128]{2,1,0:T(8,128)(2,1)S(1)}, u32[]{:S(2)}, u32[]{:S(2)}) collective-permute-start(bf16[6,24,128]{2,1,0:T(8,128)(2,1)S(1)} %pad_maximum_fusion.2), channel_id=1, source_target_pairs={{0,32},{32,0},{1,33},{33,1},{2,34},{34,2},{3,35},{35,3},{4,36},{36... | collective-permute-start | bytes 110600 | tf_op jit(solution)/shard_map/ppermute | solution.py:90
  6.6 0.7 multiply_subtract_fusion
  7.3 0.1 slice.73
  7.4 0.1 slice.72
  7.5 0.7 multiply_add_fusion
  8.2 0.1 reshape.171
  8.4 0.1 broadcast_subtract_fusion
  8.4 0.1 sub.113
  8.5 0.1 sub.121
  8.6 0.1 sub.118
  8.7 0.1 pad_maximum_fusion.3.refs_0_
  8.8 0.1 sub.124.refs_0_
  8.9 0.0 collective-permute-done
  8.9 0.1 fusion.4
  9.0 0.1 pad_maximum_fusion.1
  9.1 33.1 %all_gather.3.refs_5_ = bf16[12,288,128]{2,1,0:T(8,128)(2,1)S(1)} all-gather(bf16[1,288,128]{2,1,0:T(8,128)(2,1)S(1)} %bitcast.52), channel_id=1, replica_groups=mesh['z'=12,'h'=2,'l'=2,'y'=8,'c'=2] {'z'}, dimensions={0}, use_global_device_ids=true | all-gather | bytes 958464 | tf_op jit(solution)/shard_map/all_gather | solution.py:110
  42.2 2.2 %collective-permute-start.3 = (bf16[12,288,128]{2,1,0:T(8,128)(2,1)S(1)}, bf16[12,288,128]{2,1,0:T(8,128)(2,1)S(1)}, u32[]{:S(2)}, u32[]{:S(2)}) collective-permute-start(bf16[12,288,128]{2,1,0:T(8,128)(2,1)S(1)} %all_gather.3.refs_5_), channel_id=1, source_target_pairs={{0,48},{16,0},{32,16},{48,32},{1,17},{17,33},{33,49},{49,1},{2,50}... | collective-permute-start | bytes 2654216 | tf_op jit(solution)/shard_map/ppermute | solution.py:116
  44.4 4.2 %collective-permute-start.2 = (bf16[12,288,128]{2,1,0:T(8,128)(2,1)S(1)}, bf16[12,288,128]{2,1,0:T(8,128)(2,1)}, u32[]{:S(2)}, u32[]{:S(2)}) collective-permute-start(bf16[12,288,128]{2,1,0:T(8,128)(2,1)S(1)} %all_gather.3.refs_5_), channel_id=1, source_target_pairs={{0,16},{16,32},{32,48},{48,0},{1,49},{17,1},{33,17},{49,33},{2,18}... | collective-permute-start | bytes 2654216 | tf_op jit(solution)/shard_map/ppermute | solution.py:116
  48.7 0.8 broadcast_in_dim.5
  49.5 6.8 %all-to-all-start = ((bf16[8,24,1536]{2,1,0:T(8,128)(2,1)}), bf16[8,24,1536]{2,1,0:T(8,128)(2,1)S(1)}, u32[]{:S(2)}, u32[]{:S(2)}) async-start(bf16[8,24,1536]{2,1,0:T(8,128)(2,1)} %broadcast_in_dim.5), calls=%async_computation | async-start | bytes 1179648 | tf_op jit(solution)/shard_map/all_to_all | solution.py:123
  56.4 0.8 collective-permute-done.3.refs_7_
  57.2 7.0 %collective-permute-done.2.refs_6_ = bf16[12,288,128]{2,1,0:T(8,128)(2,1)} collective-permute-done((bf16[12,288,128]{2,1,0:T(8,128)(2,1)S(1)}, bf16[12,288,128]{2,1,0:T(8,128)(2,1)}, u32[]{:S(2)}, u32[]{:S(2)}) %collective-permute-start.2) | collective-permute-done | bytes 884768 | tf_op jit(solution)/shard_map/ppermute | solution.py:116
  64.1 5.3 %collective-permute-start.4 = (bf16[12,288,128]{2,1,0:T(8,128)(2,1)}, bf16[12,288,128]{2,1,0:T(8,128)(2,1)}, u32[]{:S(2)}, u32[]{:S(2)}) collective-permute-start(bf16[12,288,128]{2,1,0:T(8,128)(2,1)} %collective-permute-done.2.refs_6_), channel_id=1, source_target_pairs={{0,16},{16,32},{32,48},{48,0},{1,49},{17,1},{33,17},{49,33},{2,18}... | collective-permute-start | bytes 2654216 | tf_op jit(solution)/shard_map/ppermute | solution.py:116
  69.5 0.0 all-to-all-done
  69.5 8.8 %collective-permute-start.1 = (bf16[192,1536]{1,0:T(8,128)(2,1)S(1)}, bf16[192,1536]{1,0:T(8,128)(2,1)S(1)}, u32[]{:S(2)}, u32[]{:S(2)}) collective-permute-start(bf16[192,1536]{1,0:T(8,128)(2,1)S(1)} %bitcast.46), channel_id=1, source_target_pairs={{0,1},{1,0},{2,3},{3,2},{4,5},{5,4},{6,7},{7,6},{8,9},{9,8},{10,11... | collective-permute-start | bytes 1769480 | tf_op jit(solution)/shard_map/ppermute | solution.py:126
  78.3 0.6 dynamic_slice.11
  78.9 0.7 subtract_bitcast_fusion
  79.6 0.1 select_n.158.refs_4_
  79.7 0.1 select_n.157.refs_3_
  79.8 0.1 collective-permute-done.1.refs_1_
  79.9 4.4 %shard_map.37 = (f32[192,1536]{1,0:T(8,128)S(1)}, f32[192,1536]{1,0:T(8,128)S(1)}) custom-call(f32[1,864]{1,0:T(1,128)S(1)} %pad_maximum_fusion.3.refs_0_, bf16[192,1536]{1,0:T(8,128)(2,1)S(1)} %collective-permute-done.1.refs_1_, bf16[192,1536]{1,0:T(8,128)(2,1)S(1)} %bitcast.47, f32[192,1]{1,0:T(8,128)S(1)} %select_n.157.refs_3_, ...), custom_call_target="tpu_custom_call" | custom-call | flops 1024 | bytes 4 | tf_op jit(solution)/shard_map/pallas_call | solution.py:65
  84.2 0.0 collective-permute-done.4.refs_5_
  84.3 2.8 %shard_map.38 = (bf16[192,1536]{1,0:T(8,128)(2,1)S(1)}, f32[192,1536]{1,0:T(8,128)S(1)}) custom-call(f32[1,288]{1,0:T(1,128)S(1)} %sub.124.refs_0_, bf16[192,1536]{1,0:T(8,128)(2,1)S(1)} %collective-permute-done.1.refs_1_, bf16[192,1536]{1,0:T(8,128)(2,1)S(1)} %bitcast.48, f32[192,1]{1,0:T(8,128)S(1)} %select_n.157.refs_3_, f32[192,1]{1,0:T(8,128)S(1)} %select_n.158.refs_4_, ...), custom_call_target="tpu_custom_call" | custom-call | flops 679477248 | bytes 2654208 | tf_op jit(solution)/shard_map/pallas_call | solution.py:65
  87.0 3.1 %collective-permute-start.5 = (bf16[192,1536]{1,0:T(8,128)(2,1)S(1)}, bf16[192,1536]{1,0:T(8,128)(2,1)S(1)}, u32[]{:S(2)}, u32[]{:S(2)}) collective-permute-start(bf16[192,1536]{1,0:T(8,128)(2,1)S(1)} %get-tuple-element.28), channel_id=1, source_target_pairs={{0,1},{1,0},{2,3},{3,2},{4,5},{5,4},{6,7},{7,6},{8,9},{9,8},{10,11... | collective-permute-start | bytes 1769480 | tf_op jit(solution)/shard_map/ppermute | solution.py:137
  90.1 1.6 %collective-permute-done.5 = bf16[192,1536]{1,0:T(8,128)(2,1)S(1)} collective-permute-done((bf16[192,1536]{1,0:T(8,128)(2,1)S(1)}, bf16[192,1536]{1,0:T(8,128)(2,1)S(1)}, u32[]{:S(2)}, u32[]{:S(2)}) %collective-permute-start.5) | collective-permute-done | bytes 589856 | tf_op jit(solution)/shard_map/ppermute | solution.py:137
  91.7 0.1 add_convert_fusion
  91.9 25.1 %all_to_all.10.shares_ref = bf16[8,24,1536]{2,1,0:T(8,128)(2,1)} all-to-all(bf16[8,24,1536]{2,1,0:T(8,128)(2,1)S(1)} %bitcast.49), channel_id=1, replica_groups=mesh['z'=12,'h'=2,'l'=2,'y'=8,'c'=2] {'y'}, dimensions={0} | all-to-all | bytes 1179648 | tf_op jit(solution)/shard_map/all_to_all | solution.py:139
  117.0 1.8 %shard_map.39 = f32[24,1,1536]{2,1,0:T(1,128)} custom-call(bf16[8,24,1536]{2,1,0:T(8,128)(2,1)} %all_to_all.10.shares_ref), custom_call_target="tpu_custom_call" | custom-call | tf_op jit(solution)/shard_map/pallas_call | solution.py:147
  (9 shorter events, 0.1 us)
Async XLA Ops:
  1.1 7.7 %collective-permute-start = (bf16[6,24,128]{2,1,0:T(8,128)(2,1)S(1)}, bf16[6,24,128]{2,1,0:T(8,128)(2,1)S(1)}, u32[]{:S(2)}, u32[]{:S(2)}) collective-permute-start(bf16[6,24,128]{2,1,0:T(8,128)(2,1)S(1)} %pad_maximum_fusion.2), channel_id=1, source_target_pairs={{0,32},{32,0},{1,33},{33,1},{2,34},{34,2},{3,35},{35,3},{4,36},{36... | collective-permute-start | bytes 110600 | tf_op jit(solution)/shard_map/ppermute | solution.py:90
  42.2 15.0 %collective-permute-start.3 = (bf16[12,288,128]{2,1,0:T(8,128)(2,1)S(1)}, bf16[12,288,128]{2,1,0:T(8,128)(2,1)S(1)}, u32[]{:S(2)}, u32[]{:S(2)}) collective-permute-start(bf16[12,288,128]{2,1,0:T(8,128)(2,1)S(1)} %all_gather.3.refs_5_), channel_id=1, source_target_pairs={{0,48},{16,0},{32,16},{48,32},{1,17},{17,33},{33,49},{49,1},{2,50}... | collective-permute-start | bytes 2654216 | tf_op jit(solution)/shard_map/ppermute | solution.py:116
  44.4 19.7 %collective-permute-start.2 = (bf16[12,288,128]{2,1,0:T(8,128)(2,1)S(1)}, bf16[12,288,128]{2,1,0:T(8,128)(2,1)}, u32[]{:S(2)}, u32[]{:S(2)}) collective-permute-start(bf16[12,288,128]{2,1,0:T(8,128)(2,1)S(1)} %all_gather.3.refs_5_), channel_id=1, source_target_pairs={{0,16},{16,32},{32,48},{48,0},{1,49},{17,1},{33,17},{49,33},{2,18}... | collective-permute-start | bytes 2654216 | tf_op jit(solution)/shard_map/ppermute | solution.py:116
  49.5 19.9 %all-to-all-start = ((bf16[8,24,1536]{2,1,0:T(8,128)(2,1)}), bf16[8,24,1536]{2,1,0:T(8,128)(2,1)S(1)}, u32[]{:S(2)}, u32[]{:S(2)}) async-start(bf16[8,24,1536]{2,1,0:T(8,128)(2,1)} %broadcast_in_dim.5), calls=%async_computation | async-start | bytes 1179648 | tf_op jit(solution)/shard_map/all_to_all | solution.py:123
  64.1 20.1 %collective-permute-start.4 = (bf16[12,288,128]{2,1,0:T(8,128)(2,1)}, bf16[12,288,128]{2,1,0:T(8,128)(2,1)}, u32[]{:S(2)}, u32[]{:S(2)}) collective-permute-start(bf16[12,288,128]{2,1,0:T(8,128)(2,1)} %collective-permute-done.2.refs_6_), channel_id=1, source_target_pairs={{0,16},{16,32},{32,48},{48,0},{1,49},{17,1},{33,17},{49,33},{2,18}... | collective-permute-start | bytes 2654216 | tf_op jit(solution)/shard_map/ppermute | solution.py:116
  69.5 10.4 %collective-permute-start.1 = (bf16[192,1536]{1,0:T(8,128)(2,1)S(1)}, bf16[192,1536]{1,0:T(8,128)(2,1)S(1)}, u32[]{:S(2)}, u32[]{:S(2)}) collective-permute-start(bf16[192,1536]{1,0:T(8,128)(2,1)S(1)} %bitcast.46), channel_id=1, source_target_pairs={{0,1},{1,0},{2,3},{3,2},{4,5},{5,4},{6,7},{7,6},{8,9},{9,8},{10,11... | collective-permute-start | bytes 1769480 | tf_op jit(solution)/shard_map/ppermute | solution.py:126
  87.0 4.7 %collective-permute-start.5 = (bf16[192,1536]{1,0:T(8,128)(2,1)S(1)}, bf16[192,1536]{1,0:T(8,128)(2,1)S(1)}, u32[]{:S(2)}, u32[]{:S(2)}) collective-permute-start(bf16[192,1536]{1,0:T(8,128)(2,1)S(1)} %get-tuple-element.28), channel_id=1, source_target_pairs={{0,1},{1,0},{2,3},{3,2},{4,5},{5,4},{6,7},{7,6},{8,9},{9,8},{10,11... | collective-permute-start | bytes 1769480 | tf_op jit(solution)/shard_map/ppermute | solution.py:137
